TPU v7x, 256 devices: a whole 4x4x8 slice. The times are simulated.
256 devices in a mesh: row: 8 (over x, core), col: 32 (over z, y).
Axes of the slice: x: 4, y: 4, z: 8, core: 2. Of those that a mesh axis runs over, the one named last changes fastest.
Arguments:
- inputs: bfloat16 [1024, 8192], P('col', 'row'), may hold values from -6 to 6
- cotangent: bfloat16 [1024, 8192], P('col', 'row'), may hold values from -6 to 6
- gate_pre: bfloat16 [1024, 28672], P('row', 'col'), may hold values from -6 to 6
- up_pre: bfloat16 [1024, 28672], P('row', 'col'), may hold values from -6 to 6
- gate_weight: bfloat16 [8192, 28672], P('row', 'col'), may hold values from -0.0625 to 0.0625
- up_weight: bfloat16 [8192, 28672], P('row', 'col'), may hold values from -0.0625 to 0.0625
- down_weight: bfloat16 [28672, 8192], P('col', 'row'), may hold values from -0.03125 to 0.03125
- pair_ids: int32 [1024], P('col'), may hold values from 0 to 7, never falling along the last dimension, each value on 1 to 512 neighbouring positions
- flags: int32 [1024], P('col'), may hold values 0 or 1
- pair_scale: float32 [8], replicated, may hold values from 0.5 to 2
Outputs:
- grad_input: bfloat16 [1024, 8192], P('col', 'row')
- grad_gate: bfloat16 [8192, 28672], P('row', 'col')
- grad_up: bfloat16 [8192, 28672], P('row', 'col')
- grad_down: bfloat16 [28672, 8192], P('col', 'row')
Inputs may be any that keep to these rules, and one draw needn't show every extreme that they name: `pair_ids`: never falls from one token to the next.
All inputs are finite; a program needn't handle non-finite values. No bound on the sum of `flags` on one device may be relied on, other than what follows from the above.
Results may differ from a plain program's by a relative error of at most 0.0057.
Values may be sent and summed in bfloat16 or wider, within the bound.
No kernel may reach another device: no remote copies, remote signals or barrier semaphores. Data moves between devices by JAX's collectives and lax.ppermute only.
A program may use at most 128 MiB of HBM per device.

v0:
```python
import jax
import jax.numpy as jnp
from jax import lax
from jax.sharding import PartitionSpec as P


def swiglu_grads(d_hidden, gate_vals, up_vals):
    gate_f = gate_vals.astype(jnp.float32)
    up_f = up_vals.astype(jnp.float32)
    sigmoid_gate = jax.nn.sigmoid(gate_f)
    hidden = (gate_f * sigmoid_gate * up_f).astype(jnp.bfloat16)
    d_up = (d_hidden * gate_f * sigmoid_gate).astype(jnp.bfloat16)
    d_gate = (d_hidden * up_f * sigmoid_gate * (1.0 + gate_f * (1.0 - sigmoid_gate))).astype(
        jnp.bfloat16
    )
    return (hidden, d_gate, d_up)


def token_product(left, right):
    return lax.dot_general(
        left, right, (((0,), (0,)), ((), ())), preferred_element_type=jnp.float32
    )


def right_transposed(left, right):
    return lax.dot_general(
        left, right, (((1,), (1,)), ((), ())), preferred_element_type=jnp.float32
    )


def on_device(
    inputs,
    cotangent,
    gate_pre,
    up_pre,
    gate_weight,
    up_weight,
    down_weight,
    pair_ids,
    flags,
    pair_scale,
):
    matches = pair_ids[:, None] == jnp.arange(pair_scale.shape[0], dtype=jnp.int32)[None, :]
    scales = jnp.sum(
        jnp.where(matches, pair_scale[None, :], jnp.zeros((), pair_scale.dtype)), axis=1
    )
    weight = (2 * flags - 1).astype(jnp.float32) * scales
    scaled = (cotangent.astype(jnp.float32) * weight[:, None]).astype(jnp.bfloat16)
    x_all, dy_all = (
        lax.all_gather(inputs, "col", axis=0, tiled=True),
        lax.all_gather(scaled, "col", axis=0, tiled=True),
    )
    d_hidden = lax.psum_scatter(
        right_transposed(dy_all, down_weight), "row", scatter_dimension=0, tiled=True
    )
    hidden, d_gate, d_up = swiglu_grads(d_hidden, gate_pre, up_pre)
    hidden_all, gate_grads, up_grads = (
        lax.all_gather(hidden, "row", axis=0, tiled=True),
        lax.all_gather(d_gate, "row", axis=0, tiled=True),
        lax.all_gather(d_up, "row", axis=0, tiled=True),
    )
    grad_down = token_product(hidden_all, dy_all).astype(jnp.bfloat16)
    grad_gate = token_product(x_all, gate_grads).astype(jnp.bfloat16)
    grad_up = token_product(x_all, up_grads).astype(jnp.bfloat16)
    grad_total = lax.psum_scatter(
        right_transposed(gate_grads, gate_weight) + right_transposed(up_grads, up_weight),
        "col",
        scatter_dimension=0,
        tiled=True,
    )
    return (grad_total.astype(jnp.bfloat16), grad_gate, grad_up, grad_down)


def solution(mesh):
    return jax.shard_map(
        on_device,
        mesh=mesh,
        in_specs=(
            P("col", "row"),
            P("col", "row"),
            P("row", "col"),
            P("row", "col"),
            P("row", "col"),
            P("row", "col"),
            P("col", "row"),
            P("col"),
            P("col"),
            P(),
        ),
        out_specs=(P("col", "row"), P("row", "col"), P("row", "col"), P("col", "row")),
        check_vma=False,
    )
```

profile of v0, /device:TPU:24, one launch (start us, length us, event | category | flops | bytes accessed | tf_op | source)
XLA Modules:
  0.0 533.4 jit_solution(16570217168676191808)
XLA Ops:
  7.2 0.0 copy-start
  7.2 0.0 all-gather.6.cloned.1.call-start
  7.2 0.9 select_reduce_fusion
  8.1 0.7 convert_multiply_fusion.5
  8.8 1.5 multiply_convert_fusion
  10.3 0.0 all-gather.6.cloned.1.call-update
  10.3 0.0 reduce-scatter.3.cloned.1.call-start
  10.4 80.0 %all-gather.6.cloned.1.call-done = bf16[1024,1024]{1,0:T(8,128)(2,1)} async-done(((bf16[32,1024]{1,0:T(8,128)(2,1)}), bf16[1024,1024]{1,0:T(8,128)(2,1)}) %all-gather.6.cloned.1.call-update) | async-done | bytes 2097168 | tf_op jit(solution)/shard_map/all_gather | solution.py:51
  90.4 6.3 %fusion.10 = f32[1024,896]{1,0:T(8,128)} fusion(bf16[1024,1024]{1,0:T(8,128)(2,1)} %all-gather.6.cloned.1.call-done, bf16[896,1024]{1,0:T(8,128)(2,1)} %param.16), kind=kOutput, calls=%fused_computation.24 | convolution fusion | flops 1879048192 | bytes 7602176 | tf_op jit(solution)/shard_map/dot_general | solution.py:26
  96.7 0.0 copy-start.1
  96.7 0.0 copy-start.2
  96.7 0.0 reduce-scatter.3.cloned.1.call-update
  96.7 0.0 all-gather.8.cloned.1.call-start
  96.7 38.1 %reduce-scatter.3.cloned.1.call-done = f32[128,896]{1,0:T(8,128)} async-done(((f32[1024,896]{1,0:T(8,128)}), f32[128,896]{1,0:T(8,128)}) %reduce-scatter.3.cloned.1.call-update) | async-done | bytes 458768 | tf_op jit(solution)/shard_map/reduce_scatter | solution.py:53
  134.9 0.0 copy-done.1
  134.9 0.0 copy-done.2
  134.9 2.1 fusion.9
  137.0 0.0 all-gather.8.cloned.1.call-update
  137.0 0.0 all-gather.10.cloned.1.call-start
  137.0 0.5 all-gather.10.cloned.1.call-update
  137.6 0.0 all-gather.12.cloned.1.call-start
  137.6 0.5 all-gather.12.cloned.1.call-update
  138.2 0.0 all-gather.14.cloned.1.call-start
  138.2 0.5 all-gather.14.cloned.1.call-update
  138.7 0.0 reduce-scatter.5.cloned.1.call-start
  138.8 24.7 %all-gather.8.cloned.1.call-done = bf16[1024,896]{1,0:T(8,128)(2,1)} async-done(((bf16[128,896]{1,0:T(8,128)(2,1)}), bf16[1024,896]{1,0:T(8,128)(2,1)}) %all-gather.8.cloned.1.call-update) | async-done | bytes 1835024 | tf_op jit(solution)/shard_map/all_gather | solution.py:59
  163.5 0.0 copy-done
  163.5 5.8 %fusion.11 = f32[1024,1024]{1,0:T(8,128)} fusion(bf16[1024,896]{1,0:T(8,128)(2,1)} %all-gather.8.cloned.1.call-done, bf16[1024,896]{1,0:T(8,128)(2,1)S(1)} %copy-done), kind=kOutput, calls=%fused_computation.25 | convolution fusion | flops 1879048192 | bytes 7864320 | tf_op jit(solution)/shard_map/dot_general | solution.py:26
  169.3 24.1 %all-gather.10.cloned.1.call-done = bf16[1024,896]{1,0:T(8,128)(2,1)} async-done(((bf16[128,896]{1,0:T(8,128)(2,1)}), bf16[1024,896]{1,0:T(8,128)(2,1)}) %all-gather.10.cloned.1.call-update) | async-done | bytes 1835024 | tf_op jit(solution)/shard_map/all_gather | solution.py:60
  193.4 7.6 %convolution_add_fusion = f32[1024,1024]{1,0:T(8,128)} fusion(f32[1024,1024]{1,0:T(8,128)} %fusion.11, bf16[1024,896]{1,0:T(8,128)(2,1)} %all-gather.10.cloned.1.call-done, bf16[1024,896]{1,0:T(8,128)(2,1)} %param.15), kind=kOutput, calls=%fused_computation | convolution fusion | flops 1880096768 | bytes 12058624 | tf_op jit(solution)/shard_map/dot_general | solution.py:26
  201.0 0.0 reduce-scatter.5.cloned.1.call-update
  201.0 71.6 %all-gather.12.cloned.1.call-done = bf16[1024,1024]{1,0:T(8,128)(2,1)} async-done(((bf16[32,1024]{1,0:T(8,128)(2,1)}), bf16[1024,1024]{1,0:T(8,128)(2,1)}) %all-gather.12.cloned.1.call-update) | async-done | bytes 2097168 | tf_op jit(solution)/shard_map/all_gather | solution.py:50
  272.6 5.5 %convert_bitcast_fusion.1 = bf16[1024,896]{0,1:T(8,128)(2,1)} fusion(bf16[1024,896]{1,0:T(8,128)(2,1)} %all-gather.8.cloned.1.call-done, bf16[1024,1024]{1,0:T(8,128)(2,1)} %all-gather.12.cloned.1.call-done), kind=kOutput, calls=%fused_computation.2 | convolution fusion | flops 1879965696 | bytes 5767168 | tf_op jit(solution)/shard_map/dot_general | solution.py:20
  278.1 3.8 copy.16
  281.9 5.5 %convert_bitcast_fusion = bf16[1024,896]{0,1:T(8,128)(2,1)} fusion(bf16[1024,896]{1,0:T(8,128)(2,1)} %all-gather.10.cloned.1.call-done, bf16[1024,1024]{1,0:T(8,128)(2,1)} %all-gather.12.cloned.1.call-done), kind=kOutput, calls=%fused_computation.1 | convolution fusion | flops 1879965696 | bytes 5767168 | tf_op jit(solution)/shard_map/dot_general | solution.py:20
  287.4 3.8 copy.17
  291.2 9.1 %all-gather.14.cloned.1.call-done = bf16[1024,896]{1,0:T(8,128)(2,1)} async-done(((bf16[128,896]{1,0:T(8,128)(2,1)}), bf16[1024,896]{1,0:T(8,128)(2,1)}) %all-gather.14.cloned.1.call-update) | async-done | bytes 1835024 | tf_op jit(solution)/shard_map/all_gather | solution.py:58
  300.3 5.5 %convolution_convert_fusion = bf16[896,1024]{1,0:T(8,128)(2,1)} fusion(bf16[1024,896]{1,0:T(8,128)(2,1)} %all-gather.14.cloned.1.call-done, bf16[1024,1024]{1,0:T(8,128)(2,1)} %all-gather.6.cloned.1.call-done), kind=kOutput, calls=%fused_computation.3 | convolution fusion | flops 1879965696 | bytes 5767168 | tf_op jit(solution)/shard_map/dot_general | solution.py:20
  305.8 219.3 %reduce-scatter.5.cloned.1.call-done = f32[32,1024]{1,0:T(8,128)} async-done(((f32[1024,1024]{1,0:T(8,128)}), f32[32,1024]{1,0:T(8,128)}) %reduce-scatter.5.cloned.1.call-update) | async-done | bytes 131088 | tf_op jit(solution)/shard_map/reduce_scatter | solution.py:65
  525.1 1.5 convert_element_type.49
Async XLA Ops:
  7.2 156.3 %copy-start = (bf16[1024,896]{1,0:T(8,128)(2,1)S(1)}, bf16[1024,896]{1,0:T(8,128)(2,1)}, u32[]{:S(2)}) copy-start(bf16[1024,896]{1,0:T(8,128)(2,1)} %param.14) | copy-start | bytes 5505028
  7.2 83.2 %all-gather.6.cloned.1.call-start = ((), (), s32[]{:S(2)}) async-start(), calls=%async_computation.2 | async-start | bytes 2162688 | tf_op jit(solution)/shard_map/all_gather | solution.py:51
  10.3 124.5 %reduce-scatter.3.cloned.1.call-start = ((), (), s32[]{:S(2)}) async-start(), calls=%async_computation.3 | async-start | bytes 4128768 | tf_op jit(solution)/shard_map/reduce_scatter | solution.py:53
  96.7 38.2 %copy-start.1 = (bf16[128,896]{1,0:T(8,128)(2,1)S(1)}, bf16[128,896]{1,0:T(8,128)(2,1)}, u32[]{:S(2)}) copy-start(bf16[128,896]{1,0:T(8,128)(2,1)} %param.12) | copy-start | bytes 688132
  96.7 38.2 %copy-start.2 = (bf16[128,896]{1,0:T(8,128)(2,1)S(1)}, bf16[128,896]{1,0:T(8,128)(2,1)}, u32[]{:S(2)}) copy-start(bf16[128,896]{1,0:T(8,128)(2,1)} %param.13) | copy-start | bytes 688132
  96.7 66.8 %all-gather.8.cloned.1.call-start = ((), (), s32[]{:S(2)}) async-start(), calls=%async_computation.4 | async-start | bytes 2064384 | tf_op jit(solution)/shard_map/all_gather | solution.py:59
  137.0 56.4 %all-gather.10.cloned.1.call-start = ((), (), s32[]{:S(2)}) async-start(), calls=%async_computation.5 | async-start | bytes 2064384 | tf_op jit(solution)/shard_map/all_gather | solution.py:60
  137.6 135.1 %all-gather.12.cloned.1.call-start = ((), (), s32[]{:S(2)}) async-start(), calls=%async_computation.7 | async-start | bytes 2162688 | tf_op jit(solution)/shard_map/all_gather | solution.py:50
  138.2 162.1 %all-gather.14.cloned.1.call-start = ((), (), s32[]{:S(2)}) async-start(), calls=%async_computation.8 | async-start | bytes 2064384 | tf_op jit(solution)/shard_map/all_gather | solution.py:58
  138.7 386.3 %reduce-scatter.5.cloned.1.call-start = ((), (), s32[]{:S(2)}) async-start(), calls=%async_computation.6 | async-start | bytes 4325376 | tf_op jit(solution)/shard_map/reduce_scatter | solution.py:65
Sparse Core Ops, SparseCore 0:
  11.2 79.1 all-gather.5
  96.8 38.0 reduce-scatter.2
  137.3 26.1 all-gather.7
  165.7 27.5 all-gather.9
  195.8 76.7 all-gather.11
  274.3 25.9 all-gather.13
  304.2 220.8 reduce-scatter.4
where the time goes:
time: 535 us; the launch traced here: 533 us
  waiting for transfers between devices  469 us (88%)
  matrix products  36.2 us (7%)
  between operations  14.1 us (3%)
  local copies, waits for them, and re-layouts  7.61 us (1%)
  other arithmetic  6.71 us (1%)
    reduce_scatter x1, waiting for transfers between devices, on_device(): lax.psum_scatter(right_transposed(gate_grads, gate_weight) + right_transp...  219 us
    all_gather x1, waiting for transfers between devices, on_device(): lax.all_gather(scaled, 'col', axis=0, tiled=True)  80 us
    all_gather x1, waiting for transfers between devices, on_device(): lax.all_gather(inputs, 'col', axis=0, tiled=True)  71.6 us
    reduce_scatter x1, waiting for transfers between devices, on_device(): lax.psum_scatter(right_transposed(dy_all, down_weight), 'row', scatter_di...  38.1 us
    all_gather x1, waiting for transfers between devices, on_device(): lax.all_gather(d_gate, 'row', axis=0, tiled=True)  24.7 us
    all_gather x1, waiting for transfers between devices, on_device(): lax.all_gather(d_up, 'row', axis=0, tiled=True)  24.1 us
    dot_general x3, matrix products, right_transposed(): lax.dot_general(left, right, (((1,), (1,)), ((), ())), preferred_element_...  19.7 us
    dot_general x3, matrix products, token_product(): lax.dot_general(left, right, (((0,), (0,)), ((), ())), preferred_element_...  16.4 us
  transfers between devices with their start and end apart: 7, of which 7 were waited for; matrix products, arithmetic and copies ran while one was open for 7% of the time, Pallas kernels for 0%

commit v1 on v0

v1 whole, which is shorter than its diff:
```python
import jax
import jax.numpy as jnp
from jax import lax
from jax.experimental import pallas as pl
from jax.experimental.pallas import tpu as pltpu
from jax.sharding import PartitionSpec as P

NX, NC, NZ, NY = 4, 2, 8, 4
TOK = 32
BLK = NY * TOK
BF, F32 = jnp.bfloat16, jnp.float32


def from_z(v, k):
    perm = [(z * NY + y, (z - k) % NZ * NY + y) for z in range(NZ) for y in range(NY)]
    return lax.ppermute(v, "col", perm)


def from_y(v, k):
    perm = [(z * NY + y, z * NY + (y - k) % NY) for z in range(NZ) for y in range(NY)]
    return lax.ppermute(v, "col", perm)


def from_x(v, k):
    perm = [(x * NC + c, (x - k) % NX * NC + c) for x in range(NX) for c in range(NC)]
    return lax.ppermute(v, "row", perm)


def from_core(v):
    return lax.ppermute(v, "row", [(r, r ^ 1) for r in range(NX * NC)])


def halves_kernel(u, d, r1, r2, r3, low, high):
    half = BLK // 2
    low[...] = u[:half, :]
    high[...] = d[half:, :]


def halves(u, d, after):
    block = pl.BlockSpec(u.shape, lambda t: (0, 0))
    half = pl.BlockSpec((BLK // 2, u.shape[1]), lambda t: (0, 0))
    sds = jax.ShapeDtypeStruct((BLK // 2, u.shape[1]), BF)
    return pl.pallas_call(
        halves_kernel,
        grid=(1,),
        in_specs=[block, block] + [pl.BlockSpec(memory_space=pl.ANY)] * 3,
        out_specs=[half, half],
        out_shape=[sds, sds],
        compiler_params=pltpu.CompilerParams(vmem_limit_bytes=4 << 20),
        cost_estimate=pl.CostEstimate(flops=0, bytes_accessed=4 * u.size, transcendentals=0),
        name="halves",
    )(u, d, *after)


def gather_z(blk, pre_of):
    up, down = [blk], [blk]
    for r in range(3):
        up.append(from_z(up[-1], 1))
        down.append(from_z(down[-1], -1))
        if r == 0:
            pre = pre_of(up[-1])
            others = [from_x(pre, k) for k in range(1, NX)]
    low, high = halves(up[3], down[3], others)
    far = [from_z(low, 1), from_z(high, -1)]
    all_rows = jnp.concatenate(up + far + [down[3], down[2], down[1]], axis=0)
    return all_rows, jnp.stack([pre] + others, axis=0)


def near_kernel(b3, b5, up, down, after, up_out, down_out):
    half = BLK // 2
    up_out[:half, :] = (b3[:half, :].astype(F32) + up[...].astype(F32)).astype(BF)
    up_out[half:, :] = b3[half:, :]
    down_out[:half, :] = b5[:half, :]
    down_out[half:, :] = (b5[half:, :].astype(F32) + down[...].astype(F32)).astype(BF)


def step_kernel(bu, bd, up, down, after, up_out, down_out):
    up_out[...] = (bu[...].astype(F32) + up[...].astype(F32)).astype(BF)
    down_out[...] = (bd[...].astype(F32) + down[...].astype(F32)).astype(BF)


def step(kernel, p, i, j, up, down, after):
    width = p.shape[1]
    sds = jax.ShapeDtypeStruct((BLK, width), BF)
    whole = pl.BlockSpec(up.shape, lambda t: (0, 0))
    block = pl.BlockSpec((BLK, width), lambda t: (0, 0))
    return pl.pallas_call(
        kernel,
        grid=(1,),
        in_specs=[
            pl.BlockSpec((BLK, width), lambda t: (i, 0)),
            pl.BlockSpec((BLK, width), lambda t: (j, 0)),
            whole,
            whole,
            pl.BlockSpec(memory_space=pl.ANY),
        ],
        out_specs=[block, block],
        out_shape=[sds, sds],
        compiler_params=pltpu.CompilerParams(vmem_limit_bytes=6 << 20),
        cost_estimate=pl.CostEstimate(flops=2 * BLK * width, bytes_accessed=12 * BLK * width, transcendentals=0),
        name="step",
    )(p, p, up, down, after)


def own_kernel(b0, up, down, after, own, s1, s2, s3):
    total = b0[...].astype(F32) + up[...].astype(F32) + down[...].astype(F32)
    own[...] = total[:TOK, :]
    for k, out in enumerate((s1, s2, s3), 1):
        out[...] = total[k * TOK:(k + 1) * TOK, :].astype(BF)


def own_of(p, up, down, after):
    width = p.shape[1]
    block = pl.BlockSpec((BLK, width), lambda t: (0, 0))
    out = pl.BlockSpec((TOK, width), lambda t: (0, 0))
    return pl.pallas_call(
        own_kernel,
        grid=(1,),
        in_specs=[block] * 3 + [pl.BlockSpec(memory_space=pl.ANY)],
        out_specs=[out] * 4,
        out_shape=[jax.ShapeDtypeStruct((TOK, width), F32)] + [jax.ShapeDtypeStruct((TOK, width), BF)] * 3,
        compiler_params=pltpu.CompilerParams(vmem_limit_bytes=6 << 20),
        cost_estimate=pl.CostEstimate(flops=2 * BLK * width, bytes_accessed=8 * BLK * width, transcendentals=0),
        name="own",
    )(p, up, down, after)


def scatter_z_y(p, marks):
    half = BLK // 2
    far = p[4 * BLK:5 * BLK]
    up, down = from_z(far[:half], -1), from_z(far[half:], 1)
    up, down = step(near_kernel, p, 3, 5, up, down, marks[0])
    for n, i, j in ((1, 2, 6), (2, 1, 7)):
        up, down = step(step_kernel, p, i, j, from_z(up, -1), from_z(down, 1), marks[n])
    own, *sent = own_of(p, from_z(up, -1), from_z(down, 1), marks[3])
    return total_of(own, [from_y(v, -k) for k, v in enumerate(sent, 1)], own)


def weigh_kernel(ids, flags, scale, cot, x, out):
    row = lax.broadcasted_iota(jnp.int32, cot.shape, 0)
    weight = jnp.zeros(cot.shape, F32)
    for r in range(TOK):
        w = (2 * flags[r] - 1).astype(F32) * scale[ids[r]]
        weight = jnp.where(row == r, w, weight)
    out[:TOK, :] = (cot[...].astype(F32) * weight).astype(BF)
    out[TOK:, :] = x[...]


def weigh(cotangent, inputs, pair_ids, flags, pair_scale):
    smem = pl.BlockSpec(memory_space=pltpu.SMEM)
    vmem = pl.BlockSpec(memory_space=pltpu.VMEM)
    return pl.pallas_call(
        weigh_kernel,
        in_specs=[smem, smem, smem, vmem, vmem],
        out_specs=vmem,
        out_shape=jax.ShapeDtypeStruct((2 * TOK, cotangent.shape[1]), BF),
        compiler_params=pltpu.CompilerParams(vmem_limit_bytes=60 << 20),
        cost_estimate=pl.CostEstimate(flops=cotangent.size, bytes_accessed=4 * cotangent.size, transcendentals=0),
        name="weigh",
    )(pair_ids, flags, pair_scale, cotangent, inputs)


def prep_kernel(s, mine, other, after, hidden_t, a_out, b_out, mark):
    y = s[3]
    same = lax.rem(lax.rem(s[2] + pl.program_id(0), NZ), NC) == s[1]

    def turned(i):
        rows = [pl.ds(pl.multiple_of(lax.rem(y + j, NY) * TOK, TOK), TOK) for j in range(NY)]
        got = [jnp.where(same, mine[0, i, r, :], other[0, i, r, :]) for r in rows]
        return jnp.concatenate(got, axis=0).astype(F32)

    g, u = turned(0), turned(1)
    sig = 1.0 / (1.0 + jnp.exp(-g))
    gs = g * sig
    a_out[...] = gs
    b_out[...] = u * sig * (1.0 + g * (1.0 - sig))
    hidden_t[...] = (gs * u).astype(BF).T
    mark[...] = jnp.zeros(mark.shape, F32)


def prep(place, mine, other, after):
    ff = mine.shape[-1]
    tokens = NZ * BLK

    def piece(t, s):
        block = lax.rem(s[2] + t, NZ)
        return (lax.rem(lax.div(block, NC) - s[0] + NX, NX), 0, 0, 0)

    spec = pl.BlockSpec((1, 2, BLK, ff), piece)
    return pl.pallas_call(
        prep_kernel,
        grid_spec=pltpu.PrefetchScalarGridSpec(
            num_scalar_prefetch=1,
            grid=(NZ,),
            in_specs=[
                spec,
                spec,
                pl.BlockSpec(memory_space=pl.ANY),
            ],
            out_specs=[
                pl.BlockSpec((ff, BLK), lambda t, s: (0, t)),
                pl.BlockSpec((BLK, ff), lambda t, s: (t, 0)),
                pl.BlockSpec((BLK, ff), lambda t, s: (t, 0)),
                pl.BlockSpec((8, 128), lambda t, s: (0, 0)),
            ],
        ),
        out_shape=[
            jax.ShapeDtypeStruct((ff, tokens), BF),
            jax.ShapeDtypeStruct((tokens, ff), F32),
            jax.ShapeDtypeStruct((tokens, ff), F32),
            jax.ShapeDtypeStruct((8, 128), F32),
        ],
        compiler_params=pltpu.CompilerParams(vmem_limit_bytes=8 << 20),
        cost_estimate=pl.CostEstimate(flops=30 * tokens * ff, bytes_accessed=14 * tokens * ff, transcendentals=0),
        name="prep",
    )(place, mine, other, after)


def turn_kernel(s, x_in, after, x_out, mark):
    x_out[...] = x_in[...].T
    mark[...] = jnp.zeros(mark.shape, F32)


def turn(place, x_all, after):
    tokens, width = x_all.shape
    return pl.pallas_call(
        turn_kernel,
        grid_spec=pltpu.PrefetchScalarGridSpec(
            num_scalar_prefetch=1,
            grid=(NZ,),
            in_specs=[
                pl.BlockSpec((BLK, width), lambda t, s: (lax.rem(s[2] + t, NZ), 0)),
                pl.BlockSpec(memory_space=pl.ANY),
            ],
            out_specs=[
                pl.BlockSpec((width, BLK), lambda t, s: (0, t)),
                pl.BlockSpec((8, 128), lambda t, s: (0, 0)),
            ],
        ),
        out_shape=[jax.ShapeDtypeStruct((width, tokens), BF), jax.ShapeDtypeStruct((8, 128), F32)],
        compiler_params=pltpu.CompilerParams(vmem_limit_bytes=8 << 20),
        cost_estimate=pl.CostEstimate(flops=0, bytes_accessed=4 * tokens * width, transcendentals=0),
        name="turn",
    )(place, x_all, after)


def nt(a, b):
    return lax.dot_general(a, b, (((1,), (1,)), ((), ())), preferred_element_type=F32)


def first_kernel(s, dy, w, out):
    x = s[0]
    for b in range(2):
        acc = nt(dy[b * 256:(b + 1) * 256, :], w[...]).astype(out.dtype)
        for h in range(2):
            t = 2 * b + h
            at = pl.multiple_of(lax.rem(t - x + NX, NX) * BLK, BLK)
            out[pl.ds(at, BLK), :] = acc[h * BLK:(h + 1) * BLK, :]


def first(place, dy_all, down_weight, flip, dtype):
    tokens, width = dy_all.shape
    ff = down_weight.shape[0]
    half = tokens // 2
    return pl.pallas_call(
        first_kernel,
        grid_spec=pltpu.PrefetchScalarGridSpec(
            num_scalar_prefetch=1,
            grid=(1,),
            in_specs=[
                pl.BlockSpec((half, width), lambda i, s: (lax.rem(s[1] + flip, NC), 0)),
                pl.BlockSpec((ff, width), lambda i, s: (0, 0)),
            ],
            out_specs=pl.BlockSpec((half, ff), lambda i, s: (0, 0)),
        ),
        out_shape=jax.ShapeDtypeStruct((half, ff), dtype),
        compiler_params=pltpu.CompilerParams(vmem_limit_bytes=14 << 20),
        cost_estimate=pl.CostEstimate(flops=2 * half * ff * width, bytes_accessed=2 * (half * width + ff * width + half * ff), transcendentals=0),
        name="first",
    )(place, dy_all, down_weight)


def second_kernel(s, m0, m1, o0, o1, a, b, gw, uw, dg, du, p):
    x, c = s[0], s[1]
    half = lax.div(pl.program_id(0), 2)
    same = half == c
    for h, (m, o) in enumerate(((m0, o0), (m1, o1))):
        rows = pl.ds(h * BLK, BLK)
        d = jnp.where(same, m[...], o[...]).astype(F32)
        du[rows, :] = (d * a[rows, :]).astype(BF)
        dg[rows, :] = (d * b[rows, :]).astype(BF)
    p[...] = (nt(dg[...], gw[...]) + nt(du[...], uw[...])).astype(BF)


def second(place, mine, other, a, b, gate_weight, up_weight):
    tokens, ff = a.shape
    width = gate_weight.shape[0]

    def at(h):
        return pl.BlockSpec(
            (BLK, ff), lambda t, s: (lax.rem(lax.rem(2 * t + h, NX) - s[0] + NX, NX), 0)
        )

    tile = 2 * BLK
    row = pl.BlockSpec((tile, ff), lambda t, s: (t, 0))
    whole = pl.BlockSpec((width, ff), lambda t, s: (0, 0))
    return pl.pallas_call(
        second_kernel,
        grid_spec=pltpu.PrefetchScalarGridSpec(
            num_scalar_prefetch=1,
            grid=(tokens // tile,),
            in_specs=[at(0), at(1), at(0), at(1), row, row, whole, whole],
            out_specs=[row, row, pl.BlockSpec((tile, width), lambda t, s: (t, 0))],
        ),
        out_shape=[
            jax.ShapeDtypeStruct((tokens, ff), BF),
            jax.ShapeDtypeStruct((tokens, ff), BF),
            jax.ShapeDtypeStruct((tokens, width), BF),
        ],
        compiler_params=pltpu.CompilerParams(vmem_limit_bytes=22 << 20),
        cost_estimate=pl.CostEstimate(flops=4 * tokens * ff * width, bytes_accessed=2 * (8 * tokens * ff + 2 * ff * width), transcendentals=0),
        name="second",
    )(place, mine, mine, other, other, a, b, gate_weight, up_weight)


def pack_kernel(g, u, after, out):
    out[0] = g[...]
    out[1] = u[...]


def pack(gate_pre, up_pre, after):
    vmem = pl.BlockSpec(memory_space=pltpu.VMEM)
    return pl.pallas_call(
        pack_kernel,
        in_specs=[vmem, vmem, pl.BlockSpec(memory_space=pl.ANY)],
        out_specs=vmem,
        out_shape=jax.ShapeDtypeStruct((2,) + gate_pre.shape, BF),
        compiler_params=pltpu.CompilerParams(vmem_limit_bytes=60 << 20),
        cost_estimate=pl.CostEstimate(flops=0, bytes_accessed=8 * gate_pre.size, transcendentals=0),
        name="pack",
    )(gate_pre, up_pre, after)


def total_kernel(own, r1, r2, r3, after, out):
    out[...] = (own[...] + r1[...].astype(F32) + r2[...].astype(F32) + r3[...].astype(F32)).astype(BF)


def total_of(own, parts, after):
    vmem = pl.BlockSpec(memory_space=pltpu.VMEM)
    return pl.pallas_call(
        total_kernel,
        in_specs=[vmem] * 4 + [pl.BlockSpec(memory_space=pl.ANY)],
        out_specs=vmem,
        out_shape=jax.ShapeDtypeStruct(own.shape, BF),
        compiler_params=pltpu.CompilerParams(vmem_limit_bytes=8 << 20),
        cost_estimate=pl.CostEstimate(flops=3 * own.size, bytes_accessed=12 * own.size, transcendentals=0),
        name="total",
    )(own, *parts, after)


def product_kernel(a, b, after, out, mark):
    out[...] = jnp.dot(a[...], b[...], preferred_element_type=F32).astype(BF)
    mark[...] = jnp.zeros(mark.shape, F32)


def product(a, b, tile, after):
    m, k = a.shape
    n = b.shape[1]
    return pl.pallas_call(
        product_kernel,
        grid=(m // tile,),
        in_specs=[
            pl.BlockSpec((tile, k), lambda i: (i, 0)),
            pl.BlockSpec((k, n), lambda i: (0, 0)),
            pl.BlockSpec(memory_space=pl.ANY),
        ],
        out_specs=[pl.BlockSpec((tile, n), lambda i: (i, 0)), pl.BlockSpec((8, 128), lambda i: (0, 0))],
        out_shape=[jax.ShapeDtypeStruct((m, n), BF), jax.ShapeDtypeStruct((8, 128), F32)],
        compiler_params=pltpu.CompilerParams(vmem_limit_bytes=14 << 20),
        cost_estimate=pl.CostEstimate(flops=2 * m * k * n, bytes_accessed=2 * (m * k + k * n + m * n), transcendentals=0),
        name="product",
    )(a, b, after)


def on_device(
    inputs,
    cotangent,
    gate_pre,
    up_pre,
    gate_weight,
    up_weight,
    down_weight,
    pair_ids,
    flags,
    pair_scale,
):
    row, col = lax.axis_index("row"), lax.axis_index("col")
    place = jnp.stack([row // NC, row % NC, col // NY, col % NY]).astype(jnp.int32)
    both = weigh(cotangent, inputs, pair_ids, flags, pair_scale)
    rows = [both] + [from_y(both, k) for k in range(1, NY)]
    x_all = lax.all_gather(
        jnp.concatenate([v[TOK:] for v in rows], axis=0),
        "col",
        axis=0,
        tiled=True,
        axis_index_groups=[[z * NY + y for z in range(NZ)] for y in range(NY)],
    )
    dy_all, pre_mine = gather_z(
        jnp.concatenate([v[:TOK] for v in rows], axis=0),
        lambda v: pack(gate_pre, up_pre, v),
    )
    pre_other = from_core(pre_mine)

    sent = first(place, dy_all, down_weight, 1, BF)
    theirs = from_core(sent)
    hidden_t, a, b, ready = prep(place, pre_mine, pre_other, x_all[:16, :128])
    pair = first(place, dy_all, down_weight, 0, F32) + theirs.astype(F32)
    pair = pair.reshape(NX, BLK, -1)
    total = total_of(pair[0], [from_x(pair[k].astype(BF), -k) for k in range(1, NX)], ready)
    mine = jnp.concatenate([total] + [from_x(total, k) for k in range(1, NX)], axis=0)
    other = from_core(mine)
    d_gate, d_up, part = second(place, mine, other, a, b, gate_weight, up_weight)
    grad_down, mark_0 = product(hidden_t, dy_all, 448, part[:8, :128])
    x_t, mark_1 = turn(place, x_all, mark_0)
    grad_gate, mark_2 = product(x_t, d_gate, 512, mark_1)
    grad_up, mark_3 = product(x_t, d_up, 512, mark_2)
    grad_input = scatter_z_y(part, (mark_0, mark_1, mark_2, mark_3))
    return (grad_input, grad_gate, grad_up, grad_down)


def solution(mesh):
    return jax.shard_map(
        on_device,
        mesh=mesh,
        in_specs=(
            P("col", "row"),
            P("col", "row"),
            P("row", "col"),
            P("row", "col"),
            P("row", "col"),
            P("row", "col"),
            P("col", "row"),
            P("col"),
            P("col"),
            P(),
        ),
        out_specs=(P("col", "row"), P("row", "col"), P("row", "col"), P("col", "row")),
        check_vma=False,
    )
```

time: 535 us -> 168 us (0.31)
  waiting for transfers between devices: 469 us -> 62.5 us
  starting transfers between devices: 0.28 us -> 48.1 us
  matrix products: 36.2 us -> 0 us
  Pallas kernels: 0 us -> 33.3 us
    reduce_scatter x2 -> x0, waiting for transfers between devices: 257 us -> none  [the longest x1 219 us: on_device(): lax.psum_scatter(right_transposed(gate_grads, gate_weight) + right_transp...]
    all_gather x5 -> x1, waiting for transfers between devices: 209 us -> 0.02 us  [on_device(): lax.all_gather(jnp.concatenate([v[TOK:] for v in rows], axis=0), 'col', a...]
    ppermute x0 -> x34, waiting for transfers between devices: none -> 62.4 us  [the longest x16 24.2 us: from_z(): return lax.ppermute(v, 'col', perm)]
    ppermute x0 -> x34, starting transfers between devices: none -> 48 us  [the longest x16 28.3 us: from_z(): return lax.ppermute(v, 'col', perm)]
    dot_general x6 -> x0, matrix products: 36.2 us -> none  [the longest x3 19.7 us: right_transposed(): lax.dot_general(left, right, (((1,), (1,)), ((), ())), preferred_element_...]
    pallas_call x0 -> x17, Pallas kernels: none -> 33.3 us  [the longest x3 10 us: product(): pl.pallas_call(product_kernel, grid=(m // tile,), in_specs=[pl.BlockSpec(...]
  transfers between devices with their start and end apart: 7 -> 35, of which waited for: 7 -> 23; matrix products, arithmetic and copies ran while one was open for 7% -> 5% of each run, Pallas kernels for 0% -> 15%
where the time goes in v1:
time: 168 us; the launch traced here: 167 us
  waiting for transfers between devices  62.5 us (37%)
  starting transfers between devices  48.1 us (29%)
  Pallas kernels  33.3 us (20%)
  between operations  14.3 us (9%)
  local copies, waits for them, and re-layouts  6.47 us (4%)
  other arithmetic  2.6 us (2%)
    ppermute x16, starting transfers between devices, from_z(): return lax.ppermute(v, 'col', perm)  28.3 us
    ppermute x16, waiting for transfers between devices, from_z(): return lax.ppermute(v, 'col', perm)  24.2 us
    ppermute x9, waiting for transfers between devices, from_x(): return lax.ppermute(v, 'row', perm)  23.2 us
    ppermute x9, starting transfers between devices, from_x(): return lax.ppermute(v, 'row', perm)  13.7 us
    ppermute x6, waiting for transfers between devices, from_y(): return lax.ppermute(v, 'col', perm)  12 us
    pallas_call x3, Pallas kernels, product(): pl.pallas_call(product_kernel, grid=(m // tile,), in_specs=[pl.BlockSpec(...  10 us
    pallas_call x1, Pallas kernels, prep(): pl.pallas_call(prep_kernel, grid_spec=pltpu.PrefetchScalarGridSpec(num_sc...  7.16 us
    ppermute x6, starting transfers between devices, from_y(): return lax.ppermute(v, 'col', perm)  5.87 us
  transfers between devices with their start and end apart: 35, of which 23 were waited for; matrix products, arithmetic and copies ran while one was open for 5% of the time, Pallas kernels for 15%

profile of v1, /device:TPU:24, one launch (start us, length us, event | category | flops | bytes accessed | tf_op | source)
XLA Modules:
  0.0 167.2 jit_solution(2399904909906445813)
XLA Ops:
  7.2 1.6 weigh.1
  8.8 2.0 %collective-permute-start.2 = (bf16[64,1024]{1,0:T(8,128)(2,1)}, bf16[64,1024]{1,0:T(8,128)(2,1)S(1)}, u32[]{:S(2)}, u32[]{:S(2)}) collective-permute-start(bf16[64,1024]{1,0:T(8,128)(2,1)} %weigh.1), channel_id=1, source_target_pairs={{0,1},{1,2},{2,3},{3,0},{4,5},{5,6},{6,7},{7,4},{8,9},{9,10},{10,1... | collective-permute-start | bytes 393224 | tf_op jit(solution)/shard_map/ppermute | solution.py:21
  12.6 6.6 %collective-permute-done = bf16[64,1024]{1,0:T(8,128)(2,1)S(1)} collective-permute-done((bf16[64,1024]{1,0:T(8,128)(2,1)}, bf16[64,1024]{1,0:T(8,128)(2,1)S(1)}, u32[]{:S(2)}, u32[]{:S(2)}) %collective-permute-start) | collective-permute-done | bytes 131104 | tf_op jit(solution)/shard_map/ppermute | solution.py:21
  20.0 1.4 collective-permute-start.6
  21.4 4.0 %collective-permute-start.3 = (bf16[128,1024]{1,0:T(8,128)(2,1)S(1)}, bf16[128,1024]{1,0:T(8,128)(2,1)}, u32[]{:S(2)}, u32[]{:S(2)}) collective-permute-start(bf16[128,1024]{1,0:T(8,128)(2,1)S(1)} %pad_maximum_fusion.2), channel_id=1, source_target_pairs={{0,28},{1,29},{2,30},{3,31},{4,0},{5,1},{6,2},{7,3},{8,4},{9,5},{1... | collective-permute-start | bytes 786440 | tf_op jit(solution)/shard_map/ppermute | solution.py:16
  25.5 5.7 %collective-permute-done.6 = bf16[128,1024]{1,0:T(8,128)(2,1)} collective-permute-done((bf16[128,1024]{1,0:T(8,128)(2,1)S(1)}, bf16[128,1024]{1,0:T(8,128)(2,1)}, u32[]{:S(2)}, u32[]{:S(2)}) %collective-permute-start.6) | collective-permute-done | bytes 262176 | tf_op jit(solution)/shard_map/ppermute | solution.py:16
  31.2 3.2 %collective-permute-start.4 = (bf16[128,1024]{1,0:T(8,128)(2,1)}, bf16[128,1024]{1,0:T(8,128)(2,1)}, u32[]{:S(2)}, u32[]{:S(2)}) collective-permute-start(bf16[128,1024]{1,0:T(8,128)(2,1)} %collective-permute-done.3.after), channel_id=1, source_target_pairs={{0,28},{1,29},{2,30},{3,31},{4,0},{5,1},{6,2},{7,3},{8,4},{9,5},{1... | collective-permute-start | bytes 786440 | tf_op jit(solution)/shard_map/ppermute | solution.py:16
  34.4 1.8 %pack.1 = bf16[2,128,896]{2,1,0:T(8,128)(2,1)} custom-call(bf16[128,896]{1,0:T(8,128)(2,1)} %g.1, bf16[128,896]{1,0:T(8,128)(2,1)} %u.1, bf16[128,1024]{1,0:T(8,128)(2,1)} %collective-permute-done.3.after), custom_call_target="tpu_custom_call" | custom-call | bytes 917504 | tf_op jit(solution)/shard_map/pack/pallas_call | solution.py:333
  36.2 1.5 collective-permute-start.11
  37.7 2.7 %collective-permute-start.10 = (bf16[2,128,896]{2,1,0:T(8,128)(2,1)}, bf16[2,128,896]{2,1,0:T(8,128)(2,1)S(1)}, u32[]{:S(2)}, u32[]{:S(2)}) collective-permute-start(bf16[2,128,896]{2,1,0:T(8,128)(2,1)} %pack.1), channel_id=1, source_target_pairs={{0,128},{32,160},{64,192},{96,224},{128,0},{160,32},{192,64},{224,... | collective-permute-start | bytes 1376264 | tf_op jit(solution)/shard_map/ppermute | solution.py:26
  40.5 1.4 collective-permute-start.9
  41.9 1.2 collective-permute-done.7
  43.1 1.5 collective-permute-done.4
  44.6 3.7 %collective-permute-start.5 = (bf16[128,1024]{1,0:T(8,128)(2,1)}, bf16[128,1024]{1,0:T(8,128)(2,1)S(1)}, u32[]{:S(2)}, u32[]{:S(2)}) collective-permute-start(bf16[128,1024]{1,0:T(8,128)(2,1)} %collective-permute-done.4), channel_id=1, source_target_pairs={{0,28},{1,29},{2,30},{3,31},{4,0},{5,1},{6,2},{7,3},{8,4},{9,5},{1... | collective-permute-start | bytes 786440 | tf_op jit(solution)/shard_map/ppermute | solution.py:16
  49.4 1.0 constant_dynamic-update-slice_fusion.6
  50.4 8.6 %collective-permute-done.10.r2 = bf16[2,128,896]{2,1,0:T(8,128)(2,1)S(1)} collective-permute-done((bf16[2,128,896]{2,1,0:T(8,128)(2,1)}, bf16[2,128,896]{2,1,0:T(8,128)(2,1)S(1)}, u32[]{:S(2)}, u32[]{:S(2)}) %collective-permute-start.10) | collective-permute-done | bytes 458784 | tf_op jit(solution)/shard_map/ppermute | solution.py:26
  59.6 3.7 %collective-permute-start.12 = (bf16[64,1024]{1,0:T(8,128)(2,1)S(1)}, bf16[64,1024]{1,0:T(8,128)(2,1)S(1)}, u32[]{:S(2)}, u32[]{:S(2)}) collective-permute-start(bf16[64,1024]{1,0:T(8,128)(2,1)S(1)} %get-tuple-element.31), channel_id=1, source_target_pairs={{0,28},{1,29},{2,30},{3,31},{4,0},{5,1},{6,2},{7,3},{8,4},{9,5},{1... | collective-permute-start | bytes 393224 | tf_op jit(solution)/shard_map/ppermute | solution.py:16
  63.2 1.5 pad_maximum_fusion.mine
  64.8 1.9 %collective-permute-done.12 = bf16[64,1024]{1,0:T(8,128)(2,1)S(1)} collective-permute-done((bf16[64,1024]{1,0:T(8,128)(2,1)S(1)}, bf16[64,1024]{1,0:T(8,128)(2,1)S(1)}, u32[]{:S(2)}, u32[]{:S(2)}) %collective-permute-start.12) | collective-permute-done | bytes 131104 | tf_op jit(solution)/shard_map/ppermute | solution.py:16
  66.7 5.1 %collective-permute-done.13 = bf16[64,1024]{1,0:T(8,128)(2,1)S(1)} collective-permute-done((bf16[64,1024]{1,0:T(8,128)(2,1)S(1)}, bf16[64,1024]{1,0:T(8,128)(2,1)S(1)}, u32[]{:S(2)}, u32[]{:S(2)}) %collective-permute-start.13) | collective-permute-done | bytes 131104 | tf_op jit(solution)/shard_map/ppermute | solution.py:16
  72.9 1.0 constant_dynamic-update-slice_fusion.dy.b
  73.9 1.8 %first.3 = bf16[512,896]{1,0:T(8,128)(2,1)S(1)} custom-call(s32[4]{0:T(128)S(1)} %pad_add_fusion.s, bf16[1024,1024]{1,0:T(8,128)(2,1)S(1)} %constant_dynamic-update-slice_fusion.dy.b, bf16[896,1024]{1,0:T(8,128)(2,1)S(1)} %copy-done), custom_call_target="tpu_custom_call" | custom-call | flops 939524096 | bytes 3801088 | tf_op jit(solution)/shard_map/first/pallas_call | solution.py:265
  75.8 1.8 %first.2 = f32[512,896]{1,0:T(8,128)S(1)} custom-call(s32[4]{0:T(128)S(1)} %pad_add_fusion.s, bf16[1024,1024]{1,0:T(8,128)(2,1)S(1)} %constant_dynamic-update-slice_fusion.dy.b, bf16[896,1024]{1,0:T(8,128)(2,1)S(1)} %copy-done), custom_call_target="tpu_custom_call" | custom-call | flops 939524096 | bytes 3801088 | tf_op jit(solution)/shard_map/first/pallas_call | solution.py:265
  79.3 2.2 %collective-permute-start.17 = (bf16[128,896]{1,0:T(8,128)(2,1)}, bf16[128,896]{1,0:T(8,128)(2,1)S(1)}, u32[]{:S(2)}, u32[]{:S(2)}) collective-permute-start(bf16[128,896]{1,0:T(8,128)(2,1)} %get-tuple-element.62), channel_id=1, source_target_pairs={{0,192},{32,224},{64,0},{96,32},{128,64},{160,96},{192,128},{224,1... | collective-permute-start | bytes 688136 | tf_op jit(solution)/shard_map/ppermute | solution.py:26
  82.2 1.4 collective-permute-start.15
  84.4 7.2 %prep.1 = (bf16[896,1024]{1,0:T(8,128)(2,1)S(1)}, f32[1024,896]{1,0:T(8,128)S(1)}, f32[1024,896]{1,0:T(8,128)S(1)}, f32[8,128]{1,0:T(8,128)S(1)}) custom-call(s32[4]{0:T(128)S(1)} %pad_add_fusion.s, bf16[4,2,128,896]{3,2,1,0:T(8,128)(2,1)} %pad_maximum_fusion.mine, bf16[4,2,128,896]{3,2,1,0:T(8,128)(2,1)} %collective-permute-done.18.other, ...), custom_call_target="tpu_custom_call" | custom-call | flops 27525120 | bytes 12845056 | tf_op jit(solution)/shard_map/prep/pallas_call | solution.py:190
  91.9 3.6 %collective-permute-done.15.r1 = bf16[128,896]{1,0:T(8,128)(2,1)S(1)} collective-permute-done((bf16[128,896]{1,0:T(8,128)(2,1)S(1)}, bf16[128,896]{1,0:T(8,128)(2,1)S(1)}, u32[]{:S(2)}, u32[]{:S(2)}) %collective-permute-start.15) | collective-permute-done | bytes 229408 | tf_op jit(solution)/shard_map/ppermute | solution.py:26
  95.7 2.1 %collective-permute-start.20 = (bf16[128,896]{1,0:T(8,128)(2,1)S(1)}, bf16[128,896]{1,0:T(8,128)(2,1)S(1)}, u32[]{:S(2)}, u32[]{:S(2)}) collective-permute-start(bf16[128,896]{1,0:T(8,128)(2,1)S(1)} %total.2), channel_id=1, source_target_pairs={{0,128},{32,160},{64,192},{96,224},{128,0},{160,32},{192,64},{224,... | collective-permute-start | bytes 688136 | tf_op jit(solution)/shard_map/ppermute | solution.py:26
  97.7 1.5 collective-permute-start.19
  99.3 10.0 %collective-permute-done.21 = bf16[128,896]{1,0:T(8,128)(2,1)S(1)} collective-permute-done((bf16[128,896]{1,0:T(8,128)(2,1)S(1)}, bf16[128,896]{1,0:T(8,128)(2,1)S(1)}, u32[]{:S(2)}, u32[]{:S(2)}) %collective-permute-start.21) | collective-permute-done | bytes 229408 | tf_op jit(solution)/shard_map/ppermute | solution.py:26
  110.1 2.5 %collective-permute-done.22.o0.o1 = bf16[512,896]{1,0:T(8,128)(2,1)S(1)} collective-permute-done((bf16[512,896]{1,0:T(8,128)(2,1)S(1)}, bf16[512,896]{1,0:T(8,128)(2,1)S(1)}, u32[]{:S(2)}, u32[]{:S(2)}) %collective-permute-start.22) | collective-permute-done | bytes 917536 | tf_op jit(solution)/shard_map/ppermute | solution.py:30
  112.6 5.7 %second.1 = (bf16[1024,896]{1,0:T(8,128)(2,1)S(1)}, bf16[1024,896]{1,0:T(8,128)(2,1)S(1)}, bf16[1024,1024]{1,0:T(8,128)(2,1)S(1)}) custom-call(s32[4]{0:T(128)S(1)} %pad_add_fusion.s, bf16[512,896]{1,0:T(8,128)(2,1)S(1)} %pad_maximum_fusion.1.m0.m1, bf16[512,896]{1,0:T(8,128)(2,1)S(1)} %pad_maximum_fusion.1.m0.m1, ...), custom_call_target="tpu_custom_call" | custom-call | flops 3758096384 | bytes 18350080 | tf_op jit(solution)/shard_map/second/pallas_call | solution.py:307
  118.5 2.0 %collective-permute-start.23 = (bf16[64,1024]{1,0:T(8,128)(2,1)S(1)}, bf16[64,1024]{1,0:T(8,128)(2,1)S(1)}, u32[]{:S(2)}, u32[]{:S(2)}) collective-permute-start(bf16[64,1024]{1,0:T(8,128)(2,1)S(1)} %get-tuple-element.61), channel_id=1, source_target_pairs={{0,4},{1,5},{2,6},{3,7},{4,8},{5,9},{6,10},{7,11},{8,12},{9,13},{1... | collective-permute-start | bytes 393224 | tf_op jit(solution)/shard_map/ppermute | solution.py:16
  120.5 3.2 %product.3 = (bf16[896,1024]{1,0:T(8,128)(2,1)}, f32[8,128]{1,0:T(8,128)S(1)}) custom-call(bf16[896,1024]{1,0:T(8,128)(2,1)S(1)} %get-tuple-element.37.a, bf16[1024,1024]{1,0:T(8,128)(2,1)S(1)} %constant_dynamic-update-slice_fusion.dy.b, bf16[8,128]{1,0:T(8,128)(2,1)S(1)} %slice.73.after), custom_call_target="tpu_custom_call" | custom-call | flops 1879048192 | bytes 5767168 | tf_op jit(solution)/shard_map/product/pallas_call | solution.py:369
  124.0 1.3 collective-permute-done.23.up
  126.1 2.8 %collective-permute-start.26 = (bf16[128,1024]{1,0:T(8,128)(2,1)S(1)}, bf16[128,1024]{1,0:T(8,128)(2,1)S(1)}, u32[]{:S(2)}, u32[]{:S(2)}) collective-permute-start(bf16[128,1024]{1,0:T(8,128)(2,1)S(1)} %get-tuple-element.40), channel_id=1, source_target_pairs={{0,28},{1,29},{2,30},{3,31},{4,0},{5,1},{6,2},{7,3},{8,4},{9,5},{1... | collective-permute-start | bytes 786440 | tf_op jit(solution)/shard_map/ppermute | solution.py:16
  128.9 2.1 %turn.1 = (bf16[1024,1024]{1,0:T(8,128)(2,1)S(1)}, f32[8,128]{1,0:T(8,128)S(1)}) custom-call(s32[4]{0:T(128)S(1)} %pad_add_fusion.s, bf16[1024,1024]{1,0:T(8,128)(2,1)S(1)} %copy-done.1, f32[8,128]{1,0:T(8,128)S(1)} %get-tuple-element.38.after), custom_call_target="tpu_custom_call" | custom-call | bytes 4194304 | tf_op jit(solution)/shard_map/turn/pallas_call | solution.py:226
  131.0 3.4 %collective-permute-done.25.up = bf16[128,1024]{1,0:T(8,128)(2,1)S(1)} collective-permute-done((bf16[128,1024]{1,0:T(8,128)(2,1)S(1)}, bf16[128,1024]{1,0:T(8,128)(2,1)S(1)}, u32[]{:S(2)}, u32[]{:S(2)}) %collective-permute-start.25) | collective-permute-done | bytes 262176 | tf_op jit(solution)/shard_map/ppermute | solution.py:16
  134.6 3.2 %collective-permute-start.28 = (bf16[128,1024]{1,0:T(8,128)(2,1)S(1)}, bf16[128,1024]{1,0:T(8,128)(2,1)S(1)}, u32[]{:S(2)}, u32[]{:S(2)}) collective-permute-start(bf16[128,1024]{1,0:T(8,128)(2,1)S(1)} %get-tuple-element.43), channel_id=1, source_target_pairs={{0,28},{1,29},{2,30},{3,31},{4,0},{5,1},{6,2},{7,3},{8,4},{9,5},{1... | collective-permute-start | bytes 786440 | tf_op jit(solution)/shard_map/ppermute | solution.py:16
  137.8 3.4 %product.4 = (bf16[1024,896]{1,0:T(8,128)(2,1)}, f32[8,128]{1,0:T(8,128)S(1)}) custom-call(bf16[1024,1024]{1,0:T(8,128)(2,1)S(1)} %get-tuple-element.44.a, bf16[1024,896]{1,0:T(8,128)(2,1)S(1)} %get-tuple-element.45.b, f32[8,128]{1,0:T(8,128)S(1)} %get-tuple-element.41.after), custom_call_target="tpu_custom_call" | custom-call | flops 1879048192 | bytes 5767168 | tf_op jit(solution)/shard_map/product/pallas_call | solution.py:369
  141.3 1.1 collective-permute-done.27.up
  142.5 2.2 %collective-permute-start.29 = (bf16[128,1024]{1,0:T(8,128)(2,1)S(1)}, bf16[128,1024]{1,0:T(8,128)(2,1)S(1)}, u32[]{:S(2)}, u32[]{:S(2)}) collective-permute-start(bf16[128,1024]{1,0:T(8,128)(2,1)S(1)} %get-tuple-element.47), channel_id=1, source_target_pairs={{0,4},{1,5},{2,6},{3,7},{4,8},{5,9},{6,10},{7,11},{8,12},{9,13},{1... | collective-permute-start | bytes 786440 | tf_op jit(solution)/shard_map/ppermute | solution.py:16
  144.8 1.1 collective-permute-start.30
  145.8 3.4 %product.5 = (bf16[1024,896]{1,0:T(8,128)(2,1)}, f32[8,128]{1,0:T(8,128)S(1)}) custom-call(bf16[1024,1024]{1,0:T(8,128)(2,1)S(1)} %get-tuple-element.44.a, bf16[1024,896]{1,0:T(8,128)(2,1)S(1)} %get-tuple-element.49.b, f32[8,128]{1,0:T(8,128)S(1)} %get-tuple-element.46.after), custom_call_target="tpu_custom_call" | custom-call | flops 1879048192 | bytes 5767168 | tf_op jit(solution)/shard_map/product/pallas_call | solution.py:369
  152.1 2.2 %collective-permute-start.32 = (bf16[32,1024]{1,0:T(8,128)(2,1)S(1)}, bf16[32,1024]{1,0:T(8,128)(2,1)S(1)}, u32[]{:S(2)}, u32[]{:S(2)}) collective-permute-start(bf16[32,1024]{1,0:T(8,128)(2,1)S(1)} %get-tuple-element.53), channel_id=1, source_target_pairs={{0,2},{1,3},{2,0},{3,1},{4,6},{5,7},{6,4},{7,5},{8,10},{9,11},{10,... | collective-permute-start | bytes 196616 | tf_op jit(solution)/shard_map/ppermute | solution.py:21
  154.3 1.3 collective-permute-done.31.r1
  155.6 2.2 %collective-permute-done.32.r2 = bf16[32,1024]{1,0:T(8,128)(2,1)S(1)} collective-permute-done((bf16[32,1024]{1,0:T(8,128)(2,1)S(1)}, bf16[32,1024]{1,0:T(8,128)(2,1)S(1)}, u32[]{:S(2)}, u32[]{:S(2)}) %collective-permute-start.32) | collective-permute-done | bytes 65568 | tf_op jit(solution)/shard_map/ppermute | solution.py:21
  157.8 1.9 %collective-permute-done.33.r3 = bf16[32,1024]{1,0:T(8,128)(2,1)S(1)} collective-permute-done((bf16[32,1024]{1,0:T(8,128)(2,1)S(1)}, bf16[32,1024]{1,0:T(8,128)(2,1)S(1)}, u32[]{:S(2)}, u32[]{:S(2)}) %collective-permute-start.33) | collective-permute-done | bytes 65568 | tf_op jit(solution)/shard_map/ppermute | solution.py:21
  (73 shorter events, 15.0 us)
Async XLA Ops:
  7.2 76.5 %all-gather.2.cloned.1.call-start = ((), (), s32[]{:S(2)}) async-start(), calls=%async_computation | async-start | bytes 2359296 | tf_op jit(solution)/shard_map/all_gather | solution.py:401
  8.8 10.4 %collective-permute-start.2 = (bf16[64,1024]{1,0:T(8,128)(2,1)}, bf16[64,1024]{1,0:T(8,128)(2,1)S(1)}, u32[]{:S(2)}, u32[]{:S(2)}) collective-permute-start(bf16[64,1024]{1,0:T(8,128)(2,1)} %weigh.1), channel_id=1, source_target_pairs={{0,1},{1,2},{2,3},{3,0},{4,5},{5,6},{6,7},{7,4},{8,9},{9,10},{10,1... | collective-permute-start | bytes 393224 | tf_op jit(solution)/shard_map/ppermute | solution.py:21
  10.8 8.4 %collective-permute-start.1 = (bf16[64,1024]{1,0:T(8,128)(2,1)}, bf16[64,1024]{1,0:T(8,128)(2,1)S(1)}, u32[]{:S(2)}, u32[]{:S(2)}) collective-permute-start(bf16[64,1024]{1,0:T(8,128)(2,1)} %weigh.1), channel_id=1, source_target_pairs={{0,2},{1,3},{2,0},{3,1},{4,6},{5,7},{6,4},{7,5},{8,10},{9,11},{10,... | collective-permute-start | bytes 393224 | tf_op jit(solution)/shard_map/ppermute | solution.py:21
  11.6 7.5 %collective-permute-start = (bf16[64,1024]{1,0:T(8,128)(2,1)}, bf16[64,1024]{1,0:T(8,128)(2,1)S(1)}, u32[]{:S(2)}, u32[]{:S(2)}) collective-permute-start(bf16[64,1024]{1,0:T(8,128)(2,1)} %weigh.1), channel_id=1, source_target_pairs={{0,3},{1,0},{2,1},{3,2},{4,7},{5,4},{6,5},{7,6},{8,11},{9,8},{10,9... | collective-permute-start | bytes 393224 | tf_op jit(solution)/shard_map/ppermute | solution.py:21
  20.0 11.2 %collective-permute-start.6 = (bf16[128,1024]{1,0:T(8,128)(2,1)S(1)}, bf16[128,1024]{1,0:T(8,128)(2,1)}, u32[]{:S(2)}, u32[]{:S(2)}) collective-permute-start(bf16[128,1024]{1,0:T(8,128)(2,1)S(1)} %pad_maximum_fusion.2), channel_id=1, source_target_pairs={{0,4},{1,5},{2,6},{3,7},{4,8},{5,9},{6,10},{7,11},{8,12},{9,13},{1... | collective-permute-start | bytes 786440 | tf_op jit(solution)/shard_map/ppermute | solution.py:16
  21.4 9.7 %collective-permute-start.3 = (bf16[128,1024]{1,0:T(8,128)(2,1)S(1)}, bf16[128,1024]{1,0:T(8,128)(2,1)}, u32[]{:S(2)}, u32[]{:S(2)}) collective-permute-start(bf16[128,1024]{1,0:T(8,128)(2,1)S(1)} %pad_maximum_fusion.2), channel_id=1, source_target_pairs={{0,28},{1,29},{2,30},{3,31},{4,0},{5,1},{6,2},{7,3},{8,4},{9,5},{1... | collective-permute-start | bytes 786440 | tf_op jit(solution)/shard_map/ppermute | solution.py:16
  31.2 11.9 %collective-permute-start.7 = (bf16[128,1024]{1,0:T(8,128)(2,1)}, bf16[128,1024]{1,0:T(8,128)(2,1)}, u32[]{:S(2)}, u32[]{:S(2)}) collective-permute-start(bf16[128,1024]{1,0:T(8,128)(2,1)} %collective-permute-done.6), channel_id=1, source_target_pairs={{0,4},{1,5},{2,6},{3,7},{4,8},{5,9},{6,10},{7,11},{8,12},{9,13},{1... | collective-permute-start | bytes 786440 | tf_op jit(solution)/shard_map/ppermute | solution.py:16
  31.2 13.5 %collective-permute-start.4 = (bf16[128,1024]{1,0:T(8,128)(2,1)}, bf16[128,1024]{1,0:T(8,128)(2,1)}, u32[]{:S(2)}, u32[]{:S(2)}) collective-permute-start(bf16[128,1024]{1,0:T(8,128)(2,1)} %collective-permute-done.3.after), channel_id=1, source_target_pairs={{0,28},{1,29},{2,30},{3,31},{4,0},{5,1},{6,2},{7,3},{8,4},{9,5},{1... | collective-permute-start | bytes 786440 | tf_op jit(solution)/shard_map/ppermute | solution.py:16
  36.2 14.1 %collective-permute-start.11 = (bf16[2,128,896]{2,1,0:T(8,128)(2,1)}, bf16[2,128,896]{2,1,0:T(8,128)(2,1)S(1)}, u32[]{:S(2)}, u32[]{:S(2)}) collective-permute-start(bf16[2,128,896]{2,1,0:T(8,128)(2,1)} %pack.1), channel_id=1, source_target_pairs={{0,64},{32,96},{64,128},{96,160},{128,192},{160,224},{192,0},{224,... | collective-permute-start | bytes 1376264 | tf_op jit(solution)/shard_map/ppermute | solution.py:26
  37.7 21.2 %collective-permute-start.10 = (bf16[2,128,896]{2,1,0:T(8,128)(2,1)}, bf16[2,128,896]{2,1,0:T(8,128)(2,1)S(1)}, u32[]{:S(2)}, u32[]{:S(2)}) collective-permute-start(bf16[2,128,896]{2,1,0:T(8,128)(2,1)} %pack.1), channel_id=1, source_target_pairs={{0,128},{32,160},{64,192},{96,224},{128,0},{160,32},{192,64},{224,... | collective-permute-start | bytes 1376264 | tf_op jit(solution)/shard_map/ppermute | solution.py:26
  40.5 18.4 %collective-permute-start.9 = (bf16[2,128,896]{2,1,0:T(8,128)(2,1)}, bf16[2,128,896]{2,1,0:T(8,128)(2,1)S(1)}, u32[]{:S(2)}, u32[]{:S(2)}) collective-permute-start(bf16[2,128,896]{2,1,0:T(8,128)(2,1)} %pack.1), channel_id=1, source_target_pairs={{0,192},{32,224},{64,0},{96,32},{128,64},{160,96},{192,128},{224,1... | collective-permute-start | bytes 1376264 | tf_op jit(solution)/shard_map/ppermute | solution.py:26
  41.9 21.3 %copy-start.4 = (bf16[2,128,896]{2,1,0:T(8,128)(2,1)S(1)}, bf16[2,128,896]{2,1,0:T(8,128)(2,1)}, u32[]{:S(2)}) copy-start(bf16[2,128,896]{2,1,0:T(8,128)(2,1)} %pack.1) | copy-start | bytes 1376260
  43.1 15.8 %collective-permute-start.8 = (bf16[128,1024]{1,0:T(8,128)(2,1)}, bf16[128,1024]{1,0:T(8,128)(2,1)S(1)}, u32[]{:S(2)}, u32[]{:S(2)}) collective-permute-start(bf16[128,1024]{1,0:T(8,128)(2,1)} %collective-permute-done.7), channel_id=1, source_target_pairs={{0,4},{1,5},{2,6},{3,7},{4,8},{5,9},{6,10},{7,11},{8,12},{9,13},{1... | collective-permute-start | bytes 786440 | tf_op jit(solution)/shard_map/ppermute | solution.py:16
  44.6 14.9 %collective-permute-start.5 = (bf16[128,1024]{1,0:T(8,128)(2,1)}, bf16[128,1024]{1,0:T(8,128)(2,1)S(1)}, u32[]{:S(2)}, u32[]{:S(2)}) collective-permute-start(bf16[128,1024]{1,0:T(8,128)(2,1)} %collective-permute-done.4), channel_id=1, source_target_pairs={{0,28},{1,29},{2,30},{3,31},{4,0},{5,1},{6,2},{7,3},{8,4},{9,5},{1... | collective-permute-start | bytes 786440 | tf_op jit(solution)/shard_map/ppermute | solution.py:16
  59.6 7.1 %collective-permute-start.12 = (bf16[64,1024]{1,0:T(8,128)(2,1)S(1)}, bf16[64,1024]{1,0:T(8,128)(2,1)S(1)}, u32[]{:S(2)}, u32[]{:S(2)}) collective-permute-start(bf16[64,1024]{1,0:T(8,128)(2,1)S(1)} %get-tuple-element.31), channel_id=1, source_target_pairs={{0,28},{1,29},{2,30},{3,31},{4,0},{5,1},{6,2},{7,3},{8,4},{9,5},{1... | collective-permute-start | bytes 393224 | tf_op jit(solution)/shard_map/ppermute | solution.py:16
  64.7 9.1 %copy-start = (bf16[896,1024]{1,0:T(8,128)(2,1)S(1)}, bf16[896,1024]{1,0:T(8,128)(2,1)}, u32[]{:S(2)}) copy-start(bf16[896,1024]{1,0:T(8,128)(2,1)} %w.3) | copy-start | bytes 5505028
  64.7 19.6 %collective-permute-start.18 = (bf16[4,2,128,896]{3,2,1,0:T(8,128)(2,1)}, bf16[4,2,128,896]{3,2,1,0:T(8,128)(2,1)}, u32[]{:S(2)}, u32[]{:S(2)}) collective-permute-start(bf16[4,2,128,896]{3,2,1,0:T(8,128)(2,1)} %pad_maximum_fusion.mine), channel_id=1, source_target_pairs={{0,32},{32,0},{64,96},{96,64},{128,160},{160,128},{192,224},{224,1... | collective-permute-start | bytes 5505032 | tf_op jit(solution)/shard_map/ppermute | solution.py:30
  64.7 7.1 %collective-permute-start.13 = (bf16[64,1024]{1,0:T(8,128)(2,1)S(1)}, bf16[64,1024]{1,0:T(8,128)(2,1)S(1)}, u32[]{:S(2)}, u32[]{:S(2)}) collective-permute-start(bf16[64,1024]{1,0:T(8,128)(2,1)S(1)} %get-tuple-element.32), channel_id=1, source_target_pairs={{0,4},{1,5},{2,6},{3,7},{4,8},{5,9},{6,10},{7,11},{8,12},{9,13},{1... | collective-permute-start | bytes 393224 | tf_op jit(solution)/shard_map/ppermute | solution.py:16
  75.7 2.6 %collective-permute-start.14 = (bf16[512,896]{1,0:T(8,128)(2,1)S(1)}, bf16[512,896]{1,0:T(8,128)(2,1)S(1)}, u32[]{:S(2)}, u32[]{:S(2)}) collective-permute-start(bf16[512,896]{1,0:T(8,128)(2,1)S(1)} %first.3), channel_id=1, source_target_pairs={{0,32},{32,0},{64,96},{96,64},{128,160},{160,128},{192,224},{224,1... | collective-permute-start | bytes 2752520 | tf_op jit(solution)/shard_map/ppermute | solution.py:30
  79.3 12.6 %collective-permute-start.17 = (bf16[128,896]{1,0:T(8,128)(2,1)}, bf16[128,896]{1,0:T(8,128)(2,1)S(1)}, u32[]{:S(2)}, u32[]{:S(2)}) collective-permute-start(bf16[128,896]{1,0:T(8,128)(2,1)} %get-tuple-element.62), channel_id=1, source_target_pairs={{0,192},{32,224},{64,0},{96,32},{128,64},{160,96},{192,128},{224,1... | collective-permute-start | bytes 688136 | tf_op jit(solution)/shard_map/ppermute | solution.py:26
  81.5 10.4 %collective-permute-start.16 = (bf16[128,896]{1,0:T(8,128)(2,1)}, bf16[128,896]{1,0:T(8,128)(2,1)S(1)}, u32[]{:S(2)}, u32[]{:S(2)}) collective-permute-start(bf16[128,896]{1,0:T(8,128)(2,1)} %get-tuple-element.63), channel_id=1, source_target_pairs={{0,128},{32,160},{64,192},{96,224},{128,0},{160,32},{192,64},{224,... | collective-permute-start | bytes 688136 | tf_op jit(solution)/shard_map/ppermute | solution.py:26
  82.2 13.3 %collective-permute-start.15 = (bf16[128,896]{1,0:T(8,128)(2,1)S(1)}, bf16[128,896]{1,0:T(8,128)(2,1)S(1)}, u32[]{:S(2)}, u32[]{:S(2)}) collective-permute-start(bf16[128,896]{1,0:T(8,128)(2,1)S(1)} %get-tuple-element.64), channel_id=1, source_target_pairs={{0,64},{32,96},{64,128},{96,160},{128,192},{160,224},{192,0},{224,... | collective-permute-start | bytes 688136 | tf_op jit(solution)/shard_map/ppermute | solution.py:26
  84.4 28.2 %copy-start.3 = (bf16[1024,896]{1,0:T(8,128)(2,1)S(1)}, bf16[1024,896]{1,0:T(8,128)(2,1)}, u32[]{:S(2)}) copy-start(bf16[1024,896]{1,0:T(8,128)(2,1)} %uw.1) | copy-start | bytes 5505028
  91.5 21.1 %copy-start.2 = (bf16[1024,896]{1,0:T(8,128)(2,1)S(1)}, bf16[1024,896]{1,0:T(8,128)(2,1)}, u32[]{:S(2)}) copy-start(bf16[1024,896]{1,0:T(8,128)(2,1)} %gw.1) | copy-start | bytes 5505028
  95.6 13.7 %collective-permute-start.21 = (bf16[128,896]{1,0:T(8,128)(2,1)S(1)}, bf16[128,896]{1,0:T(8,128)(2,1)S(1)}, u32[]{:S(2)}, u32[]{:S(2)}) collective-permute-start(bf16[128,896]{1,0:T(8,128)(2,1)S(1)} %total.2), channel_id=1, source_target_pairs={{0,64},{32,96},{64,128},{96,160},{128,192},{160,224},{192,0},{224,... | collective-permute-start | bytes 688136 | tf_op jit(solution)/shard_map/ppermute | solution.py:26
  95.7 13.6 %collective-permute-start.20 = (bf16[128,896]{1,0:T(8,128)(2,1)S(1)}, bf16[128,896]{1,0:T(8,128)(2,1)S(1)}, u32[]{:S(2)}, u32[]{:S(2)}) collective-permute-start(bf16[128,896]{1,0:T(8,128)(2,1)S(1)} %total.2), channel_id=1, source_target_pairs={{0,128},{32,160},{64,192},{96,224},{128,0},{160,32},{192,64},{224,... | collective-permute-start | bytes 688136 | tf_op jit(solution)/shard_map/ppermute | solution.py:26
  97.7 12.2 %collective-permute-start.19 = (bf16[128,896]{1,0:T(8,128)(2,1)S(1)}, bf16[128,896]{1,0:T(8,128)(2,1)S(1)}, u32[]{:S(2)}, u32[]{:S(2)}) collective-permute-start(bf16[128,896]{1,0:T(8,128)(2,1)S(1)} %total.2), channel_id=1, source_target_pairs={{0,192},{32,224},{64,0},{96,32},{128,64},{160,96},{192,128},{224,1... | collective-permute-start | bytes 688136 | tf_op jit(solution)/shard_map/ppermute | solution.py:26
  110.0 2.6 %collective-permute-start.22 = (bf16[512,896]{1,0:T(8,128)(2,1)S(1)}, bf16[512,896]{1,0:T(8,128)(2,1)S(1)}, u32[]{:S(2)}, u32[]{:S(2)}) collective-permute-start(bf16[512,896]{1,0:T(8,128)(2,1)S(1)} %pad_maximum_fusion.1.m0.m1), channel_id=1, source_target_pairs={{0,32},{32,0},{64,96},{96,64},{128,160},{160,128},{192,224},{224,1... | collective-permute-start | bytes 2752520 | tf_op jit(solution)/shard_map/ppermute | solution.py:30
  118.4 5.6 %collective-permute-start.24 = (bf16[64,1024]{1,0:T(8,128)(2,1)S(1)}, bf16[64,1024]{1,0:T(8,128)(2,1)S(1)}, u32[]{:S(2)}, u32[]{:S(2)}) collective-permute-start(bf16[64,1024]{1,0:T(8,128)(2,1)S(1)} %get-tuple-element.60), channel_id=1, source_target_pairs={{0,28},{1,29},{2,30},{3,31},{4,0},{5,1},{6,2},{7,3},{8,4},{9,5},{1... | collective-permute-start | bytes 393224 | tf_op jit(solution)/shard_map/ppermute | solution.py:16
  118.5 6.8 %collective-permute-start.23 = (bf16[64,1024]{1,0:T(8,128)(2,1)S(1)}, bf16[64,1024]{1,0:T(8,128)(2,1)S(1)}, u32[]{:S(2)}, u32[]{:S(2)}) collective-permute-start(bf16[64,1024]{1,0:T(8,128)(2,1)S(1)} %get-tuple-element.61), channel_id=1, source_target_pairs={{0,4},{1,5},{2,6},{3,7},{4,8},{5,9},{6,10},{7,11},{8,12},{9,13},{1... | collective-permute-start | bytes 393224 | tf_op jit(solution)/shard_map/ppermute | solution.py:16
  125.3 3.6 %copy-start.1 = (bf16[1024,1024]{1,0:T(8,128)(2,1)S(1)}, bf16[1024,1024]{1,0:T(8,128)(2,1)}, u32[]{:S(2)}) copy-start(bf16[1024,1024]{1,0:T(8,128)(2,1)} %all-gather.2.cloned.1.call-done.x_in) | copy-start | bytes 6291460
  125.4 9.0 %collective-permute-start.25 = (bf16[128,1024]{1,0:T(8,128)(2,1)S(1)}, bf16[128,1024]{1,0:T(8,128)(2,1)S(1)}, u32[]{:S(2)}, u32[]{:S(2)}) collective-permute-start(bf16[128,1024]{1,0:T(8,128)(2,1)S(1)} %get-tuple-element.39), channel_id=1, source_target_pairs={{0,4},{1,5},{2,6},{3,7},{4,8},{5,9},{6,10},{7,11},{8,12},{9,13},{1... | collective-permute-start | bytes 786440 | tf_op jit(solution)/shard_map/ppermute | solution.py:16
  126.1 8.3 %collective-permute-start.26 = (bf16[128,1024]{1,0:T(8,128)(2,1)S(1)}, bf16[128,1024]{1,0:T(8,128)(2,1)S(1)}, u32[]{:S(2)}, u32[]{:S(2)}) collective-permute-start(bf16[128,1024]{1,0:T(8,128)(2,1)S(1)} %get-tuple-element.40), channel_id=1, source_target_pairs={{0,28},{1,29},{2,30},{3,31},{4,0},{5,1},{6,2},{7,3},{8,4},{9,5},{1... | collective-permute-start | bytes 786440 | tf_op jit(solution)/shard_map/ppermute | solution.py:16
  134.5 7.9 %collective-permute-start.27 = (bf16[128,1024]{1,0:T(8,128)(2,1)S(1)}, bf16[128,1024]{1,0:T(8,128)(2,1)S(1)}, u32[]{:S(2)}, u32[]{:S(2)}) collective-permute-start(bf16[128,1024]{1,0:T(8,128)(2,1)S(1)} %get-tuple-element.42), channel_id=1, source_target_pairs={{0,4},{1,5},{2,6},{3,7},{4,8},{5,9},{6,10},{7,11},{8,12},{9,13},{1... | collective-permute-start | bytes 786440 | tf_op jit(solution)/shard_map/ppermute | solution.py:16
  134.6 7.8 %collective-permute-start.28 = (bf16[128,1024]{1,0:T(8,128)(2,1)S(1)}, bf16[128,1024]{1,0:T(8,128)(2,1)S(1)}, u32[]{:S(2)}, u32[]{:S(2)}) collective-permute-start(bf16[128,1024]{1,0:T(8,128)(2,1)S(1)} %get-tuple-element.43), channel_id=1, source_target_pairs={{0,28},{1,29},{2,30},{3,31},{4,0},{5,1},{6,2},{7,3},{8,4},{9,5},{1... | collective-permute-start | bytes 786440 | tf_op jit(solution)/shard_map/ppermute | solution.py:16
  142.5 7.7 %collective-permute-start.29 = (bf16[128,1024]{1,0:T(8,128)(2,1)S(1)}, bf16[128,1024]{1,0:T(8,128)(2,1)S(1)}, u32[]{:S(2)}, u32[]{:S(2)}) collective-permute-start(bf16[128,1024]{1,0:T(8,128)(2,1)S(1)} %get-tuple-element.47), channel_id=1, source_target_pairs={{0,4},{1,5},{2,6},{3,7},{4,8},{5,9},{6,10},{7,11},{8,12},{9,13},{1... | collective-permute-start | bytes 786440 | tf_op jit(solution)/shard_map/ppermute | solution.py:16
  144.8 6.4 %collective-permute-start.30 = (bf16[128,1024]{1,0:T(8,128)(2,1)S(1)}, bf16[128,1024]{1,0:T(8,128)(2,1)S(1)}, u32[]{:S(2)}, u32[]{:S(2)}) collective-permute-start(bf16[128,1024]{1,0:T(8,128)(2,1)S(1)} %get-tuple-element.48), channel_id=1, source_target_pairs={{0,28},{1,29},{2,30},{3,31},{4,0},{5,1},{6,2},{7,3},{8,4},{9,5},{1... | collective-permute-start | bytes 786440 | tf_op jit(solution)/shard_map/ppermute | solution.py:16
  151.2 4.3 %collective-permute-start.31 = (bf16[32,1024]{1,0:T(8,128)(2,1)S(1)}, bf16[32,1024]{1,0:T(8,128)(2,1)S(1)}, u32[]{:S(2)}, u32[]{:S(2)}) collective-permute-start(bf16[32,1024]{1,0:T(8,128)(2,1)S(1)} %get-tuple-element.52), channel_id=1, source_target_pairs={{0,1},{1,2},{2,3},{3,0},{4,5},{5,6},{6,7},{7,4},{8,9},{9,10},{10,1... | collective-permute-start | bytes 196616 | tf_op jit(solution)/shard_map/ppermute | solution.py:21
  152.1 5.8 %collective-permute-start.32 = (bf16[32,1024]{1,0:T(8,128)(2,1)S(1)}, bf16[32,1024]{1,0:T(8,128)(2,1)S(1)}, u32[]{:S(2)}, u32[]{:S(2)}) collective-permute-start(bf16[32,1024]{1,0:T(8,128)(2,1)S(1)} %get-tuple-element.53), channel_id=1, source_target_pairs={{0,2},{1,3},{2,0},{3,1},{4,6},{5,7},{6,4},{7,5},{8,10},{9,11},{10,... | collective-permute-start | bytes 196616 | tf_op jit(solution)/shard_map/ppermute | solution.py:21
  154.2 5.5 %collective-permute-start.33 = (bf16[32,1024]{1,0:T(8,128)(2,1)S(1)}, bf16[32,1024]{1,0:T(8,128)(2,1)S(1)}, u32[]{:S(2)}, u32[]{:S(2)}) collective-permute-start(bf16[32,1024]{1,0:T(8,128)(2,1)S(1)} %get-tuple-element.54), channel_id=1, source_target_pairs={{0,3},{1,0},{2,1},{3,2},{4,7},{5,4},{6,5},{7,6},{8,11},{9,8},{10,9... | collective-permute-start | bytes 196616 | tf_op jit(solution)/shard_map/ppermute | solution.py:21
Sparse Core Ops, SparseCore 0:
  20.1 48.2 all-gather.1

commit v2 on v0

v2 whole, which is shorter than its diff:
```python
import functools

import jax
import jax.numpy as jnp
from jax import lax
from jax.experimental import pallas as pl
from jax.experimental.pallas import tpu as pltpu
from jax.sharding import PartitionSpec as P

NX, NC, NZ, NY = 4, 2, 8, 4
TOK = 32
BLK = NY * TOK
HALF = BLK // NC
SUB = HALF // NX
ORDER = (0, 1, 2, 3, 5, 6, 7, 4)
BF, F32 = jnp.bfloat16, jnp.float32
HBM = pl.BlockSpec(memory_space=pltpu.HBM)
VMEM = pl.BlockSpec(memory_space=pltpu.VMEM)
SMEM = pl.BlockSpec(memory_space=pltpu.SMEM)


def stay(v):
    return pltpu.with_memory_space_constraint(v, pltpu.HBM)


def params(mib):
    return pltpu.CompilerParams(vmem_limit_bytes=mib << 20)


def cost(flops, size):
    return pl.CostEstimate(flops=flops, bytes_accessed=size, transcendentals=0)


def from_z(v, k):
    perm = [(z * NY + y, (z - k) % NZ * NY + y) for z in range(NZ) for y in range(NY)]
    return lax.ppermute(v, "col", perm)


def from_y(v, k):
    perm = [(z * NY + y, z * NY + (y - k) % NY) for z in range(NZ) for y in range(NY)]
    return lax.ppermute(v, "col", perm)


def from_x(v, k):
    perm = [(x * NC + c, (x - k) % NX * NC + c) for x in range(NX) for c in range(NC)]
    return lax.ppermute(v, "row", perm)


def from_core(v):
    return lax.ppermute(v, "row", [(r, r ^ 1) for r in range(NX * NC)])


def weigh_kernel(ids_in, flags_in, scale_in, cot_in, out, ids, flags, scale, cot, sems):
    copies = [
        pltpu.make_async_copy(src, dst, sems.at[i])
        for i, (src, dst) in enumerate(
            ((ids_in, ids), (flags_in, flags), (scale_in, scale), (cot_in, cot))
        )
    ]
    for copy in copies:
        copy.start()
    for copy in copies:
        copy.wait()
    row = lax.broadcasted_iota(jnp.int32, cot.shape, 0)
    weight = jnp.zeros(cot.shape, F32)
    for r in range(TOK):
        w = (2 * flags[r] - 1).astype(F32) * scale[ids[r]]
        weight = jnp.where(row == r, w, weight)
    out[...] = (cot[...].astype(F32) * weight).astype(BF)


def weigh(cotangent, pair_ids, flags, pair_scale):
    return pl.pallas_call(
        weigh_kernel,
        in_specs=[HBM] * 4,
        out_specs=VMEM,
        out_shape=jax.ShapeDtypeStruct(cotangent.shape, BF),
        scratch_shapes=[
            pltpu.SMEM(pair_ids.shape, jnp.int32),
            pltpu.SMEM(flags.shape, jnp.int32),
            pltpu.SMEM(pair_scale.shape, F32),
            pltpu.VMEM(cotangent.shape, BF),
            pltpu.SemaphoreType.DMA((4,)),
        ],
        compiler_params=params(4),
        cost_estimate=cost(cotangent.size, 8 * cotangent.size),
        name="weigh",
    )(*map(stay, (pair_ids, flags, pair_scale, cotangent)))


def lead_kernel(r0, r1, r2, r3, g, u, rows, pre, sems):
    copies = [pltpu.make_async_copy(v, pre.at[i], sems.at[i]) for i, v in enumerate((g, u))]
    for copy in copies:
        copy.start()
    for k, r in enumerate((r0, r1, r2, r3)):
        rows[k * TOK:(k + 1) * TOK, :] = r[...]
    for copy in copies:
        copy.wait()


def lead(parts, gate_pre, up_pre):
    return pl.pallas_call(
        lead_kernel,
        in_specs=[VMEM] * 4 + [HBM] * 2,
        out_specs=[VMEM, HBM],
        out_shape=[
            jax.ShapeDtypeStruct((BLK, parts[0].shape[1]), BF),
            pltpu.HBM((2,) + gate_pre.shape, BF),
        ],
        scratch_shapes=[pltpu.SemaphoreType.DMA((2,))],
        compiler_params=params(4),
        cost_estimate=cost(0, 8 * (parts[0].size * 2 + gate_pre.size)),
        name="lead",
    )(*parts, stay(gate_pre), stay(up_pre))


def halves_kernel(u, d, r1, r2, r3, low, high):
    low[...] = u[:HALF, :]
    high[...] = d[HALF:, :]


def halves(u, d, after):
    half = jax.ShapeDtypeStruct((HALF, u.shape[1]), BF)
    return pl.pallas_call(
        halves_kernel,
        in_specs=[VMEM] * 2 + [HBM] * 3,
        out_specs=[VMEM] * 2,
        out_shape=[half, half],
        compiler_params=params(4),
        cost_estimate=cost(0, 4 * u.size),
        name="halves",
    )(u, d, *after)


def nt(a, b):
    return lax.dot_general(a, b, (((1,), (1,)), ((), ())), preferred_element_type=F32)


def first_kernel(flip, s, dy, low, high, w, out):
    n = dy.shape[0]
    far = jnp.where(lax.rem(s[1] + flip, NC) == 0, low[...], high[...])
    rows = jnp.concatenate([dy[j] for j in range(n)] + [far], axis=0)
    acc = nt(rows, w[...]).astype(out.dtype)
    for xb in range(NX):
        k = lax.rem(xb - s[0] + NX, NX)
        for j in range(n + 1):
            at = j * HALF + xb * SUB
            out[k, j * SUB:(j + 1) * SUB, :] = acc[at:at + SUB, :]


def first(place, dy, low, high, w, flip):
    ff, width = w.shape
    n = dy.shape[0]
    rows = NZ * SUB
    far = pl.BlockSpec((HALF, width), lambda i, s: (0, 0))
    return pl.pallas_call(
        functools.partial(first_kernel, flip),
        grid_spec=pltpu.PrefetchScalarGridSpec(
            num_scalar_prefetch=1,
            grid=(1,),
            in_specs=[
                pl.BlockSpec((n, HALF, width), lambda i, s: (0, lax.rem(s[1] + flip, NC), 0)),
                far,
                far,
                pl.BlockSpec((ff, width), lambda i, s: (0, 0)),
            ],
            out_specs=pl.BlockSpec((NX, rows, ff), lambda i, s: (0, 0, 0)),
        ),
        out_shape=jax.ShapeDtypeStruct((NX, rows, ff), BF if flip else F32),
        compiler_params=params(16),
        cost_estimate=cost(2 * NX * rows * ff * width, 2 * ff * width + 4 * NX * rows * (ff + width)),
        name="first",
    )(place, dy, low, high, w)


def total_kernel(own, r1, r2, r3, *refs):
    refs[-1][...] = (own[...] + r1[...].astype(F32) + r2[...].astype(F32) + r3[...].astype(F32)).astype(BF)


def total_of(own, parts, *after):
    return pl.pallas_call(
        total_kernel,
        in_specs=[VMEM] * 4 + [HBM] * len(after),
        out_specs=VMEM,
        out_shape=jax.ShapeDtypeStruct(own.shape, BF),
        compiler_params=params(4),
        cost_estimate=cost(3 * own.size, 12 * own.size),
        name="total",
    )(own, *parts, *after)


def add_kernel(own, theirs, mine, s1, s2, s3):
    mine[...] = own[0] + theirs[0].astype(F32)
    for k, out in enumerate((s1, s2, s3), 1):
        out[...] = (own[k] + theirs[k].astype(F32)).astype(BF)


def pair_sums(own, theirs):
    shape = own.shape[1:]
    return pl.pallas_call(
        add_kernel,
        in_specs=[VMEM, VMEM],
        out_specs=[VMEM] * 4,
        out_shape=[jax.ShapeDtypeStruct(shape, F32)] + [jax.ShapeDtypeStruct(shape, BF)] * 3,
        compiler_params=params(6),
        cost_estimate=cost(own.size, 9 * own.size),
        name="pair",
    )(own, theirs)


def prep_kernel(s, mine, other, after, hidden_t, a_out, b_out, mark):
    y = s[3]
    same = lax.rem(lax.rem(s[2] + s[4 + pl.program_id(0)], NZ), NC) == s[1]

    def turned(i):
        rows = [pl.ds(pl.multiple_of(lax.rem(y + j, NY) * TOK, TOK), TOK) for j in range(NY)]
        got = [jnp.where(same, mine[0, i, r, :], other[0, i, r, :]) for r in rows]
        return jnp.concatenate(got, axis=0).astype(F32)

    g, u = turned(0), turned(1)
    sig = 1.0 / (1.0 + jnp.exp(-g))
    gs = g * sig
    a_out[...] = gs
    b_out[...] = u * sig * (1.0 + g * (1.0 - sig))
    hidden_t[...] = (gs * u).astype(BF).T
    mark[...] = jnp.zeros(mark.shape, F32)


def prep(place, mine, other, after):
    ff = mine.shape[-1]
    tokens = NZ * BLK
    rows = pl.BlockSpec((BLK, ff), lambda t, s: (t, 0))

    def piece(t, s):
        block = lax.rem(s[2] + s[4 + t], NZ)
        return (lax.rem(lax.div(block, NC) - s[0] + NX, NX), 0, 0, 0)

    spec = pl.BlockSpec((1, 2, BLK, ff), piece)
    return pl.pallas_call(
        prep_kernel,
        grid_spec=pltpu.PrefetchScalarGridSpec(
            num_scalar_prefetch=1,
            grid=(NZ,),
            in_specs=[spec, spec, HBM],
            out_specs=[
                pl.BlockSpec((ff, BLK), lambda t, s: (0, t)),
                rows,
                rows,
                pl.BlockSpec((8, 128), lambda t, s: (0, 0)),
            ],
        ),
        out_shape=[
            jax.ShapeDtypeStruct((ff, tokens), BF),
            jax.ShapeDtypeStruct((tokens, ff), F32),
            jax.ShapeDtypeStruct((tokens, ff), F32),
            jax.ShapeDtypeStruct((8, 128), F32),
        ],
        compiler_params=params(8),
        cost_estimate=cost(30 * tokens * ff, 14 * tokens * ff),
        name="prep",
    )(place, mine, other, after)


def turn_kernel(s, x_in, after, x_out, mark):
    rows = [pl.ds(pl.multiple_of(lax.rem(s[3] + j, NY) * TOK, TOK), TOK) for j in range(NY)]
    x_out[...] = jnp.concatenate([x_in[r, :] for r in rows], axis=0).T
    mark[...] = jnp.zeros(mark.shape, F32)


def turn(place, x_all, after):
    tokens, width = x_all.shape
    return pl.pallas_call(
        turn_kernel,
        grid_spec=pltpu.PrefetchScalarGridSpec(
            num_scalar_prefetch=1,
            grid=(NZ,),
            in_specs=[pl.BlockSpec((BLK, width), lambda t, s: (lax.rem(s[2] + s[4 + t], NZ), 0)), HBM],
            out_specs=[
                pl.BlockSpec((width, BLK), lambda t, s: (0, t)),
                pl.BlockSpec((8, 128), lambda t, s: (0, 0)),
            ],
        ),
        out_shape=[jax.ShapeDtypeStruct((width, tokens), BF), jax.ShapeDtypeStruct((8, 128), F32)],
        compiler_params=params(8),
        cost_estimate=cost(0, 4 * tokens * width),
        name="turn",
    )(place, x_all, after)


def second_kernel(s, mine, other, a, b, gw, uw, dg, du, p):
    for j in range(dg.shape[0] // BLK):
        here = slice(j * SUB, (j + 1) * SUB)
        for half in range(NC):
            for xb in range(NX):
                k = lax.rem(xb - s[0] + NX, NX)
                d = jnp.where(s[1] == half, mine[k, here, :], other[k, here, :]).astype(F32)
                at = j * BLK + half * HALF + xb * SUB
                rows = slice(at, at + SUB)
                du[rows, :] = (d * a[rows, :]).astype(BF)
                dg[rows, :] = (d * b[rows, :]).astype(BF)
    p[...] = (nt(dg[...], gw[...]) + nt(du[...], uw[...])).astype(BF)


def second(place, mine, other, a, b, gate_weight, up_weight):
    tokens, ff = a.shape
    width = gate_weight.shape[0]
    tile = 4 * BLK
    got = pl.BlockSpec((NX, 4 * SUB, ff), lambda t, s: (0, t, 0))
    row = pl.BlockSpec((tile, ff), lambda t, s: (t, 0))
    whole = pl.BlockSpec((width, ff), lambda t, s: (0, 0))
    return pl.pallas_call(
        second_kernel,
        grid_spec=pltpu.PrefetchScalarGridSpec(
            num_scalar_prefetch=1,
            grid=(tokens // tile,),
            in_specs=[got, got, row, row, whole, whole],
            out_specs=[row, row, pl.BlockSpec((tile, width), lambda t, s: (t, 0))],
        ),
        out_shape=[
            pltpu.HBM((tokens, ff), BF),
            pltpu.HBM((tokens, ff), BF),
            jax.ShapeDtypeStruct((tokens, width), BF),
        ],
        compiler_params=params(30),
        cost_estimate=cost(4 * tokens * ff * width, 16 * tokens * ff + 4 * ff * width),
        name="second",
    )(place, mine, other, a, b, gate_weight, up_weight)


def product_kernel(n, a, *refs):
    parts, (after, out, mark) = refs[:n], refs[n:]
    b = jnp.concatenate([v[...] for v in parts], axis=0)
    out[...] = jnp.dot(a[...], b, preferred_element_type=F32).astype(BF)
    mark[...] = jnp.zeros(mark.shape, F32)


def product(a, parts, tile, after):
    m, k = a.shape
    n = parts[0].shape[1]
    return pl.pallas_call(
        functools.partial(product_kernel, len(parts)),
        grid=(m // tile,),
        in_specs=[pl.BlockSpec((tile, k), lambda i: (i, 0))]
        + [pl.BlockSpec(v.shape, lambda i: (0, 0)) for v in parts]
        + [HBM],
        out_specs=[pl.BlockSpec((tile, n), lambda i: (i, 0)), pl.BlockSpec((8, 128), lambda i: (0, 0))],
        out_shape=[jax.ShapeDtypeStruct((m, n), BF), jax.ShapeDtypeStruct((8, 128), F32)],
        compiler_params=params(16),
        cost_estimate=cost(2 * m * k * n, 2 * (m * k + k * n + m * n)),
        name="product",
    )(a, *parts, after)


def near_kernel(bu, bd, up, down, *refs):
    up_out, down_out = refs[-2:]
    up_out[:HALF, :] = (bu[:HALF, :].astype(F32) + up[...].astype(F32)).astype(BF)
    up_out[HALF:, :] = bu[HALF:, :]
    down_out[:HALF, :] = bd[:HALF, :]
    down_out[HALF:, :] = (bd[HALF:, :].astype(F32) + down[...].astype(F32)).astype(BF)


def step_kernel(bu, bd, up, down, *refs):
    up_out, down_out = refs[-2:]
    up_out[...] = (bu[...].astype(F32) + up[...].astype(F32)).astype(BF)
    down_out[...] = (bd[...].astype(F32) + down[...].astype(F32)).astype(BF)


def step(kernel, p, i, j, up, down, *after):
    width = p.shape[1]
    sds = jax.ShapeDtypeStruct((BLK, width), BF)
    whole = pl.BlockSpec(up.shape, lambda t: (0, 0))
    block = pl.BlockSpec((BLK, width), lambda t: (0, 0))
    return pl.pallas_call(
        kernel,
        grid=(1,),
        in_specs=[
            pl.BlockSpec((BLK, width), lambda t: (i, 0)),
            pl.BlockSpec((BLK, width), lambda t: (j, 0)),
            whole,
            whole,
        ]
        + [HBM] * len(after),
        out_specs=[block, block],
        out_shape=[sds, sds],
        compiler_params=params(6),
        cost_estimate=cost(2 * BLK * width, 12 * BLK * width),
        name="step",
    )(p, p, up, down, *after)


def own_kernel(b0, up, down, after, own, s1, s2, s3):
    total = b0[...].astype(F32) + up[...].astype(F32) + down[...].astype(F32)
    own[...] = total[:TOK, :]
    for k, out in enumerate((s1, s2, s3), 1):
        out[...] = total[k * TOK:(k + 1) * TOK, :].astype(BF)


def own_of(p, up, down, after):
    width = p.shape[1]
    block = pl.BlockSpec((BLK, width), lambda t: (0, 0))
    out = pl.BlockSpec((TOK, width), lambda t: (0, 0))
    return pl.pallas_call(
        own_kernel,
        grid=(1,),
        in_specs=[block] * 3 + [HBM],
        out_specs=[out] * 4,
        out_shape=[jax.ShapeDtypeStruct((TOK, width), F32)] + [jax.ShapeDtypeStruct((TOK, width), BF)] * 3,
        compiler_params=params(6),
        cost_estimate=cost(2 * BLK * width, 8 * BLK * width),
        name="own",
    )(p, up, down, after)


def scatter_z_y(p, marks):
    last = p[7 * BLK:]
    up, down = from_z(last[:HALF], -1), from_z(last[HALF:], 1)
    up, down = step(near_kernel, p, 3, 4, up, down, *marks[0])
    for n, i, j in ((1, 2, 5), (2, 1, 6)):
        up, down = step(step_kernel, p, i, j, from_z(up, -1), from_z(down, 1), marks[n])
    own, *sent = own_of(p, from_z(up, -1), from_z(down, 1), marks[3])
    return total_of(own, [from_y(v, -k) for k, v in enumerate(sent, 1)])


def on_device(
    inputs,
    cotangent,
    gate_pre,
    up_pre,
    gate_weight,
    up_weight,
    down_weight,
    pair_ids,
    flags,
    pair_scale,
):
    row, col = lax.axis_index("row"), lax.axis_index("col")
    place = jnp.stack([row // NC, row % NC, col // NY, col % NY] + [jnp.int32(t) for t in ORDER])
    place = place.astype(jnp.int32)
    scaled = weigh(cotangent, pair_ids, flags, pair_scale)
    x_all = lax.all_gather(inputs, "col", axis=0, tiled=True)

    dy0, pre = lead([scaled] + [from_y(scaled, k) for k in range(1, NY)], gate_pre, up_pre)
    up, down = [dy0], [dy0]
    for _ in range(3):
        up.append(from_z(up[-1], 1))
        down.append(from_z(down[-1], -1))
    pre_parts = [from_x(pre, k) for k in range(1, NX)]
    low, high = halves(up[3], down[3], pre_parts)
    low, high = from_z(low, 1), from_z(high, -1)
    dy = jnp.stack(up + [down[3], down[2], down[1]], axis=0)
    pre_mine = jnp.stack([pre] + pre_parts, axis=0)
    pre_other = from_core(pre_mine)

    sent = first(place, dy, low, high, down_weight, 1)
    hidden_t, a, b, ready = prep(place, pre_mine, pre_other, sent)
    own, *parts = pair_sums(first(place, dy, low, high, down_weight, 0), from_core(sent))
    total = total_of(own, [from_x(v, -k) for k, v in enumerate(parts, 1)], ready)
    mine = jnp.stack([total] + [from_x(total, k) for k in range(1, NX)], axis=0)
    d_gate, d_up, part = second(place, mine, from_core(mine), a, b, gate_weight, up_weight)

    flat = dy.reshape(-1, dy.shape[2])
    grad_down, mark_0 = product(hidden_t, [flat, low, high], 448, part[:8, :128])
    x_t, mark_1 = turn(place, x_all, mark_0)
    grad_gate, mark_2 = product(x_t, [d_gate], 512, mark_1)
    grad_up, mark_3 = product(x_t, [d_up], 512, mark_2)
    grad_input = scatter_z_y(part, ((mark_0, x_all[:16, :128]), mark_1, mark_2, mark_3))
    return (grad_input, grad_gate, grad_up, grad_down)


def solution(mesh):
    return jax.shard_map(
        on_device,
        mesh=mesh,
        in_specs=(
            P("col", "row"),
            P("col", "row"),
            P("row", "col"),
            P("row", "col"),
            P("row", "col"),
            P("row", "col"),
            P("col", "row"),
            P("col"),
            P("col"),
            P(),
        ),
        out_specs=(P("col", "row"), P("row", "col"), P("row", "col"), P("col", "row")),
        check_vma=False,
    )
```

time: 535 us -> 164 us (0.31)
  waiting for transfers between devices: 469 us -> 54.5 us
  starting transfers between devices: 0.28 us -> 50.1 us
  Pallas kernels: 0 us -> 42.6 us
  matrix products: 36.2 us -> 0 us
  local copies, waits for them, and re-layouts: 7.61 us -> 0.95 us
    reduce_scatter x2 -> x0, waiting for transfers between devices: 257 us -> none  [the longest x1 219 us: on_device(): lax.psum_scatter(right_transposed(gate_grads, gate_weight) + right_transp...]
    all_gather x5 -> x1, waiting for transfers between devices: 209 us -> 0.01 us  [on_device(): x_all = lax.all_gather(inputs, 'col', axis=0, tiled=True)]
    ppermute x0 -> x34, waiting for transfers between devices: none -> 54.4 us  [the longest x9 23.6 us: from_x(): return lax.ppermute(v, 'row', perm)]
    ppermute x0 -> x34, starting transfers between devices: none -> 50.1 us  [the longest x16 27.6 us: from_z(): return lax.ppermute(v, 'col', perm)]
    pallas_call x0 -> x18, Pallas kernels: none -> 42.6 us  [the longest x1 15 us: lead(): pl.pallas_call(lead_kernel, in_specs=[VMEM] * 4 + [HBM] * 2, out_specs=[V...]
    dot_general x6 -> x0, matrix products: 36.2 us -> none  [the longest x3 19.7 us: right_transposed(): lax.dot_general(left, right, (((1,), (1,)), ((), ())), preferred_element_...]
    unnamed x8 -> x18, local copies, waits for them, and re-layouts: 7.61 us -> 0.14 us
  transfers between devices with their start and end apart: 7 -> 35, of which waited for: 7 -> 22; matrix products, arithmetic and copies ran while one was open for 7% -> 1% of each run, Pallas kernels for 0% -> 16%
where the time goes in v2:
time: 164 us
  waiting for transfers between devices  54.5 us (33%)
  starting transfers between devices  50.1 us (31%)
  Pallas kernels  42.6 us (26%)
  between operations  14.3 us (9%)
    ppermute x16, starting transfers between devices, from_z(): return lax.ppermute(v, 'col', perm)  27.6 us
    ppermute x9, waiting for transfers between devices, from_x(): return lax.ppermute(v, 'row', perm)  23.6 us
    ppermute x16, waiting for transfers between devices, from_z(): return lax.ppermute(v, 'col', perm)  18.5 us
    pallas_call x1, Pallas kernels, lead(): pl.pallas_call(lead_kernel, in_specs=[VMEM] * 4 + [HBM] * 2, out_specs=[V...  15 us
    ppermute x9, starting transfers between devices, from_x(): return lax.ppermute(v, 'row', perm)  14.7 us
    pallas_call x3, Pallas kernels, product(): pl.pallas_call(functools.partial(product_kernel, len(parts)), grid=(m //...  10.1 us
    ppermute x6, waiting for transfers between devices, from_y(): return lax.ppermute(v, 'col', perm)  9.29 us
    ppermute x6, starting transfers between devices, from_y(): return lax.ppermute(v, 'col', perm)  7.57 us
  transfers between devices with their start and end apart: 35, of which 22 were waited for; matrix products, arithmetic and copies ran while one was open for 1% of the time, Pallas kernels for 16%

profile of v2, /device:TPU:24, one launch (start us, length us, event | category | flops | bytes accessed | tf_op | source)
XLA Modules:
  0.0 163.9 jit_solution(3222363433041256086)
XLA Ops:
  7.2 0.9 weigh.1.r0
  8.2 0.8 collective-permute-start
  9.0 2.7 %collective-permute-start.1 = (bf16[32,1024]{1,0:T(8,128)(2,1)S(1)}, bf16[32,1024]{1,0:T(8,128)(2,1)S(1)}, u32[]{:S(2)}, u32[]{:S(2)}) collective-permute-start(bf16[32,1024]{1,0:T(8,128)(2,1)S(1)} %weigh.1.r0), channel_id=1, source_target_pairs={{0,2},{1,3},{2,0},{3,1},{4,6},{5,7},{6,4},{7,5},{8,10},{9,11},{10,... | collective-permute-start | bytes 196616 | tf_op jit(solution)/shard_map/ppermute | solution.py:41
  12.1 1.9 %collective-permute-done.r1 = bf16[32,1024]{1,0:T(8,128)(2,1)S(1)} collective-permute-done((bf16[32,1024]{1,0:T(8,128)(2,1)S(1)}, bf16[32,1024]{1,0:T(8,128)(2,1)S(1)}, u32[]{:S(2)}, u32[]{:S(2)}) %collective-permute-start) | collective-permute-done | bytes 65568 | tf_op jit(solution)/shard_map/ppermute | solution.py:41
  14.7 1.2 collective-permute-done.2.r3
  15.9 15.0 %lead.1 = (bf16[128,1024]{1,0:T(8,128)(2,1)S(1)}, bf16[2,128,896]{2,1,0:T(8,128)(2,1)}) custom-call(bf16[32,1024]{1,0:T(8,128)(2,1)S(1)} %weigh.1.r0, bf16[32,1024]{1,0:T(8,128)(2,1)S(1)} %collective-permute-done.r1, bf16[32,1024]{1,0:T(8,128)(2,1)S(1)} %collective-permute-done.1.r2, bf16[32,1024]{1,0:T(8,128)(2,1)S(1)} %collective-permute-done.2.r3, ...), custom_call_target="tpu_custom_call" | custom-call | bytes 1441792 | tf_op jit(solution)/shard_map/lead/pallas_call | solution.py:102
  30.9 5.3 %collective-permute-start.3 = (bf16[128,1024]{1,0:T(8,128)(2,1)S(1)}, bf16[128,1024]{1,0:T(8,128)(2,1)S(1)}, u32[]{:S(2)}, u32[]{:S(2)}) collective-permute-start(bf16[128,1024]{1,0:T(8,128)(2,1)S(1)} %get-tuple-element.37), channel_id=1, source_target_pairs={{0,28},{1,29},{2,30},{3,31},{4,0},{5,1},{6,2},{7,3},{8,4},{9,5},{1... | collective-permute-start | bytes 786440 | tf_op jit(solution)/shard_map/ppermute | solution.py:36
  36.4 3.1 %collective-permute-start.10 = (bf16[2,128,896]{2,1,0:T(8,128)(2,1)}, bf16[2,128,896]{2,1,0:T(8,128)(2,1)S(1)}, u32[]{:S(2)}, u32[]{:S(2)}) collective-permute-start(bf16[2,128,896]{2,1,0:T(8,128)(2,1)} %get-tuple-element.38), channel_id=1, source_target_pairs={{0,128},{32,160},{64,192},{96,224},{128,0},{160,32},{192,64},{224,... | collective-permute-start | bytes 1376264 | tf_op jit(solution)/shard_map/ppermute | solution.py:46
  40.1 2.6 %collective-permute-start.9 = (bf16[2,128,896]{2,1,0:T(8,128)(2,1)}, bf16[2,128,896]{2,1,0:T(8,128)(2,1)S(1)}, u32[]{:S(2)}, u32[]{:S(2)}) collective-permute-start(bf16[2,128,896]{2,1,0:T(8,128)(2,1)} %get-tuple-element.38), channel_id=1, source_target_pairs={{0,192},{32,224},{64,0},{96,32},{128,64},{160,96},{192,128},{224,1... | collective-permute-start | bytes 1376264 | tf_op jit(solution)/shard_map/ppermute | solution.py:46
  42.7 3.2 %collective-permute-start.4 = (bf16[128,1024]{1,0:T(8,128)(2,1)S(1)}, bf16[128,1024]{1,0:T(8,128)(2,1)S(1)}, u32[]{:S(2)}, u32[]{:S(2)}) collective-permute-start(bf16[128,1024]{1,0:T(8,128)(2,1)S(1)} %collective-permute-done.3), channel_id=1, source_target_pairs={{0,28},{1,29},{2,30},{3,31},{4,0},{5,1},{6,2},{7,3},{8,4},{9,5},{1... | collective-permute-start | bytes 786440 | tf_op jit(solution)/shard_map/ppermute | solution.py:36
  46.0 4.2 %collective-permute-done.4 = bf16[128,1024]{1,0:T(8,128)(2,1)S(1)} collective-permute-done((bf16[128,1024]{1,0:T(8,128)(2,1)S(1)}, bf16[128,1024]{1,0:T(8,128)(2,1)S(1)}, u32[]{:S(2)}, u32[]{:S(2)}) %collective-permute-start.4) | collective-permute-done | bytes 262176 | tf_op jit(solution)/shard_map/ppermute | solution.py:36
  50.2 3.7 %collective-permute-start.5 = (bf16[128,1024]{1,0:T(8,128)(2,1)S(1)}, bf16[128,1024]{1,0:T(8,128)(2,1)S(1)}, u32[]{:S(2)}, u32[]{:S(2)}) collective-permute-start(bf16[128,1024]{1,0:T(8,128)(2,1)S(1)} %collective-permute-done.4), channel_id=1, source_target_pairs={{0,28},{1,29},{2,30},{3,31},{4,0},{5,1},{6,2},{7,3},{8,4},{9,5},{1... | collective-permute-start | bytes 786440 | tf_op jit(solution)/shard_map/ppermute | solution.py:36
  54.3 4.5 %collective-permute-done.11.r3 = bf16[2,128,896]{2,1,0:T(8,128)(2,1)S(1)} collective-permute-done((bf16[2,128,896]{2,1,0:T(8,128)(2,1)}, bf16[2,128,896]{2,1,0:T(8,128)(2,1)S(1)}, u32[]{:S(2)}, u32[]{:S(2)}) %collective-permute-start.11) | collective-permute-done | bytes 458784 | tf_op jit(solution)/shard_map/ppermute | solution.py:46
  59.0 1.3 pad_maximum_fusion.mine
  60.4 1.8 %collective-permute-done.8.d = bf16[128,1024]{1,0:T(8,128)(2,1)S(1)} collective-permute-done((bf16[128,1024]{1,0:T(8,128)(2,1)S(1)}, bf16[128,1024]{1,0:T(8,128)(2,1)S(1)}, u32[]{:S(2)}, u32[]{:S(2)}) %collective-permute-start.8) | collective-permute-done | bytes 262176 | tf_op jit(solution)/shard_map/ppermute | solution.py:36
  62.3 1.2 collective-permute-start.12
  63.5 0.9 collective-permute-start.13
  64.5 3.1 %collective-permute-done.12.low.refs_1_ = bf16[64,1024]{1,0:T(8,128)(2,1)S(1)} collective-permute-done((bf16[64,1024]{1,0:T(8,128)(2,1)S(1)}, bf16[64,1024]{1,0:T(8,128)(2,1)S(1)}, u32[]{:S(2)}, u32[]{:S(2)}) %collective-permute-start.12) | collective-permute-done | bytes 131104 | tf_op jit(solution)/shard_map/ppermute | solution.py:36
  67.6 3.0 %collective-permute-done.13.high.refs_2_ = bf16[64,1024]{1,0:T(8,128)(2,1)S(1)} collective-permute-done((bf16[64,1024]{1,0:T(8,128)(2,1)S(1)}, bf16[64,1024]{1,0:T(8,128)(2,1)S(1)}, u32[]{:S(2)}, u32[]{:S(2)}) %collective-permute-start.13) | collective-permute-done | bytes 131104 | tf_op jit(solution)/shard_map/ppermute | solution.py:36
  70.6 1.8 %first.3.after = bf16[4,128,896]{2,1,0:T(8,128)(2,1)S(1)} custom-call(s32[12]{0:T(128)S(1)} %stack.73.s, bf16[7,128,1024]{2,1,0:T(8,128)(2,1)S(1)} %bitcast_dynamic-update-slice_fusion.dy, bf16[64,1024]{1,0:T(8,128)(2,1)S(1)} %collective-permute-done.12.low.refs_1_, bf16[64,1024]{1,0:T(8,128)(2,1)S(1)} %collective-permute-done.13.high.refs_2_, ...), custom_call_target="tpu_custom_call" | custom-call | flops 939524096 | bytes 5767168 | tf_op jit(solution)/shard_map/first/pallas_call | solution.py:156
  72.6 1.8 %first.2.own = f32[4,128,896]{2,1,0:T(8,128)S(1)} custom-call(s32[12]{0:T(128)S(1)} %stack.73.s, bf16[7,128,1024]{2,1,0:T(8,128)(2,1)S(1)} %bitcast_dynamic-update-slice_fusion.dy, bf16[64,1024]{1,0:T(8,128)(2,1)S(1)} %collective-permute-done.12.low.refs_1_, bf16[64,1024]{1,0:T(8,128)(2,1)S(1)} %collective-permute-done.13.high.refs_2_, ...), custom_call_target="tpu_custom_call" | custom-call | flops 939524096 | bytes 5767168 | tf_op jit(solution)/shard_map/first/pallas_call | solution.py:156
  75.2 1.5 collective-permute-start.15
  76.7 2.6 %collective-permute-start.16 = (bf16[128,896]{1,0:T(8,128)(2,1)S(1)}, bf16[128,896]{1,0:T(8,128)(2,1)S(1)}, u32[]{:S(2)}, u32[]{:S(2)}) collective-permute-start(bf16[128,896]{1,0:T(8,128)(2,1)S(1)} %get-tuple-element.43), channel_id=1, source_target_pairs={{0,128},{32,160},{64,192},{96,224},{128,0},{160,32},{192,64},{224,... | collective-permute-start | bytes 688136 | tf_op jit(solution)/shard_map/ppermute | solution.py:46
  79.3 0.7 collective-permute-start.17
  80.0 3.7 %prep.1 = (bf16[896,1024]{1,0:T(8,128)(2,1)S(1)}, f32[1024,896]{1,0:T(8,128)S(1)}, f32[1024,896]{1,0:T(8,128)S(1)}, f32[8,128]{1,0:T(8,128)S(1)}) custom-call(s32[12]{0:T(128)S(1)} %stack.73.s, bf16[4,2,128,896]{3,2,1,0:T(8,128)(2,1)S(1)} %pad_maximum_fusion.mine, bf16[4,2,128,896]{3,2,1,0:T(8,128)(2,1)S(1)} %collective-permute-done.18.other, ...), custom_call_target="tpu_custom_call" | custom-call | flops 27525120 | bytes 12845056 | tf_op jit(solution)/shard_map/prep/pallas_call | solution.py:239
  84.1 5.7 %collective-permute-done.16.r2 = bf16[128,896]{1,0:T(8,128)(2,1)S(1)} collective-permute-done((bf16[128,896]{1,0:T(8,128)(2,1)S(1)}, bf16[128,896]{1,0:T(8,128)(2,1)S(1)}, u32[]{:S(2)}, u32[]{:S(2)}) %collective-permute-start.16) | collective-permute-done | bytes 229408 | tf_op jit(solution)/shard_map/ppermute | solution.py:46
  90.0 2.5 %collective-permute-start.19 = (bf16[128,896]{1,0:T(8,128)(2,1)S(1)}, bf16[128,896]{1,0:T(8,128)(2,1)S(1)}, u32[]{:S(2)}, u32[]{:S(2)}) collective-permute-start(bf16[128,896]{1,0:T(8,128)(2,1)S(1)} %total.2), channel_id=1, source_target_pairs={{0,192},{32,224},{64,0},{96,32},{128,64},{160,96},{192,128},{224,1... | collective-permute-start | bytes 688136 | tf_op jit(solution)/shard_map/ppermute | solution.py:46
  92.5 0.9 collective-permute-start.20
  93.4 9.1 %collective-permute-done.19 = bf16[128,896]{1,0:T(8,128)(2,1)S(1)} collective-permute-done((bf16[128,896]{1,0:T(8,128)(2,1)S(1)}, bf16[128,896]{1,0:T(8,128)(2,1)S(1)}, u32[]{:S(2)}, u32[]{:S(2)}) %collective-permute-start.19) | collective-permute-done | bytes 229408 | tf_op jit(solution)/shard_map/ppermute | solution.py:46
  102.5 3.7 %collective-permute-done.21 = bf16[128,896]{1,0:T(8,128)(2,1)S(1)} collective-permute-done((bf16[128,896]{1,0:T(8,128)(2,1)S(1)}, bf16[128,896]{1,0:T(8,128)(2,1)S(1)}, u32[]{:S(2)}, u32[]{:S(2)}) %collective-permute-start.21) | collective-permute-done | bytes 229408 | tf_op jit(solution)/shard_map/ppermute | solution.py:46
  106.5 2.5 %collective-permute-done.22.other = bf16[4,128,896]{2,1,0:T(8,128)(2,1)S(1)} collective-permute-done((bf16[4,128,896]{2,1,0:T(8,128)(2,1)S(1)}, bf16[4,128,896]{2,1,0:T(8,128)(2,1)S(1)}, u32[]{:S(2)}, u32[]{:S(2)}) %collective-permute-start.22) | collective-permute-done | bytes 917536 | tf_op jit(solution)/shard_map/ppermute | solution.py:50
  108.9 5.8 %second.1 = (bf16[1024,896]{1,0:T(8,128)(2,1)}, bf16[1024,896]{1,0:T(8,128)(2,1)}, bf16[1024,1024]{1,0:T(8,128)(2,1)S(1)}) custom-call(s32[12]{0:T(128)S(1)} %stack.73.s, bf16[4,128,896]{2,1,0:T(8,128)(2,1)S(1)} %pad_maximum_fusion.1.mine, bf16[4,128,896]{2,1,0:T(8,128)(2,1)S(1)} %collective-permute-done.22.other, f32[1024,896]{1,0:T(8,128)S(1)} %get-tuple-element.46.a, ...), custom_call_target="tpu_custom_call" | custom-call | flops 3758096384 | bytes 18350080 | tf_op jit(solution)/shard_map/second/pallas_call | solution.py:311
  114.9 3.2 %collective-permute-start.24 = (bf16[64,1024]{1,0:T(8,128)(2,1)S(1)}, bf16[64,1024]{1,0:T(8,128)(2,1)S(1)}, u32[]{:S(2)}, u32[]{:S(2)}) collective-permute-start(bf16[64,1024]{1,0:T(8,128)(2,1)S(1)} %get-tuple-element.70), channel_id=1, source_target_pairs={{0,28},{1,29},{2,30},{3,31},{4,0},{5,1},{6,2},{7,3},{8,4},{9,5},{1... | collective-permute-start | bytes 393224 | tf_op jit(solution)/shard_map/ppermute | solution.py:36
  118.1 3.2 %product.3 = (bf16[896,1024]{1,0:T(8,128)(2,1)}, f32[8,128]{1,0:T(8,128)S(1)}) custom-call(bf16[896,1024]{1,0:T(8,128)(2,1)S(1)} %get-tuple-element.49.a, bf16[896,1024]{1,0:T(8,128)(2,1)S(1)} %bitcast.27, bf16[64,1024]{1,0:T(8,128)(2,1)S(1)} %collective-permute-done.12.low.refs_1_, bf16[64,1024]{1,0:T(8,128)(2,1)S(1)} %collective-permute-done.13.high.refs_2_, ...), custom_call_target="tpu_custom_call" | custom-call | flops 1879048192 | bytes 5767168 | tf_op jit(solution)/shard_map/product/pallas_call | solution.py:340
  122.1 3.2 %collective-permute-start.26 = (bf16[128,1024]{1,0:T(8,128)(2,1)S(1)}, bf16[128,1024]{1,0:T(8,128)(2,1)S(1)}, u32[]{:S(2)}, u32[]{:S(2)}) collective-permute-start(bf16[128,1024]{1,0:T(8,128)(2,1)S(1)} %get-tuple-element.52), channel_id=1, source_target_pairs={{0,28},{1,29},{2,30},{3,31},{4,0},{5,1},{6,2},{7,3},{8,4},{9,5},{1... | collective-permute-start | bytes 786440 | tf_op jit(solution)/shard_map/ppermute | solution.py:36
  125.3 2.1 %turn.1 = (bf16[1024,1024]{1,0:T(8,128)(2,1)S(1)}, f32[8,128]{1,0:T(8,128)S(1)}) custom-call(s32[12]{0:T(128)S(1)} %stack.73.s, bf16[1024,1024]{1,0:T(8,128)(2,1)S(1)} %copy-done.1, f32[8,128]{1,0:T(8,128)S(1)} %get-tuple-element.50.refs_0_.after), custom_call_target="tpu_custom_call" | custom-call | bytes 4194304 | tf_op jit(solution)/shard_map/turn/pallas_call | solution.py:272
  127.4 3.6 %collective-permute-done.25.up = bf16[128,1024]{1,0:T(8,128)(2,1)S(1)} collective-permute-done((bf16[128,1024]{1,0:T(8,128)(2,1)S(1)}, bf16[128,1024]{1,0:T(8,128)(2,1)S(1)}, u32[]{:S(2)}, u32[]{:S(2)}) %collective-permute-start.25) | collective-permute-done | bytes 262176 | tf_op jit(solution)/shard_map/ppermute | solution.py:36
  131.3 3.2 %collective-permute-start.28 = (bf16[128,1024]{1,0:T(8,128)(2,1)S(1)}, bf16[128,1024]{1,0:T(8,128)(2,1)S(1)}, u32[]{:S(2)}, u32[]{:S(2)}) collective-permute-start(bf16[128,1024]{1,0:T(8,128)(2,1)S(1)} %get-tuple-element.55), channel_id=1, source_target_pairs={{0,28},{1,29},{2,30},{3,31},{4,0},{5,1},{6,2},{7,3},{8,4},{9,5},{1... | collective-permute-start | bytes 786440 | tf_op jit(solution)/shard_map/ppermute | solution.py:36
  134.5 3.4 %product.4 = (bf16[1024,896]{1,0:T(8,128)(2,1)}, f32[8,128]{1,0:T(8,128)S(1)}) custom-call(bf16[1024,1024]{1,0:T(8,128)(2,1)S(1)} %get-tuple-element.56.a, bf16[1024,896]{1,0:T(8,128)(2,1)S(1)} %copy-done.5, f32[8,128]{1,0:T(8,128)S(1)} %get-tuple-element.53.refs_0_.refs_1_), custom_call_target="tpu_custom_call" | custom-call | flops 1879048192 | bytes 5767168 | tf_op jit(solution)/shard_map/product/pallas_call | solution.py:340
  138.0 1.4 collective-permute-done.27.up
  139.6 3.2 %collective-permute-start.30 = (bf16[128,1024]{1,0:T(8,128)(2,1)S(1)}, bf16[128,1024]{1,0:T(8,128)(2,1)S(1)}, u32[]{:S(2)}, u32[]{:S(2)}) collective-permute-start(bf16[128,1024]{1,0:T(8,128)(2,1)S(1)} %get-tuple-element.60), channel_id=1, source_target_pairs={{0,28},{1,29},{2,30},{3,31},{4,0},{5,1},{6,2},{7,3},{8,4},{9,5},{1... | collective-permute-start | bytes 786440 | tf_op jit(solution)/shard_map/ppermute | solution.py:36
  142.8 3.4 %product.5 = (bf16[1024,896]{1,0:T(8,128)(2,1)}, f32[8,128]{1,0:T(8,128)S(1)}) custom-call(bf16[1024,1024]{1,0:T(8,128)(2,1)S(1)} %get-tuple-element.56.a, bf16[1024,896]{1,0:T(8,128)(2,1)S(1)} %copy-done.4, f32[8,128]{1,0:T(8,128)S(1)} %get-tuple-element.58.refs_0_.refs_1_), custom_call_target="tpu_custom_call" | custom-call | flops 1879048192 | bytes 5767168 | tf_op jit(solution)/shard_map/product/pallas_call | solution.py:340
  146.3 0.9 collective-permute-done.29.up
  147.3 2.4 %collective-permute-start.31 = (bf16[32,1024]{1,0:T(8,128)(2,1)S(1)}, bf16[32,1024]{1,0:T(8,128)(2,1)S(1)}, u32[]{:S(2)}, u32[]{:S(2)}) collective-permute-start(bf16[32,1024]{1,0:T(8,128)(2,1)S(1)} %get-tuple-element.64), channel_id=1, source_target_pairs={{0,1},{1,2},{2,3},{3,0},{4,5},{5,6},{6,7},{7,4},{8,9},{9,10},{10,1... | collective-permute-start | bytes 196616 | tf_op jit(solution)/shard_map/ppermute | solution.py:41
  149.6 1.3 collective-permute-start.32
  150.9 1.2 collective-permute-done.31.r1
  152.1 3.3 %collective-permute-done.32.r2 = bf16[32,1024]{1,0:T(8,128)(2,1)S(1)} collective-permute-done((bf16[32,1024]{1,0:T(8,128)(2,1)S(1)}, bf16[32,1024]{1,0:T(8,128)(2,1)S(1)}, u32[]{:S(2)}, u32[]{:S(2)}) %collective-permute-start.32) | collective-permute-done | bytes 65568 | tf_op jit(solution)/shard_map/ppermute | solution.py:41
  155.4 1.0 collective-permute-done.33.r3
  (66 shorter events, 6.4 us)
Async XLA Ops:
  7.2 114.1 %all-gather.2.cloned.1.call-start = ((), (), s32[]{:S(2)}) async-start(), calls=%async_computation | async-start | bytes 2162688 | tf_op jit(solution)/shard_map/all_gather | solution.py:440
  8.2 5.9 %collective-permute-start = (bf16[32,1024]{1,0:T(8,128)(2,1)S(1)}, bf16[32,1024]{1,0:T(8,128)(2,1)S(1)}, u32[]{:S(2)}, u32[]{:S(2)}) collective-permute-start(bf16[32,1024]{1,0:T(8,128)(2,1)S(1)} %weigh.1.r0), channel_id=1, source_target_pairs={{0,3},{1,0},{2,1},{3,2},{4,7},{5,4},{6,5},{7,6},{8,11},{9,8},{10,9... | collective-permute-start | bytes 196616 | tf_op jit(solution)/shard_map/ppermute | solution.py:41
  9.0 5.8 %collective-permute-start.1 = (bf16[32,1024]{1,0:T(8,128)(2,1)S(1)}, bf16[32,1024]{1,0:T(8,128)(2,1)S(1)}, u32[]{:S(2)}, u32[]{:S(2)}) collective-permute-start(bf16[32,1024]{1,0:T(8,128)(2,1)S(1)} %weigh.1.r0), channel_id=1, source_target_pairs={{0,2},{1,3},{2,0},{3,1},{4,6},{5,7},{6,4},{7,5},{8,10},{9,11},{10,... | collective-permute-start | bytes 196616 | tf_op jit(solution)/shard_map/ppermute | solution.py:41
  11.7 4.3 %collective-permute-start.2 = (bf16[32,1024]{1,0:T(8,128)(2,1)S(1)}, bf16[32,1024]{1,0:T(8,128)(2,1)S(1)}, u32[]{:S(2)}, u32[]{:S(2)}) collective-permute-start(bf16[32,1024]{1,0:T(8,128)(2,1)S(1)} %weigh.1.r0), channel_id=1, source_target_pairs={{0,1},{1,2},{2,3},{3,0},{4,5},{5,6},{6,7},{7,4},{8,9},{9,10},{10,1... | collective-permute-start | bytes 196616 | tf_op jit(solution)/shard_map/ppermute | solution.py:41
  30.9 11.8 %collective-permute-start.3 = (bf16[128,1024]{1,0:T(8,128)(2,1)S(1)}, bf16[128,1024]{1,0:T(8,128)(2,1)S(1)}, u32[]{:S(2)}, u32[]{:S(2)}) collective-permute-start(bf16[128,1024]{1,0:T(8,128)(2,1)S(1)} %get-tuple-element.37), channel_id=1, source_target_pairs={{0,28},{1,29},{2,30},{3,31},{4,0},{5,1},{6,2},{7,3},{8,4},{9,5},{1... | collective-permute-start | bytes 786440 | tf_op jit(solution)/shard_map/ppermute | solution.py:36
  36.2 9.7 %collective-permute-start.6 = (bf16[128,1024]{1,0:T(8,128)(2,1)S(1)}, bf16[128,1024]{1,0:T(8,128)(2,1)S(1)}, u32[]{:S(2)}, u32[]{:S(2)}) collective-permute-start(bf16[128,1024]{1,0:T(8,128)(2,1)S(1)} %get-tuple-element.37), channel_id=1, source_target_pairs={{0,4},{1,5},{2,6},{3,7},{4,8},{5,9},{6,10},{7,11},{8,12},{9,13},{1... | collective-permute-start | bytes 786440 | tf_op jit(solution)/shard_map/ppermute | solution.py:36
  36.4 17.9 %collective-permute-start.10 = (bf16[2,128,896]{2,1,0:T(8,128)(2,1)}, bf16[2,128,896]{2,1,0:T(8,128)(2,1)S(1)}, u32[]{:S(2)}, u32[]{:S(2)}) collective-permute-start(bf16[2,128,896]{2,1,0:T(8,128)(2,1)} %get-tuple-element.38), channel_id=1, source_target_pairs={{0,128},{32,160},{64,192},{96,224},{128,0},{160,32},{192,64},{224,... | collective-permute-start | bytes 1376264 | tf_op jit(solution)/shard_map/ppermute | solution.py:46
  39.5 19.4 %collective-permute-start.11 = (bf16[2,128,896]{2,1,0:T(8,128)(2,1)}, bf16[2,128,896]{2,1,0:T(8,128)(2,1)S(1)}, u32[]{:S(2)}, u32[]{:S(2)}) collective-permute-start(bf16[2,128,896]{2,1,0:T(8,128)(2,1)} %get-tuple-element.38), channel_id=1, source_target_pairs={{0,64},{32,96},{64,128},{96,160},{128,192},{160,224},{192,0},{224,... | collective-permute-start | bytes 1376264 | tf_op jit(solution)/shard_map/ppermute | solution.py:46
  40.1 18.9 %collective-permute-start.9 = (bf16[2,128,896]{2,1,0:T(8,128)(2,1)}, bf16[2,128,896]{2,1,0:T(8,128)(2,1)S(1)}, u32[]{:S(2)}, u32[]{:S(2)}) collective-permute-start(bf16[2,128,896]{2,1,0:T(8,128)(2,1)} %get-tuple-element.38), channel_id=1, source_target_pairs={{0,192},{32,224},{64,0},{96,32},{128,64},{160,96},{192,128},{224,1... | collective-permute-start | bytes 1376264 | tf_op jit(solution)/shard_map/ppermute | solution.py:46
  42.7 7.5 %collective-permute-start.4 = (bf16[128,1024]{1,0:T(8,128)(2,1)S(1)}, bf16[128,1024]{1,0:T(8,128)(2,1)S(1)}, u32[]{:S(2)}, u32[]{:S(2)}) collective-permute-start(bf16[128,1024]{1,0:T(8,128)(2,1)S(1)} %collective-permute-done.3), channel_id=1, source_target_pairs={{0,28},{1,29},{2,30},{3,31},{4,0},{5,1},{6,2},{7,3},{8,4},{9,5},{1... | collective-permute-start | bytes 786440 | tf_op jit(solution)/shard_map/ppermute | solution.py:36
  46.0 8.3 %collective-permute-start.7 = (bf16[128,1024]{1,0:T(8,128)(2,1)S(1)}, bf16[128,1024]{1,0:T(8,128)(2,1)S(1)}, u32[]{:S(2)}, u32[]{:S(2)}) collective-permute-start(bf16[128,1024]{1,0:T(8,128)(2,1)S(1)} %collective-permute-done.6), channel_id=1, source_target_pairs={{0,4},{1,5},{2,6},{3,7},{4,8},{5,9},{6,10},{7,11},{8,12},{9,13},{1... | collective-permute-start | bytes 786440 | tf_op jit(solution)/shard_map/ppermute | solution.py:36
  50.2 10.2 %collective-permute-start.5 = (bf16[128,1024]{1,0:T(8,128)(2,1)S(1)}, bf16[128,1024]{1,0:T(8,128)(2,1)S(1)}, u32[]{:S(2)}, u32[]{:S(2)}) collective-permute-start(bf16[128,1024]{1,0:T(8,128)(2,1)S(1)} %collective-permute-done.4), channel_id=1, source_target_pairs={{0,28},{1,29},{2,30},{3,31},{4,0},{5,1},{6,2},{7,3},{8,4},{9,5},{1... | collective-permute-start | bytes 786440 | tf_op jit(solution)/shard_map/ppermute | solution.py:36
  54.3 7.9 %collective-permute-start.8 = (bf16[128,1024]{1,0:T(8,128)(2,1)S(1)}, bf16[128,1024]{1,0:T(8,128)(2,1)S(1)}, u32[]{:S(2)}, u32[]{:S(2)}) collective-permute-start(bf16[128,1024]{1,0:T(8,128)(2,1)S(1)} %collective-permute-done.7), channel_id=1, source_target_pairs={{0,4},{1,5},{2,6},{3,7},{4,8},{5,9},{6,10},{7,11},{8,12},{9,13},{1... | collective-permute-start | bytes 786440 | tf_op jit(solution)/shard_map/ppermute | solution.py:36
  60.3 19.8 %collective-permute-start.18 = (bf16[4,2,128,896]{3,2,1,0:T(8,128)(2,1)S(1)}, bf16[4,2,128,896]{3,2,1,0:T(8,128)(2,1)S(1)}, u32[]{:S(2)}, u32[]{:S(2)}) collective-permute-start(bf16[4,2,128,896]{3,2,1,0:T(8,128)(2,1)S(1)} %pad_maximum_fusion.mine), channel_id=1, source_target_pairs={{0,32},{32,0},{64,96},{96,64},{128,160},{160,128},{192,224},{224,1... | collective-permute-start | bytes 5505032 | tf_op jit(solution)/shard_map/ppermute | solution.py:50
  60.4 10.2 %copy-start = (bf16[896,1024]{1,0:T(8,128)(2,1)S(1)}, bf16[896,1024]{1,0:T(8,128)(2,1)}, u32[]{:S(2)}) copy-start(bf16[896,1024]{1,0:T(8,128)(2,1)} %w.3) | copy-start | bytes 5505028
  62.3 5.4 %collective-permute-start.12 = (bf16[64,1024]{1,0:T(8,128)(2,1)S(1)}, bf16[64,1024]{1,0:T(8,128)(2,1)S(1)}, u32[]{:S(2)}, u32[]{:S(2)}) collective-permute-start(bf16[64,1024]{1,0:T(8,128)(2,1)S(1)} %get-tuple-element.39), channel_id=1, source_target_pairs={{0,28},{1,29},{2,30},{3,31},{4,0},{5,1},{6,2},{7,3},{8,4},{9,5},{1... | collective-permute-start | bytes 393224 | tf_op jit(solution)/shard_map/ppermute | solution.py:36
  63.5 7.1 %collective-permute-start.13 = (bf16[64,1024]{1,0:T(8,128)(2,1)S(1)}, bf16[64,1024]{1,0:T(8,128)(2,1)S(1)}, u32[]{:S(2)}, u32[]{:S(2)}) collective-permute-start(bf16[64,1024]{1,0:T(8,128)(2,1)S(1)} %get-tuple-element.40), channel_id=1, source_target_pairs={{0,4},{1,5},{2,6},{3,7},{4,8},{5,9},{6,10},{7,11},{8,12},{9,13},{1... | collective-permute-start | bytes 393224 | tf_op jit(solution)/shard_map/ppermute | solution.py:36
  72.5 2.6 %collective-permute-start.14 = (bf16[4,128,896]{2,1,0:T(8,128)(2,1)S(1)}, bf16[4,128,896]{2,1,0:T(8,128)(2,1)S(1)}, u32[]{:S(2)}, u32[]{:S(2)}) collective-permute-start(bf16[4,128,896]{2,1,0:T(8,128)(2,1)S(1)} %first.3.after), channel_id=1, source_target_pairs={{0,32},{32,0},{64,96},{96,64},{128,160},{160,128},{192,224},{224,1... | collective-permute-start | bytes 2752520 | tf_op jit(solution)/shard_map/ppermute | solution.py:50
  75.2 8.9 %collective-permute-start.15 = (bf16[128,896]{1,0:T(8,128)(2,1)S(1)}, bf16[128,896]{1,0:T(8,128)(2,1)S(1)}, u32[]{:S(2)}, u32[]{:S(2)}) collective-permute-start(bf16[128,896]{1,0:T(8,128)(2,1)S(1)} %get-tuple-element.42), channel_id=1, source_target_pairs={{0,64},{32,96},{64,128},{96,160},{128,192},{160,224},{192,0},{224,... | collective-permute-start | bytes 688136 | tf_op jit(solution)/shard_map/ppermute | solution.py:46
  76.7 13.2 %collective-permute-start.16 = (bf16[128,896]{1,0:T(8,128)(2,1)S(1)}, bf16[128,896]{1,0:T(8,128)(2,1)S(1)}, u32[]{:S(2)}, u32[]{:S(2)}) collective-permute-start(bf16[128,896]{1,0:T(8,128)(2,1)S(1)} %get-tuple-element.43), channel_id=1, source_target_pairs={{0,128},{32,160},{64,192},{96,224},{128,0},{160,32},{192,64},{224,... | collective-permute-start | bytes 688136 | tf_op jit(solution)/shard_map/ppermute | solution.py:46
  79.3 10.5 %collective-permute-start.17 = (bf16[128,896]{1,0:T(8,128)(2,1)S(1)}, bf16[128,896]{1,0:T(8,128)(2,1)S(1)}, u32[]{:S(2)}, u32[]{:S(2)}) collective-permute-start(bf16[128,896]{1,0:T(8,128)(2,1)S(1)} %get-tuple-element.44), channel_id=1, source_target_pairs={{0,192},{32,224},{64,0},{96,32},{128,64},{160,96},{192,128},{224,1... | collective-permute-start | bytes 688136 | tf_op jit(solution)/shard_map/ppermute | solution.py:46
  80.0 28.9 %copy-start.3 = (bf16[1024,896]{1,0:T(8,128)(2,1)S(1)}, bf16[1024,896]{1,0:T(8,128)(2,1)}, u32[]{:S(2)}) copy-start(bf16[1024,896]{1,0:T(8,128)(2,1)} %uw.1) | copy-start | bytes 5505028
  83.8 25.2 %copy-start.2 = (bf16[1024,896]{1,0:T(8,128)(2,1)S(1)}, bf16[1024,896]{1,0:T(8,128)(2,1)}, u32[]{:S(2)}) copy-start(bf16[1024,896]{1,0:T(8,128)(2,1)} %gw.1) | copy-start | bytes 5505028
  90.0 12.6 %collective-permute-start.19 = (bf16[128,896]{1,0:T(8,128)(2,1)S(1)}, bf16[128,896]{1,0:T(8,128)(2,1)S(1)}, u32[]{:S(2)}, u32[]{:S(2)}) collective-permute-start(bf16[128,896]{1,0:T(8,128)(2,1)S(1)} %total.2), channel_id=1, source_target_pairs={{0,192},{32,224},{64,0},{96,32},{128,64},{160,96},{192,128},{224,1... | collective-permute-start | bytes 688136 | tf_op jit(solution)/shard_map/ppermute | solution.py:46
  92.5 10.1 %collective-permute-start.20 = (bf16[128,896]{1,0:T(8,128)(2,1)S(1)}, bf16[128,896]{1,0:T(8,128)(2,1)S(1)}, u32[]{:S(2)}, u32[]{:S(2)}) collective-permute-start(bf16[128,896]{1,0:T(8,128)(2,1)S(1)} %total.2), channel_id=1, source_target_pairs={{0,128},{32,160},{64,192},{96,224},{128,0},{160,32},{192,64},{224,... | collective-permute-start | bytes 688136 | tf_op jit(solution)/shard_map/ppermute | solution.py:46
  93.4 12.8 %collective-permute-start.21 = (bf16[128,896]{1,0:T(8,128)(2,1)S(1)}, bf16[128,896]{1,0:T(8,128)(2,1)S(1)}, u32[]{:S(2)}, u32[]{:S(2)}) collective-permute-start(bf16[128,896]{1,0:T(8,128)(2,1)S(1)} %total.2), channel_id=1, source_target_pairs={{0,64},{32,96},{64,128},{96,160},{128,192},{160,224},{192,0},{224,... | collective-permute-start | bytes 688136 | tf_op jit(solution)/shard_map/ppermute | solution.py:46
  106.4 2.6 %collective-permute-start.22 = (bf16[4,128,896]{2,1,0:T(8,128)(2,1)S(1)}, bf16[4,128,896]{2,1,0:T(8,128)(2,1)S(1)}, u32[]{:S(2)}, u32[]{:S(2)}) collective-permute-start(bf16[4,128,896]{2,1,0:T(8,128)(2,1)S(1)} %pad_maximum_fusion.1.mine), channel_id=1, source_target_pairs={{0,32},{32,0},{64,96},{96,64},{128,160},{160,128},{192,224},{224,1... | collective-permute-start | bytes 2752520 | tf_op jit(solution)/shard_map/ppermute | solution.py:50
  114.8 7.2 %collective-permute-start.23 = (bf16[64,1024]{1,0:T(8,128)(2,1)S(1)}, bf16[64,1024]{1,0:T(8,128)(2,1)S(1)}, u32[]{:S(2)}, u32[]{:S(2)}) collective-permute-start(bf16[64,1024]{1,0:T(8,128)(2,1)S(1)} %get-tuple-element.71), channel_id=1, source_target_pairs={{0,4},{1,5},{2,6},{3,7},{4,8},{5,9},{6,10},{7,11},{8,12},{9,13},{1... | collective-permute-start | bytes 393224 | tf_op jit(solution)/shard_map/ppermute | solution.py:36
  114.9 7.1 %collective-permute-start.24 = (bf16[64,1024]{1,0:T(8,128)(2,1)S(1)}, bf16[64,1024]{1,0:T(8,128)(2,1)S(1)}, u32[]{:S(2)}, u32[]{:S(2)}) collective-permute-start(bf16[64,1024]{1,0:T(8,128)(2,1)S(1)} %get-tuple-element.70), channel_id=1, source_target_pairs={{0,28},{1,29},{2,30},{3,31},{4,0},{5,1},{6,2},{7,3},{8,4},{9,5},{1... | collective-permute-start | bytes 393224 | tf_op jit(solution)/shard_map/ppermute | solution.py:36
  121.9 3.4 %copy-start.1 = (bf16[1024,1024]{1,0:T(8,128)(2,1)S(1)}, bf16[1024,1024]{1,0:T(8,128)(2,1)}, u32[]{:S(2)}) copy-start(bf16[1024,1024]{1,0:T(8,128)(2,1)} %all-gather.2.cloned.1.call-done.x_in) | copy-start | bytes 6291460
  122.0 9.1 %collective-permute-start.25 = (bf16[128,1024]{1,0:T(8,128)(2,1)S(1)}, bf16[128,1024]{1,0:T(8,128)(2,1)S(1)}, u32[]{:S(2)}, u32[]{:S(2)}) collective-permute-start(bf16[128,1024]{1,0:T(8,128)(2,1)S(1)} %get-tuple-element.51), channel_id=1, source_target_pairs={{0,4},{1,5},{2,6},{3,7},{4,8},{5,9},{6,10},{7,11},{8,12},{9,13},{1... | collective-permute-start | bytes 786440 | tf_op jit(solution)/shard_map/ppermute | solution.py:36
  122.1 9.0 %collective-permute-start.26 = (bf16[128,1024]{1,0:T(8,128)(2,1)S(1)}, bf16[128,1024]{1,0:T(8,128)(2,1)S(1)}, u32[]{:S(2)}, u32[]{:S(2)}) collective-permute-start(bf16[128,1024]{1,0:T(8,128)(2,1)S(1)} %get-tuple-element.52), channel_id=1, source_target_pairs={{0,28},{1,29},{2,30},{3,31},{4,0},{5,1},{6,2},{7,3},{8,4},{9,5},{1... | collective-permute-start | bytes 786440 | tf_op jit(solution)/shard_map/ppermute | solution.py:36
  131.1 3.4 %copy-start.5 = (bf16[1024,896]{1,0:T(8,128)(2,1)S(1)}, bf16[1024,896]{1,0:T(8,128)(2,1)}, u32[]{:S(2)}) copy-start(bf16[1024,896]{1,0:T(8,128)(2,1)} %get-tuple-element.57.refs_0_) | copy-start | bytes 5505028
  131.2 8.2 %collective-permute-start.27 = (bf16[128,1024]{1,0:T(8,128)(2,1)S(1)}, bf16[128,1024]{1,0:T(8,128)(2,1)S(1)}, u32[]{:S(2)}, u32[]{:S(2)}) collective-permute-start(bf16[128,1024]{1,0:T(8,128)(2,1)S(1)} %get-tuple-element.54), channel_id=1, source_target_pairs={{0,4},{1,5},{2,6},{3,7},{4,8},{5,9},{6,10},{7,11},{8,12},{9,13},{1... | collective-permute-start | bytes 786440 | tf_op jit(solution)/shard_map/ppermute | solution.py:36
  131.3 8.1 %collective-permute-start.28 = (bf16[128,1024]{1,0:T(8,128)(2,1)S(1)}, bf16[128,1024]{1,0:T(8,128)(2,1)S(1)}, u32[]{:S(2)}, u32[]{:S(2)}) collective-permute-start(bf16[128,1024]{1,0:T(8,128)(2,1)S(1)} %get-tuple-element.55), channel_id=1, source_target_pairs={{0,28},{1,29},{2,30},{3,31},{4,0},{5,1},{6,2},{7,3},{8,4},{9,5},{1... | collective-permute-start | bytes 786440 | tf_op jit(solution)/shard_map/ppermute | solution.py:36
  139.4 3.4 %copy-start.4 = (bf16[1024,896]{1,0:T(8,128)(2,1)S(1)}, bf16[1024,896]{1,0:T(8,128)(2,1)}, u32[]{:S(2)}) copy-start(bf16[1024,896]{1,0:T(8,128)(2,1)} %get-tuple-element.61.refs_0_) | copy-start | bytes 5505028
  139.5 7.7 %collective-permute-start.29 = (bf16[128,1024]{1,0:T(8,128)(2,1)S(1)}, bf16[128,1024]{1,0:T(8,128)(2,1)S(1)}, u32[]{:S(2)}, u32[]{:S(2)}) collective-permute-start(bf16[128,1024]{1,0:T(8,128)(2,1)S(1)} %get-tuple-element.59), channel_id=1, source_target_pairs={{0,4},{1,5},{2,6},{3,7},{4,8},{5,9},{6,10},{7,11},{8,12},{9,13},{1... | collective-permute-start | bytes 786440 | tf_op jit(solution)/shard_map/ppermute | solution.py:36
  139.6 7.6 %collective-permute-start.30 = (bf16[128,1024]{1,0:T(8,128)(2,1)S(1)}, bf16[128,1024]{1,0:T(8,128)(2,1)S(1)}, u32[]{:S(2)}, u32[]{:S(2)}) collective-permute-start(bf16[128,1024]{1,0:T(8,128)(2,1)S(1)} %get-tuple-element.60), channel_id=1, source_target_pairs={{0,28},{1,29},{2,30},{3,31},{4,0},{5,1},{6,2},{7,3},{8,4},{9,5},{1... | collective-permute-start | bytes 786440 | tf_op jit(solution)/shard_map/ppermute | solution.py:36
  147.3 4.9 %collective-permute-start.31 = (bf16[32,1024]{1,0:T(8,128)(2,1)S(1)}, bf16[32,1024]{1,0:T(8,128)(2,1)S(1)}, u32[]{:S(2)}, u32[]{:S(2)}) collective-permute-start(bf16[32,1024]{1,0:T(8,128)(2,1)S(1)} %get-tuple-element.64), channel_id=1, source_target_pairs={{0,1},{1,2},{2,3},{3,0},{4,5},{5,6},{6,7},{7,4},{8,9},{9,10},{10,1... | collective-permute-start | bytes 196616 | tf_op jit(solution)/shard_map/ppermute | solution.py:41
  149.6 5.8 %collective-permute-start.32 = (bf16[32,1024]{1,0:T(8,128)(2,1)S(1)}, bf16[32,1024]{1,0:T(8,128)(2,1)S(1)}, u32[]{:S(2)}, u32[]{:S(2)}) collective-permute-start(bf16[32,1024]{1,0:T(8,128)(2,1)S(1)} %get-tuple-element.65), channel_id=1, source_target_pairs={{0,2},{1,3},{2,0},{3,1},{4,6},{5,7},{6,4},{7,5},{8,10},{9,11},{10,... | collective-permute-start | bytes 196616 | tf_op jit(solution)/shard_map/ppermute | solution.py:41
  150.9 5.5 %collective-permute-start.33 = (bf16[32,1024]{1,0:T(8,128)(2,1)S(1)}, bf16[32,1024]{1,0:T(8,128)(2,1)S(1)}, u32[]{:S(2)}, u32[]{:S(2)}) collective-permute-start(bf16[32,1024]{1,0:T(8,128)(2,1)S(1)} %get-tuple-element.66), channel_id=1, source_target_pairs={{0,3},{1,0},{2,1},{3,2},{4,7},{5,4},{6,5},{7,6},{8,11},{9,8},{10,9... | collective-permute-start | bytes 196616 | tf_op jit(solution)/shard_map/ppermute | solution.py:41
Sparse Core Ops, SparseCore 0:
  36.4 76.3 all-gather.1

commit v3 on v2

--- a/solution.py
+++ b/solution.py
@@ -88,33 +88,28 @@
     )(*map(stay, (pair_ids, flags, pair_scale, cotangent)))
 
 
-def lead_kernel(r0, r1, r2, r3, g, u, rows, pre, sems):
+def pack_kernel(g, u, after, pre, sems):
     copies = [pltpu.make_async_copy(v, pre.at[i], sems.at[i]) for i, v in enumerate((g, u))]
     for copy in copies:
         copy.start()
-    for k, r in enumerate((r0, r1, r2, r3)):
-        rows[k * TOK:(k + 1) * TOK, :] = r[...]
     for copy in copies:
         copy.wait()
 
 
-def lead(parts, gate_pre, up_pre):
-    return pl.pallas_call(
-        lead_kernel,
-        in_specs=[VMEM] * 4 + [HBM] * 2,
-        out_specs=[VMEM, HBM],
-        out_shape=[
-            jax.ShapeDtypeStruct((BLK, parts[0].shape[1]), BF),
-            pltpu.HBM((2,) + gate_pre.shape, BF),
-        ],
+def pack(gate_pre, up_pre, after):
+    return pl.pallas_call(
+        pack_kernel,
+        in_specs=[HBM] * 3,
+        out_specs=VMEM,
+        out_shape=jax.ShapeDtypeStruct((2,) + gate_pre.shape, BF),
         scratch_shapes=[pltpu.SemaphoreType.DMA((2,))],
         compiler_params=params(4),
-        cost_estimate=cost(0, 8 * (parts[0].size * 2 + gate_pre.size)),
-        name="lead",
-    )(*parts, stay(gate_pre), stay(up_pre))
-
-
-def halves_kernel(u, d, r1, r2, r3, low, high):
+        cost_estimate=cost(0, 8 * gate_pre.size),
+        name="pack",
+    )(stay(gate_pre), stay(up_pre), after)
+
+
+def halves_kernel(u, d, r1, r2, low, high):
     low[...] = u[:HALF, :]
     high[...] = d[HALF:, :]
 
@@ -123,7 +118,7 @@
     half = jax.ShapeDtypeStruct((HALF, u.shape[1]), BF)
     return pl.pallas_call(
         halves_kernel,
-        in_specs=[VMEM] * 2 + [HBM] * 3,
+        in_specs=[VMEM] * 2 + [HBM] * 2,
         out_specs=[VMEM] * 2,
         out_shape=[half, half],
         compiler_params=params(4),
@@ -187,6 +182,24 @@
         cost_estimate=cost(3 * own.size, 12 * own.size),
         name="total",
     )(own, *parts, *after)
+
+
+def join_kernel(a, b, c, d, after, out):
+    for k, v in enumerate((a, b, c, d)):
+        out[k] = v[...]
+
+
+def join(parts, after):
+    shape = parts[0].shape
+    return pl.pallas_call(
+        join_kernel,
+        in_specs=[VMEM] * 4 + [HBM],
+        out_specs=VMEM,
+        out_shape=jax.ShapeDtypeStruct((NX,) + shape, BF),
+        compiler_params=params(4),
+        cost_estimate=cost(0, 16 * parts[0].size),
+        name="join",
+    )(*parts, after)
 
 
 def add_kernel(own, theirs, mine, s1, s2, s3):
@@ -301,28 +314,31 @@
     p[...] = (nt(dg[...], gw[...]) + nt(du[...], uw[...])).astype(BF)
 
 
-def second(place, mine, other, a, b, gate_weight, up_weight):
-    tokens, ff = a.shape
+def second(place, mine, other, a, b, gate_weight, up_weight, at, n):
+    ff = a.shape[1]
     width = gate_weight.shape[0]
-    tile = 4 * BLK
-    got = pl.BlockSpec((NX, 4 * SUB, ff), lambda t, s: (0, t, 0))
-    row = pl.BlockSpec((tile, ff), lambda t, s: (t, 0))
-    whole = pl.BlockSpec((width, ff), lambda t, s: (0, 0))
+    rows = n * BLK
+
+    def whole(*shape):
+        return pl.BlockSpec(shape, lambda t, s: (0,) * len(shape))
+
+    got = pl.BlockSpec((NX, n * SUB, ff), lambda t, s: (0, at // n, 0))
+    row = pl.BlockSpec((rows, ff), lambda t, s: (at // n, 0))
     return pl.pallas_call(
         second_kernel,
         grid_spec=pltpu.PrefetchScalarGridSpec(
             num_scalar_prefetch=1,
-            grid=(tokens // tile,),
-            in_specs=[got, got, row, row, whole, whole],
-            out_specs=[row, row, pl.BlockSpec((tile, width), lambda t, s: (t, 0))],
+            grid=(1,),
+            in_specs=[got, got, row, row, whole(width, ff), whole(width, ff)],
+            out_specs=[whole(rows, ff), whole(rows, ff), whole(rows, width)],
         ),
         out_shape=[
-            pltpu.HBM((tokens, ff), BF),
-            pltpu.HBM((tokens, ff), BF),
-            jax.ShapeDtypeStruct((tokens, width), BF),
+            pltpu.HBM((rows, ff), BF),
+            pltpu.HBM((rows, ff), BF),
+            jax.ShapeDtypeStruct((rows, width), BF),
         ],
-        compiler_params=params(30),
-        cost_estimate=cost(4 * tokens * ff * width, 16 * tokens * ff + 4 * ff * width),
+        compiler_params=params(32),
+        cost_estimate=cost(4 * rows * ff * width, 16 * rows * ff + 4 * ff * width),
         name="second",
     )(place, mine, other, a, b, gate_weight, up_weight)
 
@@ -411,10 +427,8 @@
     )(p, up, down, after)
 
 
-def scatter_z_y(p, marks):
-    last = p[7 * BLK:]
-    up, down = from_z(last[:HALF], -1), from_z(last[HALF:], 1)
-    up, down = step(near_kernel, p, 3, 4, up, down, *marks[0])
+def scatter_z_y(p, ends, marks):
+    up, down = step(near_kernel, p, 3, 4, *ends, *marks[0])
     for n, i, j in ((1, 2, 5), (2, 1, 6)):
         up, down = step(step_kernel, p, i, j, from_z(up, -1), from_z(down, 1), marks[n])
     own, *sent = own_of(p, from_z(up, -1), from_z(down, 1), marks[3])
@@ -439,31 +453,38 @@
     scaled = weigh(cotangent, pair_ids, flags, pair_scale)
     x_all = lax.all_gather(inputs, "col", axis=0, tiled=True)
 
-    dy0, pre = lead([scaled] + [from_y(scaled, k) for k in range(1, NY)], gate_pre, up_pre)
+    dy0 = jnp.concatenate([scaled] + [from_y(scaled, k) for k in range(1, NY)], axis=0)
+    pre = pack(gate_pre, up_pre, scaled)
     up, down = [dy0], [dy0]
     for _ in range(3):
         up.append(from_z(up[-1], 1))
         down.append(from_z(down[-1], -1))
-    pre_parts = [from_x(pre, k) for k in range(1, NX)]
-    low, high = halves(up[3], down[3], pre_parts)
+    next_pre, last_pre = from_x(pre, 1), from_x(pre, -1)
+    far_pre = from_x(next_pre[0], 1), from_x(last_pre[1], -1)
+    low, high = halves(up[3], down[3], far_pre)
     low, high = from_z(low, 1), from_z(high, -1)
     dy = jnp.stack(up + [down[3], down[2], down[1]], axis=0)
-    pre_mine = jnp.stack([pre] + pre_parts, axis=0)
+    pre_mine = jnp.stack([pre, next_pre, jnp.stack(far_pre, axis=0), last_pre], axis=0)
     pre_other = from_core(pre_mine)
 
     sent = first(place, dy, low, high, down_weight, 1)
     hidden_t, a, b, ready = prep(place, pre_mine, pre_other, sent)
     own, *parts = pair_sums(first(place, dy, low, high, down_weight, 0), from_core(sent))
     total = total_of(own, [from_x(v, -k) for k, v in enumerate(parts, 1)], ready)
-    mine = jnp.stack([total] + [from_x(total, k) for k in range(1, NX)], axis=0)
-    d_gate, d_up, part = second(place, mine, from_core(mine), a, b, gate_weight, up_weight)
-
     flat = dy.reshape(-1, dy.shape[2])
-    grad_down, mark_0 = product(hidden_t, [flat, low, high], 448, part[:8, :128])
-    x_t, mark_1 = turn(place, x_all, mark_0)
-    grad_gate, mark_2 = product(x_t, [d_gate], 512, mark_1)
-    grad_up, mark_3 = product(x_t, [d_up], 512, mark_2)
-    grad_input = scatter_z_y(part, ((mark_0, x_all[:16, :128]), mark_1, mark_2, mark_3))
+    grad_down, mark_0 = product(hidden_t, [flat, low, high], 448, total)
+    mine = join([total] + [from_x(total, k) for k in range(1, NX)], mark_0)
+    args = place, mine, from_core(mine), a, b, gate_weight, up_weight
+    far = second(*args, NZ - 1, 1)
+    last = far[2]
+    ends = from_z(last[:HALF], -1), from_z(last[HALF:], 1)
+    near = second(*args, 0, NZ - 1)
+    d_gate, d_up, part = zip(near, far)
+
+    x_t, mark_1 = turn(place, x_all, near[2])
+    grad_gate, mark_2 = product(x_t, d_gate, 512, mark_1)
+    grad_up, mark_3 = product(x_t, d_up, 512, mark_2)
+    grad_input = scatter_z_y(near[2], ends, ((x_all[:16, :128],), mark_1, mark_2, mark_3))
     return (grad_input, grad_gate, grad_up, grad_down)
 
 

time: 164 us -> 146 us (0.89)
  Pallas kernels: 42.6 us -> 30 us
  starting transfers between devices: 50.1 us -> 47.4 us
  waiting for transfers between devices: 54.5 us -> 52.3 us
    pallas_call x2 -> x3, Pallas kernels: 15 us -> 1.15 us  [the longest x1 1.06 us: pack(): pl.pallas_call(pack_kernel, in_specs=[HBM] * 3, out_specs=VMEM, out_shape...]
    ppermute x16, waiting for transfers between devices: 18.5 us -> 14 us  [from_z(): return lax.ppermute(v, 'col', perm)]
    ppermute x6, starting transfers between devices: 7.57 us -> 5.1 us  [from_y(): return lax.ppermute(v, 'col', perm)]
    pallas_call x1 -> x2, Pallas kernels: 5.8 us -> 7.02 us  [second(): pl.pallas_call(second_kernel, grid_spec=pltpu.PrefetchScalarGridSpec(num_...]
    ppermute x9 -> x10, waiting for transfers between devices: 23.6 us -> 24.3 us  [from_x(): return lax.ppermute(v, 'row', perm)]
    ppermute x9 -> x10, starting transfers between devices: 14.7 us -> 14.3 us  [from_x(): return lax.ppermute(v, 'row', perm)]
  transfers between devices with their start and end apart: 35 -> 36, of which waited for: 22 -> 22; matrix products, arithmetic and copies ran while one was open for 1% -> 1% of each run, Pallas kernels for 16% -> 19%
where the time goes in v3:
time: 146 us; the launch traced here: 145 us
  waiting for transfers between devices  52.3 us (36%)
  starting transfers between devices  47.4 us (32%)
  Pallas kernels  30 us (21%)
  between operations  14.4 us (10%)
    ppermute x16, starting transfers between devices, from_z(): return lax.ppermute(v, 'col', perm)  27.7 us
    ppermute x10, waiting for transfers between devices, from_x(): return lax.ppermute(v, 'row', perm)  24.3 us
    ppermute x10, starting transfers between devices, from_x(): return lax.ppermute(v, 'row', perm)  14.3 us
    ppermute x16, waiting for transfers between devices, from_z(): return lax.ppermute(v, 'col', perm)  14 us
    ppermute x6, waiting for transfers between devices, from_y(): return lax.ppermute(v, 'col', perm)  10.9 us
    pallas_call x3, Pallas kernels, product(): pl.pallas_call(functools.partial(product_kernel, len(parts)), grid=(m //...  10.1 us
    pallas_call x2, Pallas kernels, second(): pl.pallas_call(second_kernel, grid_spec=pltpu.PrefetchScalarGridSpec(num_...  7.02 us
    ppermute x6, starting transfers between devices, from_y(): return lax.ppermute(v, 'col', perm)  5.1 us
  transfers between devices with their start and end apart: 36, of which 22 were waited for; matrix products, arithmetic and copies ran while one was open for 1% of the time, Pallas kernels for 19%

profile of v3, /device:TPU:24, one launch (start us, length us, event | category | flops | bytes accessed | tf_op | source)
XLA Modules:
  0.0 145.4 jit_solution(5869830675725229014)
XLA Ops:
  7.2 0.9 weigh.1.after
  8.2 2.0 %collective-permute-start.2 = (bf16[32,1024]{1,0:T(8,128)(2,1)S(1)}, bf16[32,1024]{1,0:T(8,128)(2,1)S(1)}, u32[]{:S(2)}, u32[]{:S(2)}) collective-permute-start(bf16[32,1024]{1,0:T(8,128)(2,1)S(1)} %weigh.1.after), channel_id=1, source_target_pairs={{0,1},{1,2},{2,3},{3,0},{4,5},{5,6},{6,7},{7,4},{8,9},{9,10},{10,1... | collective-permute-start | bytes 196616 | tf_op jit(solution)/shard_map/ppermute | solution.py:41
  10.2 0.9 collective-permute-start.1
  11.1 1.6 %collective-permute-done.2 = bf16[32,1024]{1,0:T(8,128)(2,1)S(1)} collective-permute-done((bf16[32,1024]{1,0:T(8,128)(2,1)S(1)}, bf16[32,1024]{1,0:T(8,128)(2,1)S(1)}, u32[]{:S(2)}, u32[]{:S(2)}) %collective-permute-start.2) | collective-permute-done | bytes 65568 | tf_op jit(solution)/shard_map/ppermute | solution.py:41
  12.8 3.2 %collective-permute-done.1 = bf16[32,1024]{1,0:T(8,128)(2,1)S(1)} collective-permute-done((bf16[32,1024]{1,0:T(8,128)(2,1)S(1)}, bf16[32,1024]{1,0:T(8,128)(2,1)S(1)}, u32[]{:S(2)}, u32[]{:S(2)}) %collective-permute-start.1) | collective-permute-done | bytes 65568 | tf_op jit(solution)/shard_map/ppermute | solution.py:41
  16.0 0.7 collective-permute-done
  16.7 5.8 %collective-permute-start.3 = (bf16[128,1024]{1,0:T(8,128)(2,1)S(1)}, bf16[128,1024]{1,0:T(8,128)(2,1)S(1)}, u32[]{:S(2)}, u32[]{:S(2)}) collective-permute-start(bf16[128,1024]{1,0:T(8,128)(2,1)S(1)} %pad_maximum_fusion.1), channel_id=1, source_target_pairs={{0,28},{1,29},{2,30},{3,31},{4,0},{5,1},{6,2},{7,3},{8,4},{9,5},{1... | collective-permute-start | bytes 786440 | tf_op jit(solution)/shard_map/ppermute | solution.py:36
  22.5 1.1 pack.1
  23.5 2.8 %collective-permute-start.9 = (bf16[2,128,896]{2,1,0:T(8,128)(2,1)S(1)}, bf16[2,128,896]{2,1,0:T(8,128)(2,1)S(1)}, u32[]{:S(2)}, u32[]{:S(2)}) collective-permute-start(bf16[2,128,896]{2,1,0:T(8,128)(2,1)S(1)} %pack.1), channel_id=1, source_target_pairs={{0,192},{32,224},{64,0},{96,32},{128,64},{160,96},{192,128},{224,1... | collective-permute-start | bytes 1376264 | tf_op jit(solution)/shard_map/ppermute | solution.py:46
  26.6 3.5 %collective-permute-start.4 = (bf16[128,1024]{1,0:T(8,128)(2,1)S(1)}, bf16[128,1024]{1,0:T(8,128)(2,1)S(1)}, u32[]{:S(2)}, u32[]{:S(2)}) collective-permute-start(bf16[128,1024]{1,0:T(8,128)(2,1)S(1)} %collective-permute-done.3), channel_id=1, source_target_pairs={{0,28},{1,29},{2,30},{3,31},{4,0},{5,1},{6,2},{7,3},{8,4},{9,5},{1... | collective-permute-start | bytes 786440 | tf_op jit(solution)/shard_map/ppermute | solution.py:36
  30.2 4.1 %collective-permute-done.9 = bf16[2,128,896]{2,1,0:T(8,128)(2,1)S(1)} collective-permute-done((bf16[2,128,896]{2,1,0:T(8,128)(2,1)S(1)}, bf16[2,128,896]{2,1,0:T(8,128)(2,1)S(1)}, u32[]{:S(2)}, u32[]{:S(2)}) %collective-permute-start.9) | collective-permute-done | bytes 458784 | tf_op jit(solution)/shard_map/ppermute | solution.py:46
  34.3 3.8 %collective-permute-start.10 = (bf16[128,896]{1,0:T(8,128)(2,1)S(1)}, bf16[128,896]{1,0:T(8,128)(2,1)S(1)}, u32[]{:S(2)}, u32[]{:S(2)}) collective-permute-start(bf16[128,896]{1,0:T(8,128)(2,1)S(1)} %slice_bitcast_fusion.1), channel_id=1, source_target_pairs={{0,192},{32,224},{64,0},{96,32},{128,64},{160,96},{192,128},{224,1... | collective-permute-start | bytes 688136 | tf_op jit(solution)/shard_map/ppermute | solution.py:46
  38.2 3.0 %collective-permute-start.5 = (bf16[128,1024]{1,0:T(8,128)(2,1)S(1)}, bf16[128,1024]{1,0:T(8,128)(2,1)S(1)}, u32[]{:S(2)}, u32[]{:S(2)}) collective-permute-start(bf16[128,1024]{1,0:T(8,128)(2,1)S(1)} %collective-permute-done.4), channel_id=1, source_target_pairs={{0,28},{1,29},{2,30},{3,31},{4,0},{5,1},{6,2},{7,3},{8,4},{9,5},{1... | collective-permute-start | bytes 786440 | tf_op jit(solution)/shard_map/ppermute | solution.py:36
  41.6 3.8 %collective-permute-done.12.r2 = bf16[128,896]{1,0:T(8,128)(2,1)S(1)} collective-permute-done((bf16[128,896]{1,0:T(8,128)(2,1)S(1)}, bf16[128,896]{1,0:T(8,128)(2,1)S(1)}, u32[]{:S(2)}, u32[]{:S(2)}) %collective-permute-start.12) | collective-permute-done | bytes 229408 | tf_op jit(solution)/shard_map/ppermute | solution.py:46
  45.9 3.3 %collective-permute-done.8.d = bf16[128,1024]{1,0:T(8,128)(2,1)S(1)} collective-permute-done((bf16[128,1024]{1,0:T(8,128)(2,1)S(1)}, bf16[128,1024]{1,0:T(8,128)(2,1)S(1)}, u32[]{:S(2)}, u32[]{:S(2)}) %collective-permute-start.8) | collective-permute-done | bytes 262176 | tf_op jit(solution)/shard_map/ppermute | solution.py:36
  49.3 2.0 %collective-permute-start.14 = (bf16[64,1024]{1,0:T(8,128)(2,1)S(1)}, bf16[64,1024]{1,0:T(8,128)(2,1)S(1)}, u32[]{:S(2)}, u32[]{:S(2)}) collective-permute-start(bf16[64,1024]{1,0:T(8,128)(2,1)S(1)} %get-tuple-element.39), channel_id=1, source_target_pairs={{0,4},{1,5},{2,6},{3,7},{4,8},{5,9},{6,10},{7,11},{8,12},{9,13},{1... | collective-permute-start | bytes 393224 | tf_op jit(solution)/shard_map/ppermute | solution.py:36
  51.4 3.0 %collective-permute-done.13.low.refs_1_ = bf16[64,1024]{1,0:T(8,128)(2,1)S(1)} collective-permute-done((bf16[64,1024]{1,0:T(8,128)(2,1)S(1)}, bf16[64,1024]{1,0:T(8,128)(2,1)S(1)}, u32[]{:S(2)}, u32[]{:S(2)}) %collective-permute-start.13) | collective-permute-done | bytes 131104 | tf_op jit(solution)/shard_map/ppermute | solution.py:36
  54.4 1.7 %collective-permute-done.14.high.refs_2_ = bf16[64,1024]{1,0:T(8,128)(2,1)S(1)} collective-permute-done((bf16[64,1024]{1,0:T(8,128)(2,1)S(1)}, bf16[64,1024]{1,0:T(8,128)(2,1)S(1)}, u32[]{:S(2)}, u32[]{:S(2)}) %collective-permute-start.14) | collective-permute-done | bytes 131104 | tf_op jit(solution)/shard_map/ppermute | solution.py:36
  56.1 1.8 %first.3.after = bf16[4,128,896]{2,1,0:T(8,128)(2,1)S(1)} custom-call(s32[12]{0:T(128)S(1)} %stack.67.s, bf16[7,128,1024]{2,1,0:T(8,128)(2,1)S(1)} %bitcast_dynamic-update-slice_fusion.dy, bf16[64,1024]{1,0:T(8,128)(2,1)S(1)} %collective-permute-done.13.low.refs_1_, bf16[64,1024]{1,0:T(8,128)(2,1)S(1)} %collective-permute-done.14.high.refs_2_, ...), custom_call_target="tpu_custom_call" | custom-call | flops 939524096 | bytes 5767168 | tf_op jit(solution)/shard_map/first/pallas_call | solution.py:151
  58.0 1.8 %first.2.own = f32[4,128,896]{2,1,0:T(8,128)S(1)} custom-call(s32[12]{0:T(128)S(1)} %stack.67.s, bf16[7,128,1024]{2,1,0:T(8,128)(2,1)S(1)} %bitcast_dynamic-update-slice_fusion.dy, bf16[64,1024]{1,0:T(8,128)(2,1)S(1)} %collective-permute-done.13.low.refs_1_, bf16[64,1024]{1,0:T(8,128)(2,1)S(1)} %collective-permute-done.14.high.refs_2_, ...), custom_call_target="tpu_custom_call" | custom-call | flops 939524096 | bytes 5767168 | tf_op jit(solution)/shard_map/first/pallas_call | solution.py:151
  60.7 4.1 %collective-permute-start.17 = (bf16[128,896]{1,0:T(8,128)(2,1)S(1)}, bf16[128,896]{1,0:T(8,128)(2,1)S(1)}, u32[]{:S(2)}, u32[]{:S(2)}) collective-permute-start(bf16[128,896]{1,0:T(8,128)(2,1)S(1)} %get-tuple-element.42), channel_id=1, source_target_pairs={{0,128},{32,160},{64,192},{96,224},{128,0},{160,32},{192,64},{224,... | collective-permute-start | bytes 688136 | tf_op jit(solution)/shard_map/ppermute | solution.py:46
  64.8 3.7 %prep.1 = (bf16[896,1024]{1,0:T(8,128)(2,1)S(1)}, f32[1024,896]{1,0:T(8,128)S(1)}, f32[1024,896]{1,0:T(8,128)S(1)}, f32[8,128]{1,0:T(8,128)S(1)}) custom-call(s32[12]{0:T(128)S(1)} %stack.67.s, bf16[4,2,128,896]{3,2,1,0:T(8,128)(2,1)S(1)} %pad_maximum_fusion.mine, bf16[4,2,128,896]{3,2,1,0:T(8,128)(2,1)S(1)} %collective-permute-done.19.other, ...), custom_call_target="tpu_custom_call" | custom-call | flops 27525120 | bytes 12845056 | tf_op jit(solution)/shard_map/prep/pallas_call | solution.py:252
  68.5 1.0 collective-permute-done.16.r1
  69.6 5.8 %collective-permute-done.17.r2 = bf16[128,896]{1,0:T(8,128)(2,1)S(1)} collective-permute-done((bf16[128,896]{1,0:T(8,128)(2,1)S(1)}, bf16[128,896]{1,0:T(8,128)(2,1)S(1)}, u32[]{:S(2)}, u32[]{:S(2)}) %collective-permute-start.17) | collective-permute-done | bytes 229408 | tf_op jit(solution)/shard_map/ppermute | solution.py:46
  75.5 2.5 %collective-permute-start.20 = (bf16[128,896]{1,0:T(8,128)(2,1)S(1)}, bf16[128,896]{1,0:T(8,128)(2,1)S(1)}, u32[]{:S(2)}, u32[]{:S(2)}) collective-permute-start(bf16[128,896]{1,0:T(8,128)(2,1)S(1)} %total.2.refs_3_.a), channel_id=1, source_target_pairs={{0,192},{32,224},{64,0},{96,32},{128,64},{160,96},{192,128},{224,1... | collective-permute-start | bytes 688136 | tf_op jit(solution)/shard_map/ppermute | solution.py:46
  78.0 0.9 collective-permute-start.22
  78.9 3.2 %product.3 = (bf16[896,1024]{1,0:T(8,128)(2,1)}, f32[8,128]{1,0:T(8,128)S(1)}) custom-call(bf16[896,1024]{1,0:T(8,128)(2,1)S(1)} %get-tuple-element.45.a, bf16[896,1024]{1,0:T(8,128)(2,1)S(1)} %bitcast.30, bf16[64,1024]{1,0:T(8,128)(2,1)S(1)} %collective-permute-done.13.low.refs_1_, bf16[64,1024]{1,0:T(8,128)(2,1)S(1)} %collective-permute-done.14.high.refs_2_, ...), custom_call_target="tpu_custom_call" | custom-call | flops 1879048192 | bytes 5767168 | tf_op jit(solution)/shard_map/product/pallas_call | solution.py:356
  82.1 5.8 %collective-permute-done.20.b = bf16[128,896]{1,0:T(8,128)(2,1)S(1)} collective-permute-done((bf16[128,896]{1,0:T(8,128)(2,1)S(1)}, bf16[128,896]{1,0:T(8,128)(2,1)S(1)}, u32[]{:S(2)}, u32[]{:S(2)}) %collective-permute-start.20) | collective-permute-done | bytes 229408 | tf_op jit(solution)/shard_map/ppermute | solution.py:46
  87.9 3.4 %collective-permute-done.22.d = bf16[128,896]{1,0:T(8,128)(2,1)S(1)} collective-permute-done((bf16[128,896]{1,0:T(8,128)(2,1)S(1)}, bf16[128,896]{1,0:T(8,128)(2,1)S(1)}, u32[]{:S(2)}, u32[]{:S(2)}) %collective-permute-start.22) | collective-permute-done | bytes 229408 | tf_op jit(solution)/shard_map/ppermute | solution.py:46
  91.5 2.5 %collective-permute-done.23.other = bf16[4,128,896]{2,1,0:T(8,128)(2,1)S(1)} collective-permute-done((bf16[4,128,896]{2,1,0:T(8,128)(2,1)S(1)}, bf16[4,128,896]{2,1,0:T(8,128)(2,1)S(1)}, u32[]{:S(2)}, u32[]{:S(2)}) %collective-permute-start.23) | collective-permute-done | bytes 917536 | tf_op jit(solution)/shard_map/ppermute | solution.py:50
  93.9 2.4 %second.3 = (bf16[128,896]{1,0:T(8,128)(2,1)}, bf16[128,896]{1,0:T(8,128)(2,1)}, bf16[128,1024]{1,0:T(8,128)(2,1)S(1)}) custom-call(s32[12]{0:T(128)S(1)} %stack.67.s, bf16[4,128,896]{2,1,0:T(8,128)(2,1)S(1)} %join.1.mine, bf16[4,128,896]{2,1,0:T(8,128)(2,1)S(1)} %collective-permute-done.23.other, f32[1024,896]{1,0:T(8,128)S(1)} %get-tuple-element.47.a, ...), custom_call_target="tpu_custom_call" | custom-call | flops 469762048 | bytes 5505024 | tf_op jit(solution)/shard_map/second/pallas_call | solution.py:327
  96.8 2.8 %collective-permute-start.25 = (bf16[64,1024]{1,0:T(8,128)(2,1)S(1)}, bf16[64,1024]{1,0:T(8,128)(2,1)S(1)}, u32[]{:S(2)}, u32[]{:S(2)}) collective-permute-start(bf16[64,1024]{1,0:T(8,128)(2,1)S(1)} %get-tuple-element.72), channel_id=1, source_target_pairs={{0,28},{1,29},{2,30},{3,31},{4,0},{5,1},{6,2},{7,3},{8,4},{9,5},{1... | collective-permute-start | bytes 393224 | tf_op jit(solution)/shard_map/ppermute | solution.py:36
  99.7 4.6 %second.2 = (bf16[896,896]{1,0:T(8,128)(2,1)}, bf16[896,896]{1,0:T(8,128)(2,1)}, bf16[896,1024]{1,0:T(8,128)(2,1)S(1)}) custom-call(s32[12]{0:T(128)S(1)} %stack.67.s, bf16[4,128,896]{2,1,0:T(8,128)(2,1)S(1)} %join.1.mine, bf16[4,128,896]{2,1,0:T(8,128)(2,1)S(1)} %collective-permute-done.23.other, f32[1024,896]{1,0:T(8,128)S(1)} %get-tuple-element.47.a, ...), custom_call_target="tpu_custom_call" | custom-call | flops 3288334336 | bytes 16515072 | tf_op jit(solution)/shard_map/second/pallas_call | solution.py:327
  104.3 0.7 slice.22.refs_0_
  105.2 3.2 %collective-permute-start.27 = (bf16[128,1024]{1,0:T(8,128)(2,1)S(1)}, bf16[128,1024]{1,0:T(8,128)(2,1)S(1)}, u32[]{:S(2)}, u32[]{:S(2)}) collective-permute-start(bf16[128,1024]{1,0:T(8,128)(2,1)S(1)} %get-tuple-element.52), channel_id=1, source_target_pairs={{0,28},{1,29},{2,30},{3,31},{4,0},{5,1},{6,2},{7,3},{8,4},{9,5},{1... | collective-permute-start | bytes 786440 | tf_op jit(solution)/shard_map/ppermute | solution.py:36
  108.4 2.1 %turn.1 = (bf16[1024,1024]{1,0:T(8,128)(2,1)S(1)}, f32[8,128]{1,0:T(8,128)S(1)}) custom-call(s32[12]{0:T(128)S(1)} %stack.67.s, bf16[1024,1024]{1,0:T(8,128)(2,1)S(1)} %copy-done.3, bf16[896,1024]{1,0:T(8,128)(2,1)S(1)} %get-tuple-element.49.bu.bd.after.b0), custom_call_target="tpu_custom_call" | custom-call | bytes 4194304 | tf_op jit(solution)/shard_map/turn/pallas_call | solution.py:285
  110.5 3.7 %collective-permute-done.26.up = bf16[128,1024]{1,0:T(8,128)(2,1)S(1)} collective-permute-done((bf16[128,1024]{1,0:T(8,128)(2,1)S(1)}, bf16[128,1024]{1,0:T(8,128)(2,1)S(1)}, u32[]{:S(2)}, u32[]{:S(2)}) %collective-permute-start.26) | collective-permute-done | bytes 262176 | tf_op jit(solution)/shard_map/ppermute | solution.py:36
  114.4 3.2 %collective-permute-start.29 = (bf16[128,1024]{1,0:T(8,128)(2,1)S(1)}, bf16[128,1024]{1,0:T(8,128)(2,1)S(1)}, u32[]{:S(2)}, u32[]{:S(2)}) collective-permute-start(bf16[128,1024]{1,0:T(8,128)(2,1)S(1)} %get-tuple-element.55), channel_id=1, source_target_pairs={{0,28},{1,29},{2,30},{3,31},{4,0},{5,1},{6,2},{7,3},{8,4},{9,5},{1... | collective-permute-start | bytes 786440 | tf_op jit(solution)/shard_map/ppermute | solution.py:36
  117.6 3.4 %product.4 = (bf16[1024,896]{1,0:T(8,128)(2,1)}, f32[8,128]{1,0:T(8,128)S(1)}) custom-call(bf16[1024,1024]{1,0:T(8,128)(2,1)S(1)} %get-tuple-element.56.a, bf16[896,896]{1,0:T(8,128)(2,1)S(1)} %copy-done.5, bf16[128,896]{1,0:T(8,128)(2,1)S(1)} %copy-done.7, f32[8,128]{1,0:T(8,128)S(1)} %get-tuple-element.53.refs_0_.refs_2_), custom_call_target="tpu_custom_call" | custom-call | flops 1879048192 | bytes 5767168 | tf_op jit(solution)/shard_map/product/pallas_call | solution.py:356
  121.1 1.4 collective-permute-done.28.up
  122.7 3.2 %collective-permute-start.31 = (bf16[128,1024]{1,0:T(8,128)(2,1)S(1)}, bf16[128,1024]{1,0:T(8,128)(2,1)S(1)}, u32[]{:S(2)}, u32[]{:S(2)}) collective-permute-start(bf16[128,1024]{1,0:T(8,128)(2,1)S(1)} %get-tuple-element.61), channel_id=1, source_target_pairs={{0,28},{1,29},{2,30},{3,31},{4,0},{5,1},{6,2},{7,3},{8,4},{9,5},{1... | collective-permute-start | bytes 786440 | tf_op jit(solution)/shard_map/ppermute | solution.py:36
  125.9 3.4 %product.5 = (bf16[1024,896]{1,0:T(8,128)(2,1)}, f32[8,128]{1,0:T(8,128)S(1)}) custom-call(bf16[1024,1024]{1,0:T(8,128)(2,1)S(1)} %get-tuple-element.56.a, bf16[896,896]{1,0:T(8,128)(2,1)S(1)} %copy-done.4, bf16[128,896]{1,0:T(8,128)(2,1)S(1)} %copy-done.6, f32[8,128]{1,0:T(8,128)S(1)} %get-tuple-element.59.refs_0_.refs_2_), custom_call_target="tpu_custom_call" | custom-call | flops 1879048192 | bytes 5767168 | tf_op jit(solution)/shard_map/product/pallas_call | solution.py:356
  129.4 0.9 collective-permute-done.30.up
  130.4 1.0 collective-permute-start.32
  131.4 0.9 collective-permute-start.33
  132.5 2.2 %collective-permute-done.32.r1 = bf16[32,1024]{1,0:T(8,128)(2,1)S(1)} collective-permute-done((bf16[32,1024]{1,0:T(8,128)(2,1)S(1)}, bf16[32,1024]{1,0:T(8,128)(2,1)S(1)}, u32[]{:S(2)}, u32[]{:S(2)}) %collective-permute-start.32) | collective-permute-done | bytes 65568 | tf_op jit(solution)/shard_map/ppermute | solution.py:41
  134.7 2.4 %collective-permute-done.33.r2 = bf16[32,1024]{1,0:T(8,128)(2,1)S(1)} collective-permute-done((bf16[32,1024]{1,0:T(8,128)(2,1)S(1)}, bf16[32,1024]{1,0:T(8,128)(2,1)S(1)}, u32[]{:S(2)}, u32[]{:S(2)}) %collective-permute-start.33) | collective-permute-done | bytes 65568 | tf_op jit(solution)/shard_map/ppermute | solution.py:41
  137.1 0.7 collective-permute-done.34.r3
  (76 shorter events, 4.9 us)
Async XLA Ops:
  7.2 97.1 %all-gather.2.cloned.1.call-start = ((), (), s32[]{:S(2)}) async-start(), calls=%async_computation | async-start | bytes 2162688 | tf_op jit(solution)/shard_map/all_gather | solution.py:454
  8.2 4.6 %collective-permute-start.2 = (bf16[32,1024]{1,0:T(8,128)(2,1)S(1)}, bf16[32,1024]{1,0:T(8,128)(2,1)S(1)}, u32[]{:S(2)}, u32[]{:S(2)}) collective-permute-start(bf16[32,1024]{1,0:T(8,128)(2,1)S(1)} %weigh.1.after), channel_id=1, source_target_pairs={{0,1},{1,2},{2,3},{3,0},{4,5},{5,6},{6,7},{7,4},{8,9},{9,10},{10,1... | collective-permute-start | bytes 196616 | tf_op jit(solution)/shard_map/ppermute | solution.py:41
  10.2 5.8 %collective-permute-start.1 = (bf16[32,1024]{1,0:T(8,128)(2,1)S(1)}, bf16[32,1024]{1,0:T(8,128)(2,1)S(1)}, u32[]{:S(2)}, u32[]{:S(2)}) collective-permute-start(bf16[32,1024]{1,0:T(8,128)(2,1)S(1)} %weigh.1.after), channel_id=1, source_target_pairs={{0,2},{1,3},{2,0},{3,1},{4,6},{5,7},{6,4},{7,5},{8,10},{9,11},{10,... | collective-permute-start | bytes 196616 | tf_op jit(solution)/shard_map/ppermute | solution.py:41
  11.0 5.6 %collective-permute-start = (bf16[32,1024]{1,0:T(8,128)(2,1)S(1)}, bf16[32,1024]{1,0:T(8,128)(2,1)S(1)}, u32[]{:S(2)}, u32[]{:S(2)}) collective-permute-start(bf16[32,1024]{1,0:T(8,128)(2,1)S(1)} %weigh.1.after), channel_id=1, source_target_pairs={{0,3},{1,0},{2,1},{3,2},{4,7},{5,4},{6,5},{7,6},{8,11},{9,8},{10,9... | collective-permute-start | bytes 196616 | tf_op jit(solution)/shard_map/ppermute | solution.py:41
  16.7 9.9 %collective-permute-start.3 = (bf16[128,1024]{1,0:T(8,128)(2,1)S(1)}, bf16[128,1024]{1,0:T(8,128)(2,1)S(1)}, u32[]{:S(2)}, u32[]{:S(2)}) collective-permute-start(bf16[128,1024]{1,0:T(8,128)(2,1)S(1)} %pad_maximum_fusion.1), channel_id=1, source_target_pairs={{0,28},{1,29},{2,30},{3,31},{4,0},{5,1},{6,2},{7,3},{8,4},{9,5},{1... | collective-permute-start | bytes 786440 | tf_op jit(solution)/shard_map/ppermute | solution.py:36
  22.5 7.7 %collective-permute-start.6 = (bf16[128,1024]{1,0:T(8,128)(2,1)S(1)}, bf16[128,1024]{1,0:T(8,128)(2,1)S(1)}, u32[]{:S(2)}, u32[]{:S(2)}) collective-permute-start(bf16[128,1024]{1,0:T(8,128)(2,1)S(1)} %pad_maximum_fusion.1), channel_id=1, source_target_pairs={{0,4},{1,5},{2,6},{3,7},{4,8},{5,9},{6,10},{7,11},{8,12},{9,13},{1... | collective-permute-start | bytes 786440 | tf_op jit(solution)/shard_map/ppermute | solution.py:36
  23.5 10.7 %collective-permute-start.9 = (bf16[2,128,896]{2,1,0:T(8,128)(2,1)S(1)}, bf16[2,128,896]{2,1,0:T(8,128)(2,1)S(1)}, u32[]{:S(2)}, u32[]{:S(2)}) collective-permute-start(bf16[2,128,896]{2,1,0:T(8,128)(2,1)S(1)} %pack.1), channel_id=1, source_target_pairs={{0,192},{32,224},{64,0},{96,32},{128,64},{160,96},{192,128},{224,1... | collective-permute-start | bytes 1376264 | tf_op jit(solution)/shard_map/ppermute | solution.py:46
  26.4 11.7 %collective-permute-start.11 = (bf16[2,128,896]{2,1,0:T(8,128)(2,1)S(1)}, bf16[2,128,896]{2,1,0:T(8,128)(2,1)S(1)}, u32[]{:S(2)}, u32[]{:S(2)}) collective-permute-start(bf16[2,128,896]{2,1,0:T(8,128)(2,1)S(1)} %pack.1), channel_id=1, source_target_pairs={{0,64},{32,96},{64,128},{96,160},{128,192},{160,224},{192,0},{224,... | collective-permute-start | bytes 1376264 | tf_op jit(solution)/shard_map/ppermute | solution.py:46
  26.6 11.6 %collective-permute-start.4 = (bf16[128,1024]{1,0:T(8,128)(2,1)S(1)}, bf16[128,1024]{1,0:T(8,128)(2,1)S(1)}, u32[]{:S(2)}, u32[]{:S(2)}) collective-permute-start(bf16[128,1024]{1,0:T(8,128)(2,1)S(1)} %collective-permute-done.3), channel_id=1, source_target_pairs={{0,28},{1,29},{2,30},{3,31},{4,0},{5,1},{6,2},{7,3},{8,4},{9,5},{1... | collective-permute-start | bytes 786440 | tf_op jit(solution)/shard_map/ppermute | solution.py:36
  30.1 11.1 %collective-permute-start.7 = (bf16[128,1024]{1,0:T(8,128)(2,1)S(1)}, bf16[128,1024]{1,0:T(8,128)(2,1)S(1)}, u32[]{:S(2)}, u32[]{:S(2)}) collective-permute-start(bf16[128,1024]{1,0:T(8,128)(2,1)S(1)} %collective-permute-done.6), channel_id=1, source_target_pairs={{0,4},{1,5},{2,6},{3,7},{4,8},{5,9},{6,10},{7,11},{8,12},{9,13},{1... | collective-permute-start | bytes 786440 | tf_op jit(solution)/shard_map/ppermute | solution.py:36
  34.3 7.3 %collective-permute-start.10 = (bf16[128,896]{1,0:T(8,128)(2,1)S(1)}, bf16[128,896]{1,0:T(8,128)(2,1)S(1)}, u32[]{:S(2)}, u32[]{:S(2)}) collective-permute-start(bf16[128,896]{1,0:T(8,128)(2,1)S(1)} %slice_bitcast_fusion.1), channel_id=1, source_target_pairs={{0,192},{32,224},{64,0},{96,32},{128,64},{160,96},{192,128},{224,1... | collective-permute-start | bytes 688136 | tf_op jit(solution)/shard_map/ppermute | solution.py:46
  38.1 7.3 %collective-permute-start.12 = (bf16[128,896]{1,0:T(8,128)(2,1)S(1)}, bf16[128,896]{1,0:T(8,128)(2,1)S(1)}, u32[]{:S(2)}, u32[]{:S(2)}) collective-permute-start(bf16[128,896]{1,0:T(8,128)(2,1)S(1)} %slice_bitcast_fusion), channel_id=1, source_target_pairs={{0,64},{32,96},{64,128},{96,160},{128,192},{160,224},{192,0},{224,... | collective-permute-start | bytes 688136 | tf_op jit(solution)/shard_map/ppermute | solution.py:46
  38.2 7.7 %collective-permute-start.5 = (bf16[128,1024]{1,0:T(8,128)(2,1)S(1)}, bf16[128,1024]{1,0:T(8,128)(2,1)S(1)}, u32[]{:S(2)}, u32[]{:S(2)}) collective-permute-start(bf16[128,1024]{1,0:T(8,128)(2,1)S(1)} %collective-permute-done.4), channel_id=1, source_target_pairs={{0,28},{1,29},{2,30},{3,31},{4,0},{5,1},{6,2},{7,3},{8,4},{9,5},{1... | collective-permute-start | bytes 786440 | tf_op jit(solution)/shard_map/ppermute | solution.py:36
  41.2 7.9 %collective-permute-start.8 = (bf16[128,1024]{1,0:T(8,128)(2,1)S(1)}, bf16[128,1024]{1,0:T(8,128)(2,1)S(1)}, u32[]{:S(2)}, u32[]{:S(2)}) collective-permute-start(bf16[128,1024]{1,0:T(8,128)(2,1)S(1)} %collective-permute-done.7), channel_id=1, source_target_pairs={{0,4},{1,5},{2,6},{3,7},{4,8},{5,9},{6,10},{7,11},{8,12},{9,13},{1... | collective-permute-start | bytes 786440 | tf_op jit(solution)/shard_map/ppermute | solution.py:36
  45.7 10.4 %copy-start.2 = (bf16[896,1024]{1,0:T(8,128)(2,1)S(1)}, bf16[896,1024]{1,0:T(8,128)(2,1)}, u32[]{:S(2)}) copy-start(bf16[896,1024]{1,0:T(8,128)(2,1)} %w.3) | copy-start | bytes 5505028
  45.8 19.1 %collective-permute-start.19 = (bf16[4,2,128,896]{3,2,1,0:T(8,128)(2,1)S(1)}, bf16[4,2,128,896]{3,2,1,0:T(8,128)(2,1)S(1)}, u32[]{:S(2)}, u32[]{:S(2)}) collective-permute-start(bf16[4,2,128,896]{3,2,1,0:T(8,128)(2,1)S(1)} %pad_maximum_fusion.mine), channel_id=1, source_target_pairs={{0,32},{32,0},{64,96},{96,64},{128,160},{160,128},{192,224},{224,1... | collective-permute-start | bytes 5505032 | tf_op jit(solution)/shard_map/ppermute | solution.py:50
  49.2 5.2 %collective-permute-start.13 = (bf16[64,1024]{1,0:T(8,128)(2,1)S(1)}, bf16[64,1024]{1,0:T(8,128)(2,1)S(1)}, u32[]{:S(2)}, u32[]{:S(2)}) collective-permute-start(bf16[64,1024]{1,0:T(8,128)(2,1)S(1)} %get-tuple-element.38), channel_id=1, source_target_pairs={{0,28},{1,29},{2,30},{3,31},{4,0},{5,1},{6,2},{7,3},{8,4},{9,5},{1... | collective-permute-start | bytes 393224 | tf_op jit(solution)/shard_map/ppermute | solution.py:36
  49.3 6.8 %collective-permute-start.14 = (bf16[64,1024]{1,0:T(8,128)(2,1)S(1)}, bf16[64,1024]{1,0:T(8,128)(2,1)S(1)}, u32[]{:S(2)}, u32[]{:S(2)}) collective-permute-start(bf16[64,1024]{1,0:T(8,128)(2,1)S(1)} %get-tuple-element.39), channel_id=1, source_target_pairs={{0,4},{1,5},{2,6},{3,7},{4,8},{5,9},{6,10},{7,11},{8,12},{9,13},{1... | collective-permute-start | bytes 393224 | tf_op jit(solution)/shard_map/ppermute | solution.py:36
  57.9 2.6 %collective-permute-start.15 = (bf16[4,128,896]{2,1,0:T(8,128)(2,1)S(1)}, bf16[4,128,896]{2,1,0:T(8,128)(2,1)S(1)}, u32[]{:S(2)}, u32[]{:S(2)}) collective-permute-start(bf16[4,128,896]{2,1,0:T(8,128)(2,1)S(1)} %first.3.after), channel_id=1, source_target_pairs={{0,32},{32,0},{64,96},{96,64},{128,160},{160,128},{192,224},{224,1... | collective-permute-start | bytes 2752520 | tf_op jit(solution)/shard_map/ppermute | solution.py:50
  60.6 8.9 %collective-permute-start.16 = (bf16[128,896]{1,0:T(8,128)(2,1)S(1)}, bf16[128,896]{1,0:T(8,128)(2,1)S(1)}, u32[]{:S(2)}, u32[]{:S(2)}) collective-permute-start(bf16[128,896]{1,0:T(8,128)(2,1)S(1)} %get-tuple-element.41), channel_id=1, source_target_pairs={{0,64},{32,96},{64,128},{96,160},{128,192},{160,224},{192,0},{224,... | collective-permute-start | bytes 688136 | tf_op jit(solution)/shard_map/ppermute | solution.py:46
  60.7 14.6 %collective-permute-start.17 = (bf16[128,896]{1,0:T(8,128)(2,1)S(1)}, bf16[128,896]{1,0:T(8,128)(2,1)S(1)}, u32[]{:S(2)}, u32[]{:S(2)}) collective-permute-start(bf16[128,896]{1,0:T(8,128)(2,1)S(1)} %get-tuple-element.42), channel_id=1, source_target_pairs={{0,128},{32,160},{64,192},{96,224},{128,0},{160,32},{192,64},{224,... | collective-permute-start | bytes 688136 | tf_op jit(solution)/shard_map/ppermute | solution.py:46
  64.8 10.5 %collective-permute-start.18 = (bf16[128,896]{1,0:T(8,128)(2,1)S(1)}, bf16[128,896]{1,0:T(8,128)(2,1)S(1)}, u32[]{:S(2)}, u32[]{:S(2)}) collective-permute-start(bf16[128,896]{1,0:T(8,128)(2,1)S(1)} %get-tuple-element.43), channel_id=1, source_target_pairs={{0,192},{32,224},{64,0},{96,32},{128,64},{160,96},{192,128},{224,1... | collective-permute-start | bytes 688136 | tf_op jit(solution)/shard_map/ppermute | solution.py:46
  75.5 12.4 %collective-permute-start.20 = (bf16[128,896]{1,0:T(8,128)(2,1)S(1)}, bf16[128,896]{1,0:T(8,128)(2,1)S(1)}, u32[]{:S(2)}, u32[]{:S(2)}) collective-permute-start(bf16[128,896]{1,0:T(8,128)(2,1)S(1)} %total.2.refs_3_.a), channel_id=1, source_target_pairs={{0,192},{32,224},{64,0},{96,32},{128,64},{160,96},{192,128},{224,1... | collective-permute-start | bytes 688136 | tf_op jit(solution)/shard_map/ppermute | solution.py:46
  77.9 10.0 %collective-permute-start.21 = (bf16[128,896]{1,0:T(8,128)(2,1)S(1)}, bf16[128,896]{1,0:T(8,128)(2,1)S(1)}, u32[]{:S(2)}, u32[]{:S(2)}) collective-permute-start(bf16[128,896]{1,0:T(8,128)(2,1)S(1)} %total.2.refs_3_.a), channel_id=1, source_target_pairs={{0,128},{32,160},{64,192},{96,224},{128,0},{160,32},{192,64},{224,... | collective-permute-start | bytes 688136 | tf_op jit(solution)/shard_map/ppermute | solution.py:46
  78.0 13.3 %collective-permute-start.22 = (bf16[128,896]{1,0:T(8,128)(2,1)S(1)}, bf16[128,896]{1,0:T(8,128)(2,1)S(1)}, u32[]{:S(2)}, u32[]{:S(2)}) collective-permute-start(bf16[128,896]{1,0:T(8,128)(2,1)S(1)} %total.2.refs_3_.a), channel_id=1, source_target_pairs={{0,64},{32,96},{64,128},{96,160},{128,192},{160,224},{192,0},{224,... | collective-permute-start | bytes 688136 | tf_op jit(solution)/shard_map/ppermute | solution.py:46
  78.9 15.1 %copy-start.1 = (bf16[1024,896]{1,0:T(8,128)(2,1)S(1)}, bf16[1024,896]{1,0:T(8,128)(2,1)}, u32[]{:S(2)}) copy-start(bf16[1024,896]{1,0:T(8,128)(2,1)} %uw.3) | copy-start | bytes 5505028
  82.1 11.9 %copy-start = (bf16[1024,896]{1,0:T(8,128)(2,1)S(1)}, bf16[1024,896]{1,0:T(8,128)(2,1)}, u32[]{:S(2)}) copy-start(bf16[1024,896]{1,0:T(8,128)(2,1)} %gw.3) | copy-start | bytes 5505028
  91.4 2.6 %collective-permute-start.23 = (bf16[4,128,896]{2,1,0:T(8,128)(2,1)S(1)}, bf16[4,128,896]{2,1,0:T(8,128)(2,1)S(1)}, u32[]{:S(2)}, u32[]{:S(2)}) collective-permute-start(bf16[4,128,896]{2,1,0:T(8,128)(2,1)S(1)} %join.1.mine), channel_id=1, source_target_pairs={{0,32},{32,0},{64,96},{96,64},{128,160},{160,128},{192,224},{224,1... | collective-permute-start | bytes 2752520 | tf_op jit(solution)/shard_map/ppermute | solution.py:50
  96.3 8.7 %collective-permute-start.24 = (bf16[64,1024]{1,0:T(8,128)(2,1)S(1)}, bf16[64,1024]{1,0:T(8,128)(2,1)S(1)}, u32[]{:S(2)}, u32[]{:S(2)}) collective-permute-start(bf16[64,1024]{1,0:T(8,128)(2,1)S(1)} %get-tuple-element.73), channel_id=1, source_target_pairs={{0,4},{1,5},{2,6},{3,7},{4,8},{5,9},{6,10},{7,11},{8,12},{9,13},{1... | collective-permute-start | bytes 393224 | tf_op jit(solution)/shard_map/ppermute | solution.py:36
  96.8 8.2 %collective-permute-start.25 = (bf16[64,1024]{1,0:T(8,128)(2,1)S(1)}, bf16[64,1024]{1,0:T(8,128)(2,1)S(1)}, u32[]{:S(2)}, u32[]{:S(2)}) collective-permute-start(bf16[64,1024]{1,0:T(8,128)(2,1)S(1)} %get-tuple-element.72), channel_id=1, source_target_pairs={{0,28},{1,29},{2,30},{3,31},{4,0},{5,1},{6,2},{7,3},{8,4},{9,5},{1... | collective-permute-start | bytes 393224 | tf_op jit(solution)/shard_map/ppermute | solution.py:36
  105.0 3.4 %copy-start.3 = (bf16[1024,1024]{1,0:T(8,128)(2,1)S(1)}, bf16[1024,1024]{1,0:T(8,128)(2,1)}, u32[]{:S(2)}) copy-start(bf16[1024,1024]{1,0:T(8,128)(2,1)} %all-gather.2.cloned.1.call-done.x_in) | copy-start | bytes 6291460
  105.1 9.1 %collective-permute-start.26 = (bf16[128,1024]{1,0:T(8,128)(2,1)S(1)}, bf16[128,1024]{1,0:T(8,128)(2,1)S(1)}, u32[]{:S(2)}, u32[]{:S(2)}) collective-permute-start(bf16[128,1024]{1,0:T(8,128)(2,1)S(1)} %get-tuple-element.51), channel_id=1, source_target_pairs={{0,4},{1,5},{2,6},{3,7},{4,8},{5,9},{6,10},{7,11},{8,12},{9,13},{1... | collective-permute-start | bytes 786440 | tf_op jit(solution)/shard_map/ppermute | solution.py:36
  105.2 9.0 %collective-permute-start.27 = (bf16[128,1024]{1,0:T(8,128)(2,1)S(1)}, bf16[128,1024]{1,0:T(8,128)(2,1)S(1)}, u32[]{:S(2)}, u32[]{:S(2)}) collective-permute-start(bf16[128,1024]{1,0:T(8,128)(2,1)S(1)} %get-tuple-element.52), channel_id=1, source_target_pairs={{0,28},{1,29},{2,30},{3,31},{4,0},{5,1},{6,2},{7,3},{8,4},{9,5},{1... | collective-permute-start | bytes 786440 | tf_op jit(solution)/shard_map/ppermute | solution.py:36
  114.2 3.4 %copy-start.5 = (bf16[896,896]{1,0:T(8,128)(2,1)S(1)}, bf16[896,896]{1,0:T(8,128)(2,1)}, u32[]{:S(2)}) copy-start(bf16[896,896]{1,0:T(8,128)(2,1)} %get-tuple-element.57.refs_0_) | copy-start | bytes 4816900
  114.2 3.4 %copy-start.7 = (bf16[128,896]{1,0:T(8,128)(2,1)S(1)}, bf16[128,896]{1,0:T(8,128)(2,1)}, u32[]{:S(2)}) copy-start(bf16[128,896]{1,0:T(8,128)(2,1)} %get-tuple-element.58.refs_1_) | copy-start | bytes 688132
  114.3 8.2 %collective-permute-start.28 = (bf16[128,1024]{1,0:T(8,128)(2,1)S(1)}, bf16[128,1024]{1,0:T(8,128)(2,1)S(1)}, u32[]{:S(2)}, u32[]{:S(2)}) collective-permute-start(bf16[128,1024]{1,0:T(8,128)(2,1)S(1)} %get-tuple-element.54), channel_id=1, source_target_pairs={{0,4},{1,5},{2,6},{3,7},{4,8},{5,9},{6,10},{7,11},{8,12},{9,13},{1... | collective-permute-start | bytes 786440 | tf_op jit(solution)/shard_map/ppermute | solution.py:36
  114.4 8.1 %collective-permute-start.29 = (bf16[128,1024]{1,0:T(8,128)(2,1)S(1)}, bf16[128,1024]{1,0:T(8,128)(2,1)S(1)}, u32[]{:S(2)}, u32[]{:S(2)}) collective-permute-start(bf16[128,1024]{1,0:T(8,128)(2,1)S(1)} %get-tuple-element.55), channel_id=1, source_target_pairs={{0,28},{1,29},{2,30},{3,31},{4,0},{5,1},{6,2},{7,3},{8,4},{9,5},{1... | collective-permute-start | bytes 786440 | tf_op jit(solution)/shard_map/ppermute | solution.py:36
  122.5 3.4 %copy-start.4 = (bf16[896,896]{1,0:T(8,128)(2,1)S(1)}, bf16[896,896]{1,0:T(8,128)(2,1)}, u32[]{:S(2)}) copy-start(bf16[896,896]{1,0:T(8,128)(2,1)} %get-tuple-element.62.refs_0_) | copy-start | bytes 4816900
  122.5 3.4 %copy-start.6 = (bf16[128,896]{1,0:T(8,128)(2,1)S(1)}, bf16[128,896]{1,0:T(8,128)(2,1)}, u32[]{:S(2)}) copy-start(bf16[128,896]{1,0:T(8,128)(2,1)} %get-tuple-element.63.refs_1_) | copy-start | bytes 688132
  122.6 7.7 %collective-permute-start.30 = (bf16[128,1024]{1,0:T(8,128)(2,1)S(1)}, bf16[128,1024]{1,0:T(8,128)(2,1)S(1)}, u32[]{:S(2)}, u32[]{:S(2)}) collective-permute-start(bf16[128,1024]{1,0:T(8,128)(2,1)S(1)} %get-tuple-element.60), channel_id=1, source_target_pairs={{0,4},{1,5},{2,6},{3,7},{4,8},{5,9},{6,10},{7,11},{8,12},{9,13},{1... | collective-permute-start | bytes 786440 | tf_op jit(solution)/shard_map/ppermute | solution.py:36
  122.7 7.6 %collective-permute-start.31 = (bf16[128,1024]{1,0:T(8,128)(2,1)S(1)}, bf16[128,1024]{1,0:T(8,128)(2,1)S(1)}, u32[]{:S(2)}, u32[]{:S(2)}) collective-permute-start(bf16[128,1024]{1,0:T(8,128)(2,1)S(1)} %get-tuple-element.61), channel_id=1, source_target_pairs={{0,28},{1,29},{2,30},{3,31},{4,0},{5,1},{6,2},{7,3},{8,4},{9,5},{1... | collective-permute-start | bytes 786440 | tf_op jit(solution)/shard_map/ppermute | solution.py:36
  130.4 4.3 %collective-permute-start.32 = (bf16[32,1024]{1,0:T(8,128)(2,1)S(1)}, bf16[32,1024]{1,0:T(8,128)(2,1)S(1)}, u32[]{:S(2)}, u32[]{:S(2)}) collective-permute-start(bf16[32,1024]{1,0:T(8,128)(2,1)S(1)} %get-tuple-element.66), channel_id=1, source_target_pairs={{0,1},{1,2},{2,3},{3,0},{4,5},{5,6},{6,7},{7,4},{8,9},{9,10},{10,1... | collective-permute-start | bytes 196616 | tf_op jit(solution)/shard_map/ppermute | solution.py:41
  131.4 5.8 %collective-permute-start.33 = (bf16[32,1024]{1,0:T(8,128)(2,1)S(1)}, bf16[32,1024]{1,0:T(8,128)(2,1)S(1)}, u32[]{:S(2)}, u32[]{:S(2)}) collective-permute-start(bf16[32,1024]{1,0:T(8,128)(2,1)S(1)} %get-tuple-element.67), channel_id=1, source_target_pairs={{0,2},{1,3},{2,0},{3,1},{4,6},{5,7},{6,4},{7,5},{8,10},{9,11},{10,... | collective-permute-start | bytes 196616 | tf_op jit(solution)/shard_map/ppermute | solution.py:41
  132.3 5.6 %collective-permute-start.34 = (bf16[32,1024]{1,0:T(8,128)(2,1)S(1)}, bf16[32,1024]{1,0:T(8,128)(2,1)S(1)}, u32[]{:S(2)}, u32[]{:S(2)}) collective-permute-start(bf16[32,1024]{1,0:T(8,128)(2,1)S(1)} %get-tuple-element.68), channel_id=1, source_target_pairs={{0,3},{1,0},{2,1},{3,2},{4,7},{5,4},{6,5},{7,6},{8,11},{9,8},{10,9... | collective-permute-start | bytes 196616 | tf_op jit(solution)/shard_map/ppermute | solution.py:41
Sparse Core Ops, SparseCore 0:
  26.5 75.9 all-gather.1

commit v4 on v3

--- a/solution.py
+++ b/solution.py
@@ -12,7 +12,7 @@
 BLK = NY * TOK
 HALF = BLK // NC
 SUB = HALF // NX
-ORDER = (0, 1, 2, 3, 5, 6, 7, 4)
+ORDER = (0, 1, 2, 6, 7, 3, 5, 4)
 BF, F32 = jnp.bfloat16, jnp.float32
 HBM = pl.BlockSpec(memory_space=pltpu.HBM)
 VMEM = pl.BlockSpec(memory_space=pltpu.VMEM)
@@ -300,7 +300,7 @@
     )(place, x_all, after)
 
 
-def second_kernel(s, mine, other, a, b, gw, uw, dg, du, p):
+def second_kernel(s, mine, other, a, b, gw, uw, after, dg, du, p):
     for j in range(dg.shape[0] // BLK):
         here = slice(j * SUB, (j + 1) * SUB)
         for half in range(NC):
@@ -314,7 +314,7 @@
     p[...] = (nt(dg[...], gw[...]) + nt(du[...], uw[...])).astype(BF)
 
 
-def second(place, mine, other, a, b, gate_weight, up_weight, at, n):
+def second(place, mine, other, a, b, gate_weight, up_weight, at, n, after):
     ff = a.shape[1]
     width = gate_weight.shape[0]
     rows = n * BLK
@@ -322,14 +322,16 @@
     def whole(*shape):
         return pl.BlockSpec(shape, lambda t, s: (0,) * len(shape))
 
-    got = pl.BlockSpec((NX, n * SUB, ff), lambda t, s: (0, at // n, 0))
-    row = pl.BlockSpec((rows, ff), lambda t, s: (at // n, 0))
+    got = pl.BlockSpec(
+        (pl.Element(NX), pl.Element(n * SUB), pl.Element(ff)), lambda t, s: (0, at * SUB, 0)
+    )
+    row = pl.BlockSpec((pl.Element(rows), pl.Element(ff)), lambda t, s: (at * BLK, 0))
     return pl.pallas_call(
         second_kernel,
         grid_spec=pltpu.PrefetchScalarGridSpec(
             num_scalar_prefetch=1,
             grid=(1,),
-            in_specs=[got, got, row, row, whole(width, ff), whole(width, ff)],
+            in_specs=[got, got, row, row, whole(width, ff), whole(width, ff), HBM],
             out_specs=[whole(rows, ff), whole(rows, ff), whole(rows, width)],
         ),
         out_shape=[
@@ -340,7 +342,7 @@
         compiler_params=params(32),
         cost_estimate=cost(4 * rows * ff * width, 16 * rows * ff + 4 * ff * width),
         name="second",
-    )(place, mine, other, a, b, gate_weight, up_weight)
+    )(place, mine, other, a, b, gate_weight, up_weight, after)
 
 
 def product_kernel(n, a, *refs):
@@ -427,11 +429,10 @@
     )(p, up, down, after)
 
 
-def scatter_z_y(p, ends, marks):
-    up, down = step(near_kernel, p, 3, 4, *ends, *marks[0])
-    for n, i, j in ((1, 2, 5), (2, 1, 6)):
-        up, down = step(step_kernel, p, i, j, from_z(up, -1), from_z(down, 1), marks[n])
-    own, *sent = own_of(p, from_z(up, -1), from_z(down, 1), marks[3])
+def scatter_z_y(p, up, down, marks):
+    for mark, i, j in ((marks[0], 2, 3), (marks[1], 1, 4)):
+        up, down = step(step_kernel, p, i, j, from_z(up, -1), from_z(down, 1), mark)
+    own, *sent = own_of(p, from_z(up, -1), from_z(down, 1), marks[2])
     return total_of(own, [from_y(v, -k) for k, v in enumerate(sent, 1)])
 
 
@@ -463,7 +464,7 @@
     far_pre = from_x(next_pre[0], 1), from_x(last_pre[1], -1)
     low, high = halves(up[3], down[3], far_pre)
     low, high = from_z(low, 1), from_z(high, -1)
-    dy = jnp.stack(up + [down[3], down[2], down[1]], axis=0)
+    dy = jnp.stack(up[:3] + [down[2], down[1], up[3], down[3]], axis=0)
     pre_mine = jnp.stack([pre, next_pre, jnp.stack(far_pre, axis=0), last_pre], axis=0)
     pre_other = from_core(pre_mine)
 
@@ -475,16 +476,18 @@
     grad_down, mark_0 = product(hidden_t, [flat, low, high], 448, total)
     mine = join([total] + [from_x(total, k) for k in range(1, NX)], mark_0)
     args = place, mine, from_core(mine), a, b, gate_weight, up_weight
-    far = second(*args, NZ - 1, 1)
+    far = second(*args, 7, 1, mark_0)
     last = far[2]
     ends = from_z(last[:HALF], -1), from_z(last[HALF:], 1)
-    near = second(*args, 0, NZ - 1)
-    d_gate, d_up, part = zip(near, far)
+    middle = second(*args, 5, 2, last)
+    ends = step(near_kernel, middle[2], 0, 1, *ends)
+    near = second(*args, 0, 5, ends[0])
+    d_gate, d_up, _ = zip(near, middle, far)
 
     x_t, mark_1 = turn(place, x_all, near[2])
     grad_gate, mark_2 = product(x_t, d_gate, 512, mark_1)
     grad_up, mark_3 = product(x_t, d_up, 512, mark_2)
-    grad_input = scatter_z_y(near[2], ends, ((x_all[:16, :128],), mark_1, mark_2, mark_3))
+    grad_input = scatter_z_y(near[2], *ends, (mark_1, mark_2, mark_3))
     return (grad_input, grad_gate, grad_up, grad_down)
 
 

time: 146 us -> 147 us (level)
  waiting for transfers between devices: 52.3 us -> 48.9 us
  starting transfers between devices: 47.4 us -> 49.6 us
  Pallas kernels: 30 us -> 31.6 us
    ppermute x6, starting transfers between devices: 5.1 us -> 7.61 us  [from_y(): return lax.ppermute(v, 'col', perm)]
    ppermute x16, waiting for transfers between devices: 14 us -> 12.3 us  [from_z(): return lax.ppermute(v, 'col', perm)]
    unnamed x21 -> x25, local copies, waits for them, and re-layouts: 0.12 us -> 1.73 us
    ppermute x6, waiting for transfers between devices: 10.9 us -> 9.29 us  [from_y(): return lax.ppermute(v, 'col', perm)]
    pallas_call x2 -> x3, Pallas kernels: 7.02 us -> 8.56 us  [second(): pl.pallas_call(second_kernel, grid_spec=pltpu.PrefetchScalarGridSpec(num_...]
  transfers between devices with their start and end apart: 36 -> 36, of which waited for: 22 -> 23; matrix products, arithmetic and copies ran while one was open for 1% -> 0% of each run, Pallas kernels for 19% -> 20%
where the time goes in v4:
time: 147 us
  starting transfers between devices  49.6 us (34%)
  waiting for transfers between devices  48.9 us (33%)
  Pallas kernels  31.6 us (21%)
  between operations  14.4 us (10%)
  local copies, waits for them, and re-layouts  1.89 us (1%)
    ppermute x16, starting transfers between devices, from_z(): return lax.ppermute(v, 'col', perm)  27.4 us
    ppermute x10, waiting for transfers between devices, from_x(): return lax.ppermute(v, 'row', perm)  24.2 us
    ppermute x10, starting transfers between devices, from_x(): return lax.ppermute(v, 'row', perm)  14.3 us
    ppermute x16, waiting for transfers between devices, from_z(): return lax.ppermute(v, 'col', perm)  12.3 us
    pallas_call x3, Pallas kernels, product(): pl.pallas_call(functools.partial(product_kernel, len(parts)), grid=(m //...  10.1 us
    ppermute x6, waiting for transfers between devices, from_y(): return lax.ppermute(v, 'col', perm)  9.29 us
    pallas_call x3, Pallas kernels, second(): pl.pallas_call(second_kernel, grid_spec=pltpu.PrefetchScalarGridSpec(num_...  8.56 us
    ppermute x6, starting transfers between devices, from_y(): return lax.ppermute(v, 'col', perm)  7.61 us
  transfers between devices with their start and end apart: 36, of which 23 were waited for; matrix products, arithmetic and copies ran while one was open for 0% of the time, Pallas kernels for 20%

profile of v4, /device:TPU:24, one launch (start us, length us, event | category | flops | bytes accessed | tf_op | source)
XLA Modules:
  0.0 146.8 jit_solution(17185495599797618859)
XLA Ops:
  7.2 0.9 weigh.1.after
  8.2 0.8 collective-permute-start
  9.0 2.7 %collective-permute-start.1 = (bf16[32,1024]{1,0:T(8,128)(2,1)S(1)}, bf16[32,1024]{1,0:T(8,128)(2,1)S(1)}, u32[]{:S(2)}, u32[]{:S(2)}) collective-permute-start(bf16[32,1024]{1,0:T(8,128)(2,1)S(1)} %weigh.1.after), channel_id=1, source_target_pairs={{0,2},{1,3},{2,0},{3,1},{4,6},{5,7},{6,4},{7,5},{8,10},{9,11},{10,... | collective-permute-start | bytes 196616 | tf_op jit(solution)/shard_map/ppermute | solution.py:41
  12.1 1.9 %collective-permute-done = bf16[32,1024]{1,0:T(8,128)(2,1)S(1)} collective-permute-done((bf16[32,1024]{1,0:T(8,128)(2,1)S(1)}, bf16[32,1024]{1,0:T(8,128)(2,1)S(1)}, u32[]{:S(2)}, u32[]{:S(2)}) %collective-permute-start) | collective-permute-done | bytes 65568 | tf_op jit(solution)/shard_map/ppermute | solution.py:41
  14.7 1.2 collective-permute-done.2
  15.9 5.3 %collective-permute-start.3 = (bf16[128,1024]{1,0:T(8,128)(2,1)S(1)}, bf16[128,1024]{1,0:T(8,128)(2,1)S(1)}, u32[]{:S(2)}, u32[]{:S(2)}) collective-permute-start(bf16[128,1024]{1,0:T(8,128)(2,1)S(1)} %pad_maximum_fusion.1), channel_id=1, source_target_pairs={{0,28},{1,29},{2,30},{3,31},{4,0},{5,1},{6,2},{7,3},{8,4},{9,5},{1... | collective-permute-start | bytes 786440 | tf_op jit(solution)/shard_map/ppermute | solution.py:36
  21.2 1.1 pack.1
  22.3 2.8 %collective-permute-start.9 = (bf16[2,128,896]{2,1,0:T(8,128)(2,1)S(1)}, bf16[2,128,896]{2,1,0:T(8,128)(2,1)S(1)}, u32[]{:S(2)}, u32[]{:S(2)}) collective-permute-start(bf16[2,128,896]{2,1,0:T(8,128)(2,1)S(1)} %pack.1), channel_id=1, source_target_pairs={{0,192},{32,224},{64,0},{96,32},{128,64},{160,96},{192,128},{224,1... | collective-permute-start | bytes 1376264 | tf_op jit(solution)/shard_map/ppermute | solution.py:46
  25.7 3.7 %collective-permute-start.4 = (bf16[128,1024]{1,0:T(8,128)(2,1)S(1)}, bf16[128,1024]{1,0:T(8,128)(2,1)S(1)}, u32[]{:S(2)}, u32[]{:S(2)}) collective-permute-start(bf16[128,1024]{1,0:T(8,128)(2,1)S(1)} %collective-permute-done.3), channel_id=1, source_target_pairs={{0,28},{1,29},{2,30},{3,31},{4,0},{5,1},{6,2},{7,3},{8,4},{9,5},{1... | collective-permute-start | bytes 786440 | tf_op jit(solution)/shard_map/ppermute | solution.py:36
  29.4 4.1 %collective-permute-done.9 = bf16[2,128,896]{2,1,0:T(8,128)(2,1)S(1)} collective-permute-done((bf16[2,128,896]{2,1,0:T(8,128)(2,1)S(1)}, bf16[2,128,896]{2,1,0:T(8,128)(2,1)S(1)}, u32[]{:S(2)}, u32[]{:S(2)}) %collective-permute-start.9) | collective-permute-done | bytes 458784 | tf_op jit(solution)/shard_map/ppermute | solution.py:46
  33.5 3.8 %collective-permute-start.10 = (bf16[128,896]{1,0:T(8,128)(2,1)S(1)}, bf16[128,896]{1,0:T(8,128)(2,1)S(1)}, u32[]{:S(2)}, u32[]{:S(2)}) collective-permute-start(bf16[128,896]{1,0:T(8,128)(2,1)S(1)} %slice_bitcast_fusion.1), channel_id=1, source_target_pairs={{0,192},{32,224},{64,0},{96,32},{128,64},{160,96},{192,128},{224,1... | collective-permute-start | bytes 688136 | tf_op jit(solution)/shard_map/ppermute | solution.py:46
  37.4 3.0 %collective-permute-start.7 = (bf16[128,1024]{1,0:T(8,128)(2,1)S(1)}, bf16[128,1024]{1,0:T(8,128)(2,1)S(1)}, u32[]{:S(2)}, u32[]{:S(2)}) collective-permute-start(bf16[128,1024]{1,0:T(8,128)(2,1)S(1)} %collective-permute-done.4), channel_id=1, source_target_pairs={{0,28},{1,29},{2,30},{3,31},{4,0},{5,1},{6,2},{7,3},{8,4},{9,5},{1... | collective-permute-start | bytes 786440 | tf_op jit(solution)/shard_map/ppermute | solution.py:36
  40.8 3.8 %collective-permute-done.12.r2 = bf16[128,896]{1,0:T(8,128)(2,1)S(1)} collective-permute-done((bf16[128,896]{1,0:T(8,128)(2,1)S(1)}, bf16[128,896]{1,0:T(8,128)(2,1)S(1)}, u32[]{:S(2)}, u32[]{:S(2)}) %collective-permute-start.12) | collective-permute-done | bytes 229408 | tf_op jit(solution)/shard_map/ppermute | solution.py:46
  45.1 3.4 %collective-permute-done.8.d = bf16[128,1024]{1,0:T(8,128)(2,1)S(1)} collective-permute-done((bf16[128,1024]{1,0:T(8,128)(2,1)S(1)}, bf16[128,1024]{1,0:T(8,128)(2,1)S(1)}, u32[]{:S(2)}, u32[]{:S(2)}) %collective-permute-start.8) | collective-permute-done | bytes 262176 | tf_op jit(solution)/shard_map/ppermute | solution.py:36
  48.6 2.0 %collective-permute-start.14 = (bf16[64,1024]{1,0:T(8,128)(2,1)S(1)}, bf16[64,1024]{1,0:T(8,128)(2,1)S(1)}, u32[]{:S(2)}, u32[]{:S(2)}) collective-permute-start(bf16[64,1024]{1,0:T(8,128)(2,1)S(1)} %get-tuple-element.42), channel_id=1, source_target_pairs={{0,4},{1,5},{2,6},{3,7},{4,8},{5,9},{6,10},{7,11},{8,12},{9,13},{1... | collective-permute-start | bytes 393224 | tf_op jit(solution)/shard_map/ppermute | solution.py:36
  50.7 3.1 %collective-permute-done.13.low.refs_1_ = bf16[64,1024]{1,0:T(8,128)(2,1)S(1)} collective-permute-done((bf16[64,1024]{1,0:T(8,128)(2,1)S(1)}, bf16[64,1024]{1,0:T(8,128)(2,1)S(1)}, u32[]{:S(2)}, u32[]{:S(2)}) %collective-permute-start.13) | collective-permute-done | bytes 131104 | tf_op jit(solution)/shard_map/ppermute | solution.py:36
  53.8 1.6 %collective-permute-done.14.high.refs_2_ = bf16[64,1024]{1,0:T(8,128)(2,1)S(1)} collective-permute-done((bf16[64,1024]{1,0:T(8,128)(2,1)S(1)}, bf16[64,1024]{1,0:T(8,128)(2,1)S(1)}, u32[]{:S(2)}, u32[]{:S(2)}) %collective-permute-start.14) | collective-permute-done | bytes 131104 | tf_op jit(solution)/shard_map/ppermute | solution.py:36
  55.4 1.8 %first.3.after = bf16[4,128,896]{2,1,0:T(8,128)(2,1)S(1)} custom-call(s32[12]{0:T(128)S(1)} %stack.67.s, bf16[7,128,1024]{2,1,0:T(8,128)(2,1)S(1)} %bitcast_dynamic-update-slice_fusion.dy, bf16[64,1024]{1,0:T(8,128)(2,1)S(1)} %collective-permute-done.13.low.refs_1_, bf16[64,1024]{1,0:T(8,128)(2,1)S(1)} %collective-permute-done.14.high.refs_2_, ...), custom_call_target="tpu_custom_call" | custom-call | flops 939524096 | bytes 5767168 | tf_op jit(solution)/shard_map/first/pallas_call | solution.py:151
  57.3 1.8 %first.2.own = f32[4,128,896]{2,1,0:T(8,128)S(1)} custom-call(s32[12]{0:T(128)S(1)} %stack.67.s, bf16[7,128,1024]{2,1,0:T(8,128)(2,1)S(1)} %bitcast_dynamic-update-slice_fusion.dy, bf16[64,1024]{1,0:T(8,128)(2,1)S(1)} %collective-permute-done.13.low.refs_1_, bf16[64,1024]{1,0:T(8,128)(2,1)S(1)} %collective-permute-done.14.high.refs_2_, ...), custom_call_target="tpu_custom_call" | custom-call | flops 939524096 | bytes 5767168 | tf_op jit(solution)/shard_map/first/pallas_call | solution.py:151
  60.0 4.2 %collective-permute-start.17 = (bf16[128,896]{1,0:T(8,128)(2,1)S(1)}, bf16[128,896]{1,0:T(8,128)(2,1)S(1)}, u32[]{:S(2)}, u32[]{:S(2)}) collective-permute-start(bf16[128,896]{1,0:T(8,128)(2,1)S(1)} %get-tuple-element.45), channel_id=1, source_target_pairs={{0,128},{32,160},{64,192},{96,224},{128,0},{160,32},{192,64},{224,... | collective-permute-start | bytes 688136 | tf_op jit(solution)/shard_map/ppermute | solution.py:46
  64.2 3.7 %prep.1 = (bf16[896,1024]{1,0:T(8,128)(2,1)S(1)}, f32[1024,896]{1,0:T(8,128)S(1)}, f32[1024,896]{1,0:T(8,128)S(1)}, f32[8,128]{1,0:T(8,128)S(1)}) custom-call(s32[12]{0:T(128)S(1)} %stack.67.s, bf16[4,2,128,896]{3,2,1,0:T(8,128)(2,1)S(1)} %pad_maximum_fusion.mine, bf16[4,2,128,896]{3,2,1,0:T(8,128)(2,1)S(1)} %collective-permute-done.19.other, ...), custom_call_target="tpu_custom_call" | custom-call | flops 27525120 | bytes 12845056 | tf_op jit(solution)/shard_map/prep/pallas_call | solution.py:252
  68.0 0.9 collective-permute-done.16.r1
  68.8 5.9 %collective-permute-done.17.r2 = bf16[128,896]{1,0:T(8,128)(2,1)S(1)} collective-permute-done((bf16[128,896]{1,0:T(8,128)(2,1)S(1)}, bf16[128,896]{1,0:T(8,128)(2,1)S(1)}, u32[]{:S(2)}, u32[]{:S(2)}) %collective-permute-start.17) | collective-permute-done | bytes 229408 | tf_op jit(solution)/shard_map/ppermute | solution.py:46
  74.9 2.3 %collective-permute-start.20 = (bf16[128,896]{1,0:T(8,128)(2,1)S(1)}, bf16[128,896]{1,0:T(8,128)(2,1)S(1)}, u32[]{:S(2)}, u32[]{:S(2)}) collective-permute-start(bf16[128,896]{1,0:T(8,128)(2,1)S(1)} %total.2.refs_3_.a), channel_id=1, source_target_pairs={{0,192},{32,224},{64,0},{96,32},{128,64},{160,96},{192,128},{224,1... | collective-permute-start | bytes 688136 | tf_op jit(solution)/shard_map/ppermute | solution.py:46
  77.4 0.8 collective-permute-start.22
  78.1 3.2 %product.3 = (bf16[896,1024]{1,0:T(8,128)(2,1)}, f32[8,128]{1,0:T(8,128)S(1)}) custom-call(bf16[896,1024]{1,0:T(8,128)(2,1)S(1)} %get-tuple-element.48.a, bf16[896,1024]{1,0:T(8,128)(2,1)S(1)} %bitcast.30, bf16[64,1024]{1,0:T(8,128)(2,1)S(1)} %collective-permute-done.13.low.refs_1_, bf16[64,1024]{1,0:T(8,128)(2,1)S(1)} %collective-permute-done.14.high.refs_2_, ...), custom_call_target="tpu_custom_call" | custom-call | flops 1879048192 | bytes 5767168 | tf_op jit(solution)/shard_map/product/pallas_call | solution.py:358
  81.3 5.8 %collective-permute-done.20.b = bf16[128,896]{1,0:T(8,128)(2,1)S(1)} collective-permute-done((bf16[128,896]{1,0:T(8,128)(2,1)S(1)}, bf16[128,896]{1,0:T(8,128)(2,1)S(1)}, u32[]{:S(2)}, u32[]{:S(2)}) %collective-permute-start.20) | collective-permute-done | bytes 229408 | tf_op jit(solution)/shard_map/ppermute | solution.py:46
  87.2 3.4 %collective-permute-done.22.d = bf16[128,896]{1,0:T(8,128)(2,1)S(1)} collective-permute-done((bf16[128,896]{1,0:T(8,128)(2,1)S(1)}, bf16[128,896]{1,0:T(8,128)(2,1)S(1)}, u32[]{:S(2)}, u32[]{:S(2)}) %collective-permute-start.22) | collective-permute-done | bytes 229408 | tf_op jit(solution)/shard_map/ppermute | solution.py:46
  90.7 2.5 %collective-permute-done.23.other = bf16[4,128,896]{2,1,0:T(8,128)(2,1)S(1)} collective-permute-done((bf16[4,128,896]{2,1,0:T(8,128)(2,1)S(1)}, bf16[4,128,896]{2,1,0:T(8,128)(2,1)S(1)}, u32[]{:S(2)}, u32[]{:S(2)}) %collective-permute-start.23) | collective-permute-done | bytes 917536 | tf_op jit(solution)/shard_map/ppermute | solution.py:50
  93.2 2.4 %second.3 = (bf16[128,896]{1,0:T(8,128)(2,1)}, bf16[128,896]{1,0:T(8,128)(2,1)}, bf16[128,1024]{1,0:T(8,128)(2,1)S(1)}) custom-call(s32[12]{0:T(128)S(1)} %stack.67.s, bf16[4,128,896]{2,1,0:T(8,128)(2,1)S(1)} %join.1.mine, bf16[4,128,896]{2,1,0:T(8,128)(2,1)S(1)} %collective-permute-done.23.other, f32[1024,896]{1,0:T(8,128)S(1)} %get-tuple-element.50.a, ...), custom_call_target="tpu_custom_call" | custom-call | flops 469762048 | bytes 5505024 | tf_op jit(solution)/shard_map/second/pallas_call | solution.py:329
  96.2 2.8 %collective-permute-start.25 = (bf16[64,1024]{1,0:T(8,128)(2,1)S(1)}, bf16[64,1024]{1,0:T(8,128)(2,1)S(1)}, u32[]{:S(2)}, u32[]{:S(2)}) collective-permute-start(bf16[64,1024]{1,0:T(8,128)(2,1)S(1)} %get-tuple-element.78), channel_id=1, source_target_pairs={{0,28},{1,29},{2,30},{3,31},{4,0},{5,1},{6,2},{7,3},{8,4},{9,5},{1... | collective-permute-start | bytes 393224 | tf_op jit(solution)/shard_map/ppermute | solution.py:36
  98.9 2.5 %second.4 = (bf16[256,896]{1,0:T(8,128)(2,1)}, bf16[256,896]{1,0:T(8,128)(2,1)}, bf16[256,1024]{1,0:T(8,128)(2,1)S(1)}) custom-call(s32[12]{0:T(128)S(1)} %stack.67.s, bf16[4,128,896]{2,1,0:T(8,128)(2,1)S(1)} %join.1.mine, bf16[4,128,896]{2,1,0:T(8,128)(2,1)S(1)} %collective-permute-done.23.other, f32[1024,896]{1,0:T(8,128)S(1)} %get-tuple-element.50.a, ...), custom_call_target="tpu_custom_call" | custom-call | flops 939524096 | bytes 7340032 | tf_op jit(solution)/shard_map/second/pallas_call | solution.py:329
  101.4 1.4 collective-permute-done.24.up
  103.0 3.2 %collective-permute-start.27 = (bf16[128,1024]{1,0:T(8,128)(2,1)S(1)}, bf16[128,1024]{1,0:T(8,128)(2,1)S(1)}, u32[]{:S(2)}, u32[]{:S(2)}) collective-permute-start(bf16[128,1024]{1,0:T(8,128)(2,1)S(1)} %get-tuple-element.56), channel_id=1, source_target_pairs={{0,28},{1,29},{2,30},{3,31},{4,0},{5,1},{6,2},{7,3},{8,4},{9,5},{1... | collective-permute-start | bytes 786440 | tf_op jit(solution)/shard_map/ppermute | solution.py:36
  106.2 3.7 %second.5 = (bf16[640,896]{1,0:T(8,128)(2,1)}, bf16[640,896]{1,0:T(8,128)(2,1)}, bf16[640,1024]{1,0:T(8,128)(2,1)S(1)}) custom-call(s32[12]{0:T(128)S(1)} %stack.67.s, bf16[4,128,896]{2,1,0:T(8,128)(2,1)S(1)} %join.1.mine, bf16[4,128,896]{2,1,0:T(8,128)(2,1)S(1)} %collective-permute-done.23.other, f32[1024,896]{1,0:T(8,128)S(1)} %get-tuple-element.50.a, ...), custom_call_target="tpu_custom_call" | custom-call | flops 2348810240 | bytes 12845056 | tf_op jit(solution)/shard_map/second/pallas_call | solution.py:329
  109.9 1.6 %copy-done.3 = bf16[1024,1024]{1,0:T(8,128)(2,1)S(1)} copy-done((bf16[1024,1024]{1,0:T(8,128)(2,1)S(1)}, bf16[1024,1024]{1,0:T(8,128)(2,1)}, u32[]{:S(2)}) %copy-start.3) | copy-done | bytes 2097176
  111.5 2.1 %turn.1 = (bf16[1024,1024]{1,0:T(8,128)(2,1)S(1)}, f32[8,128]{1,0:T(8,128)S(1)}) custom-call(s32[12]{0:T(128)S(1)} %stack.67.s, bf16[1024,1024]{1,0:T(8,128)(2,1)S(1)} %copy-done.3, bf16[640,1024]{1,0:T(8,128)(2,1)S(1)} %get-tuple-element.55.after.bu.bd.b0), custom_call_target="tpu_custom_call" | custom-call | bytes 4194304 | tf_op jit(solution)/shard_map/turn/pallas_call | solution.py:285
  113.9 3.2 %collective-permute-start.29 = (bf16[128,1024]{1,0:T(8,128)(2,1)S(1)}, bf16[128,1024]{1,0:T(8,128)(2,1)S(1)}, u32[]{:S(2)}, u32[]{:S(2)}) collective-permute-start(bf16[128,1024]{1,0:T(8,128)(2,1)S(1)} %get-tuple-element.59), channel_id=1, source_target_pairs={{0,28},{1,29},{2,30},{3,31},{4,0},{5,1},{6,2},{7,3},{8,4},{9,5},{1... | collective-permute-start | bytes 786440 | tf_op jit(solution)/shard_map/ppermute | solution.py:36
  117.1 3.5 %product.4 = (bf16[1024,896]{1,0:T(8,128)(2,1)}, f32[8,128]{1,0:T(8,128)S(1)}) custom-call(bf16[1024,1024]{1,0:T(8,128)(2,1)S(1)} %get-tuple-element.60.a, bf16[640,896]{1,0:T(8,128)(2,1)S(1)} %copy-done.5, bf16[256,896]{1,0:T(8,128)(2,1)S(1)} %copy-done.7, bf16[128,896]{1,0:T(8,128)(2,1)S(1)} %copy-done.9, f32[8,128]{1,0:T(8,128)S(1)} %get-tuple-element.57.refs_0_.refs_3_), custom_call_target="tpu_custom_call" | custom-call | flops 1879048192 | bytes 5767168 | tf_op jit(solution)/shard_map/product/pallas_call | solution.py:358
  120.6 1.6 %collective-permute-done.28.up = bf16[128,1024]{1,0:T(8,128)(2,1)S(1)} collective-permute-done((bf16[128,1024]{1,0:T(8,128)(2,1)S(1)}, bf16[128,1024]{1,0:T(8,128)(2,1)S(1)}, u32[]{:S(2)}, u32[]{:S(2)}) %collective-permute-start.28) | collective-permute-done | bytes 262176 | tf_op jit(solution)/shard_map/ppermute | solution.py:36
  122.4 3.2 %collective-permute-start.31 = (bf16[128,1024]{1,0:T(8,128)(2,1)S(1)}, bf16[128,1024]{1,0:T(8,128)(2,1)S(1)}, u32[]{:S(2)}, u32[]{:S(2)}) collective-permute-start(bf16[128,1024]{1,0:T(8,128)(2,1)S(1)} %get-tuple-element.66), channel_id=1, source_target_pairs={{0,28},{1,29},{2,30},{3,31},{4,0},{5,1},{6,2},{7,3},{8,4},{9,5},{1... | collective-permute-start | bytes 786440 | tf_op jit(solution)/shard_map/ppermute | solution.py:36
  125.7 3.5 %product.5 = (bf16[1024,896]{1,0:T(8,128)(2,1)}, f32[8,128]{1,0:T(8,128)S(1)}) custom-call(bf16[1024,1024]{1,0:T(8,128)(2,1)S(1)} %get-tuple-element.60.a, bf16[640,896]{1,0:T(8,128)(2,1)S(1)} %copy-done.4, bf16[256,896]{1,0:T(8,128)(2,1)S(1)} %copy-done.6, bf16[128,896]{1,0:T(8,128)(2,1)S(1)} %copy-done.8, f32[8,128]{1,0:T(8,128)S(1)} %get-tuple-element.64.refs_0_.refs_3_), custom_call_target="tpu_custom_call" | custom-call | flops 1879048192 | bytes 5767168 | tf_op jit(solution)/shard_map/product/pallas_call | solution.py:358
  129.1 0.9 collective-permute-done.30.up
  130.1 2.6 %collective-permute-start.32 = (bf16[32,1024]{1,0:T(8,128)(2,1)S(1)}, bf16[32,1024]{1,0:T(8,128)(2,1)S(1)}, u32[]{:S(2)}, u32[]{:S(2)}) collective-permute-start(bf16[32,1024]{1,0:T(8,128)(2,1)S(1)} %get-tuple-element.72), channel_id=1, source_target_pairs={{0,1},{1,2},{2,3},{3,0},{4,5},{5,6},{6,7},{7,4},{8,9},{9,10},{10,1... | collective-permute-start | bytes 196616 | tf_op jit(solution)/shard_map/ppermute | solution.py:41
  132.7 1.1 collective-permute-start.33
  133.8 1.4 collective-permute-done.32.r1
  135.2 3.3 %collective-permute-done.33.r2 = bf16[32,1024]{1,0:T(8,128)(2,1)S(1)} collective-permute-done((bf16[32,1024]{1,0:T(8,128)(2,1)S(1)}, bf16[32,1024]{1,0:T(8,128)(2,1)S(1)}, u32[]{:S(2)}, u32[]{:S(2)}) %collective-permute-start.33) | collective-permute-done | bytes 65568 | tf_op jit(solution)/shard_map/ppermute | solution.py:41
  138.4 0.8 collective-permute-done.34.r3
  (80 shorter events, 6.2 us)
Async XLA Ops:
  7.2 102.7 %all-gather.2.cloned.1.call-start = ((), (), s32[]{:S(2)}) async-start(), calls=%async_computation | async-start | bytes 2162688 | tf_op jit(solution)/shard_map/all_gather | solution.py:455
  8.2 5.9 %collective-permute-start = (bf16[32,1024]{1,0:T(8,128)(2,1)S(1)}, bf16[32,1024]{1,0:T(8,128)(2,1)S(1)}, u32[]{:S(2)}, u32[]{:S(2)}) collective-permute-start(bf16[32,1024]{1,0:T(8,128)(2,1)S(1)} %weigh.1.after), channel_id=1, source_target_pairs={{0,3},{1,0},{2,1},{3,2},{4,7},{5,4},{6,5},{7,6},{8,11},{9,8},{10,9... | collective-permute-start | bytes 196616 | tf_op jit(solution)/shard_map/ppermute | solution.py:41
  9.0 5.8 %collective-permute-start.1 = (bf16[32,1024]{1,0:T(8,128)(2,1)S(1)}, bf16[32,1024]{1,0:T(8,128)(2,1)S(1)}, u32[]{:S(2)}, u32[]{:S(2)}) collective-permute-start(bf16[32,1024]{1,0:T(8,128)(2,1)S(1)} %weigh.1.after), channel_id=1, source_target_pairs={{0,2},{1,3},{2,0},{3,1},{4,6},{5,7},{6,4},{7,5},{8,10},{9,11},{10,... | collective-permute-start | bytes 196616 | tf_op jit(solution)/shard_map/ppermute | solution.py:41
  11.7 4.3 %collective-permute-start.2 = (bf16[32,1024]{1,0:T(8,128)(2,1)S(1)}, bf16[32,1024]{1,0:T(8,128)(2,1)S(1)}, u32[]{:S(2)}, u32[]{:S(2)}) collective-permute-start(bf16[32,1024]{1,0:T(8,128)(2,1)S(1)} %weigh.1.after), channel_id=1, source_target_pairs={{0,1},{1,2},{2,3},{3,0},{4,5},{5,6},{6,7},{7,4},{8,9},{9,10},{10,1... | collective-permute-start | bytes 196616 | tf_op jit(solution)/shard_map/ppermute | solution.py:41
  15.9 9.7 %collective-permute-start.3 = (bf16[128,1024]{1,0:T(8,128)(2,1)S(1)}, bf16[128,1024]{1,0:T(8,128)(2,1)S(1)}, u32[]{:S(2)}, u32[]{:S(2)}) collective-permute-start(bf16[128,1024]{1,0:T(8,128)(2,1)S(1)} %pad_maximum_fusion.1), channel_id=1, source_target_pairs={{0,28},{1,29},{2,30},{3,31},{4,0},{5,1},{6,2},{7,3},{8,4},{9,5},{1... | collective-permute-start | bytes 786440 | tf_op jit(solution)/shard_map/ppermute | solution.py:36
  21.2 8.1 %collective-permute-start.5 = (bf16[128,1024]{1,0:T(8,128)(2,1)S(1)}, bf16[128,1024]{1,0:T(8,128)(2,1)S(1)}, u32[]{:S(2)}, u32[]{:S(2)}) collective-permute-start(bf16[128,1024]{1,0:T(8,128)(2,1)S(1)} %pad_maximum_fusion.1), channel_id=1, source_target_pairs={{0,4},{1,5},{2,6},{3,7},{4,8},{5,9},{6,10},{7,11},{8,12},{9,13},{1... | collective-permute-start | bytes 786440 | tf_op jit(solution)/shard_map/ppermute | solution.py:36
  22.3 11.2 %collective-permute-start.9 = (bf16[2,128,896]{2,1,0:T(8,128)(2,1)S(1)}, bf16[2,128,896]{2,1,0:T(8,128)(2,1)S(1)}, u32[]{:S(2)}, u32[]{:S(2)}) collective-permute-start(bf16[2,128,896]{2,1,0:T(8,128)(2,1)S(1)} %pack.1), channel_id=1, source_target_pairs={{0,192},{32,224},{64,0},{96,32},{128,64},{160,96},{192,128},{224,1... | collective-permute-start | bytes 1376264 | tf_op jit(solution)/shard_map/ppermute | solution.py:46
  25.1 12.2 %collective-permute-start.11 = (bf16[2,128,896]{2,1,0:T(8,128)(2,1)S(1)}, bf16[2,128,896]{2,1,0:T(8,128)(2,1)S(1)}, u32[]{:S(2)}, u32[]{:S(2)}) collective-permute-start(bf16[2,128,896]{2,1,0:T(8,128)(2,1)S(1)} %pack.1), channel_id=1, source_target_pairs={{0,64},{32,96},{64,128},{96,160},{128,192},{160,224},{192,0},{224,... | collective-permute-start | bytes 1376264 | tf_op jit(solution)/shard_map/ppermute | solution.py:46
  25.7 11.8 %collective-permute-start.4 = (bf16[128,1024]{1,0:T(8,128)(2,1)S(1)}, bf16[128,1024]{1,0:T(8,128)(2,1)S(1)}, u32[]{:S(2)}, u32[]{:S(2)}) collective-permute-start(bf16[128,1024]{1,0:T(8,128)(2,1)S(1)} %collective-permute-done.3), channel_id=1, source_target_pairs={{0,28},{1,29},{2,30},{3,31},{4,0},{5,1},{6,2},{7,3},{8,4},{9,5},{1... | collective-permute-start | bytes 786440 | tf_op jit(solution)/shard_map/ppermute | solution.py:36
  29.3 11.1 %collective-permute-start.6 = (bf16[128,1024]{1,0:T(8,128)(2,1)S(1)}, bf16[128,1024]{1,0:T(8,128)(2,1)S(1)}, u32[]{:S(2)}, u32[]{:S(2)}) collective-permute-start(bf16[128,1024]{1,0:T(8,128)(2,1)S(1)} %collective-permute-done.5), channel_id=1, source_target_pairs={{0,4},{1,5},{2,6},{3,7},{4,8},{5,9},{6,10},{7,11},{8,12},{9,13},{1... | collective-permute-start | bytes 786440 | tf_op jit(solution)/shard_map/ppermute | solution.py:36
  33.5 7.3 %collective-permute-start.10 = (bf16[128,896]{1,0:T(8,128)(2,1)S(1)}, bf16[128,896]{1,0:T(8,128)(2,1)S(1)}, u32[]{:S(2)}, u32[]{:S(2)}) collective-permute-start(bf16[128,896]{1,0:T(8,128)(2,1)S(1)} %slice_bitcast_fusion.1), channel_id=1, source_target_pairs={{0,192},{32,224},{64,0},{96,32},{128,64},{160,96},{192,128},{224,1... | collective-permute-start | bytes 688136 | tf_op jit(solution)/shard_map/ppermute | solution.py:46
  37.3 7.3 %collective-permute-start.12 = (bf16[128,896]{1,0:T(8,128)(2,1)S(1)}, bf16[128,896]{1,0:T(8,128)(2,1)S(1)}, u32[]{:S(2)}, u32[]{:S(2)}) collective-permute-start(bf16[128,896]{1,0:T(8,128)(2,1)S(1)} %slice_bitcast_fusion), channel_id=1, source_target_pairs={{0,64},{32,96},{64,128},{96,160},{128,192},{160,224},{192,0},{224,... | collective-permute-start | bytes 688136 | tf_op jit(solution)/shard_map/ppermute | solution.py:46
  37.4 7.7 %collective-permute-start.7 = (bf16[128,1024]{1,0:T(8,128)(2,1)S(1)}, bf16[128,1024]{1,0:T(8,128)(2,1)S(1)}, u32[]{:S(2)}, u32[]{:S(2)}) collective-permute-start(bf16[128,1024]{1,0:T(8,128)(2,1)S(1)} %collective-permute-done.4), channel_id=1, source_target_pairs={{0,28},{1,29},{2,30},{3,31},{4,0},{5,1},{6,2},{7,3},{8,4},{9,5},{1... | collective-permute-start | bytes 786440 | tf_op jit(solution)/shard_map/ppermute | solution.py:36
  40.5 8.0 %collective-permute-start.8 = (bf16[128,1024]{1,0:T(8,128)(2,1)S(1)}, bf16[128,1024]{1,0:T(8,128)(2,1)S(1)}, u32[]{:S(2)}, u32[]{:S(2)}) collective-permute-start(bf16[128,1024]{1,0:T(8,128)(2,1)S(1)} %collective-permute-done.6), channel_id=1, source_target_pairs={{0,4},{1,5},{2,6},{3,7},{4,8},{5,9},{6,10},{7,11},{8,12},{9,13},{1... | collective-permute-start | bytes 786440 | tf_op jit(solution)/shard_map/ppermute | solution.py:36
  45.0 10.4 %copy-start.2 = (bf16[896,1024]{1,0:T(8,128)(2,1)S(1)}, bf16[896,1024]{1,0:T(8,128)(2,1)}, u32[]{:S(2)}) copy-start(bf16[896,1024]{1,0:T(8,128)(2,1)} %w.3) | copy-start | bytes 5505028
  45.0 19.3 %collective-permute-start.19 = (bf16[4,2,128,896]{3,2,1,0:T(8,128)(2,1)S(1)}, bf16[4,2,128,896]{3,2,1,0:T(8,128)(2,1)S(1)}, u32[]{:S(2)}, u32[]{:S(2)}) collective-permute-start(bf16[4,2,128,896]{3,2,1,0:T(8,128)(2,1)S(1)} %pad_maximum_fusion.mine), channel_id=1, source_target_pairs={{0,32},{32,0},{64,96},{96,64},{128,160},{160,128},{192,224},{224,1... | collective-permute-start | bytes 5505032 | tf_op jit(solution)/shard_map/ppermute | solution.py:50
  48.5 5.3 %collective-permute-start.13 = (bf16[64,1024]{1,0:T(8,128)(2,1)S(1)}, bf16[64,1024]{1,0:T(8,128)(2,1)S(1)}, u32[]{:S(2)}, u32[]{:S(2)}) collective-permute-start(bf16[64,1024]{1,0:T(8,128)(2,1)S(1)} %get-tuple-element.41), channel_id=1, source_target_pairs={{0,28},{1,29},{2,30},{3,31},{4,0},{5,1},{6,2},{7,3},{8,4},{9,5},{1... | collective-permute-start | bytes 393224 | tf_op jit(solution)/shard_map/ppermute | solution.py:36
  48.6 6.8 %collective-permute-start.14 = (bf16[64,1024]{1,0:T(8,128)(2,1)S(1)}, bf16[64,1024]{1,0:T(8,128)(2,1)S(1)}, u32[]{:S(2)}, u32[]{:S(2)}) collective-permute-start(bf16[64,1024]{1,0:T(8,128)(2,1)S(1)} %get-tuple-element.42), channel_id=1, source_target_pairs={{0,4},{1,5},{2,6},{3,7},{4,8},{5,9},{6,10},{7,11},{8,12},{9,13},{1... | collective-permute-start | bytes 393224 | tf_op jit(solution)/shard_map/ppermute | solution.py:36
  57.2 2.6 %collective-permute-start.15 = (bf16[4,128,896]{2,1,0:T(8,128)(2,1)S(1)}, bf16[4,128,896]{2,1,0:T(8,128)(2,1)S(1)}, u32[]{:S(2)}, u32[]{:S(2)}) collective-permute-start(bf16[4,128,896]{2,1,0:T(8,128)(2,1)S(1)} %first.3.after), channel_id=1, source_target_pairs={{0,32},{32,0},{64,96},{96,64},{128,160},{160,128},{192,224},{224,1... | collective-permute-start | bytes 2752520 | tf_op jit(solution)/shard_map/ppermute | solution.py:50
  59.9 8.9 %collective-permute-start.16 = (bf16[128,896]{1,0:T(8,128)(2,1)S(1)}, bf16[128,896]{1,0:T(8,128)(2,1)S(1)}, u32[]{:S(2)}, u32[]{:S(2)}) collective-permute-start(bf16[128,896]{1,0:T(8,128)(2,1)S(1)} %get-tuple-element.44), channel_id=1, source_target_pairs={{0,64},{32,96},{64,128},{96,160},{128,192},{160,224},{192,0},{224,... | collective-permute-start | bytes 688136 | tf_op jit(solution)/shard_map/ppermute | solution.py:46
  60.0 14.8 %collective-permute-start.17 = (bf16[128,896]{1,0:T(8,128)(2,1)S(1)}, bf16[128,896]{1,0:T(8,128)(2,1)S(1)}, u32[]{:S(2)}, u32[]{:S(2)}) collective-permute-start(bf16[128,896]{1,0:T(8,128)(2,1)S(1)} %get-tuple-element.45), channel_id=1, source_target_pairs={{0,128},{32,160},{64,192},{96,224},{128,0},{160,32},{192,64},{224,... | collective-permute-start | bytes 688136 | tf_op jit(solution)/shard_map/ppermute | solution.py:46
  64.2 10.5 %collective-permute-start.18 = (bf16[128,896]{1,0:T(8,128)(2,1)S(1)}, bf16[128,896]{1,0:T(8,128)(2,1)S(1)}, u32[]{:S(2)}, u32[]{:S(2)}) collective-permute-start(bf16[128,896]{1,0:T(8,128)(2,1)S(1)} %get-tuple-element.46), channel_id=1, source_target_pairs={{0,192},{32,224},{64,0},{96,32},{128,64},{160,96},{192,128},{224,1... | collective-permute-start | bytes 688136 | tf_op jit(solution)/shard_map/ppermute | solution.py:46
  74.9 12.3 %collective-permute-start.20 = (bf16[128,896]{1,0:T(8,128)(2,1)S(1)}, bf16[128,896]{1,0:T(8,128)(2,1)S(1)}, u32[]{:S(2)}, u32[]{:S(2)}) collective-permute-start(bf16[128,896]{1,0:T(8,128)(2,1)S(1)} %total.2.refs_3_.a), channel_id=1, source_target_pairs={{0,192},{32,224},{64,0},{96,32},{128,64},{160,96},{192,128},{224,1... | collective-permute-start | bytes 688136 | tf_op jit(solution)/shard_map/ppermute | solution.py:46
  77.2 10.0 %collective-permute-start.21 = (bf16[128,896]{1,0:T(8,128)(2,1)S(1)}, bf16[128,896]{1,0:T(8,128)(2,1)S(1)}, u32[]{:S(2)}, u32[]{:S(2)}) collective-permute-start(bf16[128,896]{1,0:T(8,128)(2,1)S(1)} %total.2.refs_3_.a), channel_id=1, source_target_pairs={{0,128},{32,160},{64,192},{96,224},{128,0},{160,32},{192,64},{224,... | collective-permute-start | bytes 688136 | tf_op jit(solution)/shard_map/ppermute | solution.py:46
  77.4 13.2 %collective-permute-start.22 = (bf16[128,896]{1,0:T(8,128)(2,1)S(1)}, bf16[128,896]{1,0:T(8,128)(2,1)S(1)}, u32[]{:S(2)}, u32[]{:S(2)}) collective-permute-start(bf16[128,896]{1,0:T(8,128)(2,1)S(1)} %total.2.refs_3_.a), channel_id=1, source_target_pairs={{0,64},{32,96},{64,128},{96,160},{128,192},{160,224},{192,0},{224,... | collective-permute-start | bytes 688136 | tf_op jit(solution)/shard_map/ppermute | solution.py:46
  78.1 15.1 %copy-start.1 = (bf16[1024,896]{1,0:T(8,128)(2,1)S(1)}, bf16[1024,896]{1,0:T(8,128)(2,1)}, u32[]{:S(2)}) copy-start(bf16[1024,896]{1,0:T(8,128)(2,1)} %uw.5) | copy-start | bytes 5505028
  81.3 11.9 %copy-start = (bf16[1024,896]{1,0:T(8,128)(2,1)S(1)}, bf16[1024,896]{1,0:T(8,128)(2,1)}, u32[]{:S(2)}) copy-start(bf16[1024,896]{1,0:T(8,128)(2,1)} %gw.5) | copy-start | bytes 5505028
  90.6 2.6 %collective-permute-start.23 = (bf16[4,128,896]{2,1,0:T(8,128)(2,1)S(1)}, bf16[4,128,896]{2,1,0:T(8,128)(2,1)S(1)}, u32[]{:S(2)}, u32[]{:S(2)}) collective-permute-start(bf16[4,128,896]{2,1,0:T(8,128)(2,1)S(1)} %join.1.mine), channel_id=1, source_target_pairs={{0,32},{32,0},{64,96},{96,64},{128,160},{160,128},{192,224},{224,1... | collective-permute-start | bytes 2752520 | tf_op jit(solution)/shard_map/ppermute | solution.py:50
  95.6 7.2 %collective-permute-start.24 = (bf16[64,1024]{1,0:T(8,128)(2,1)S(1)}, bf16[64,1024]{1,0:T(8,128)(2,1)S(1)}, u32[]{:S(2)}, u32[]{:S(2)}) collective-permute-start(bf16[64,1024]{1,0:T(8,128)(2,1)S(1)} %get-tuple-element.79), channel_id=1, source_target_pairs={{0,4},{1,5},{2,6},{3,7},{4,8},{5,9},{6,10},{7,11},{8,12},{9,13},{1... | collective-permute-start | bytes 393224 | tf_op jit(solution)/shard_map/ppermute | solution.py:36
  96.2 6.6 %collective-permute-start.25 = (bf16[64,1024]{1,0:T(8,128)(2,1)S(1)}, bf16[64,1024]{1,0:T(8,128)(2,1)S(1)}, u32[]{:S(2)}, u32[]{:S(2)}) collective-permute-start(bf16[64,1024]{1,0:T(8,128)(2,1)S(1)} %get-tuple-element.78), channel_id=1, source_target_pairs={{0,28},{1,29},{2,30},{3,31},{4,0},{5,1},{6,2},{7,3},{8,4},{9,5},{1... | collective-permute-start | bytes 393224 | tf_op jit(solution)/shard_map/ppermute | solution.py:36
  102.9 10.8 %collective-permute-start.26 = (bf16[128,1024]{1,0:T(8,128)(2,1)S(1)}, bf16[128,1024]{1,0:T(8,128)(2,1)S(1)}, u32[]{:S(2)}, u32[]{:S(2)}) collective-permute-start(bf16[128,1024]{1,0:T(8,128)(2,1)S(1)} %get-tuple-element.54.after), channel_id=1, source_target_pairs={{0,4},{1,5},{2,6},{3,7},{4,8},{5,9},{6,10},{7,11},{8,12},{9,13},{1... | collective-permute-start | bytes 786440 | tf_op jit(solution)/shard_map/ppermute | solution.py:36
  103.0 10.7 %collective-permute-start.27 = (bf16[128,1024]{1,0:T(8,128)(2,1)S(1)}, bf16[128,1024]{1,0:T(8,128)(2,1)S(1)}, u32[]{:S(2)}, u32[]{:S(2)}) collective-permute-start(bf16[128,1024]{1,0:T(8,128)(2,1)S(1)} %get-tuple-element.56), channel_id=1, source_target_pairs={{0,28},{1,29},{2,30},{3,31},{4,0},{5,1},{6,2},{7,3},{8,4},{9,5},{1... | collective-permute-start | bytes 786440 | tf_op jit(solution)/shard_map/ppermute | solution.py:36
  109.9 1.6 %copy-start.3 = (bf16[1024,1024]{1,0:T(8,128)(2,1)S(1)}, bf16[1024,1024]{1,0:T(8,128)(2,1)}, u32[]{:S(2)}) copy-start(bf16[1024,1024]{1,0:T(8,128)(2,1)} %all-gather.2.cloned.1.call-done.x_in) | copy-start | bytes 6291460
  113.6 3.5 %copy-start.5 = (bf16[640,896]{1,0:T(8,128)(2,1)S(1)}, bf16[640,896]{1,0:T(8,128)(2,1)}, u32[]{:S(2)}) copy-start(bf16[640,896]{1,0:T(8,128)(2,1)} %get-tuple-element.61.refs_0_) | copy-start | bytes 3440644
  113.6 3.5 %copy-start.7 = (bf16[256,896]{1,0:T(8,128)(2,1)S(1)}, bf16[256,896]{1,0:T(8,128)(2,1)}, u32[]{:S(2)}) copy-start(bf16[256,896]{1,0:T(8,128)(2,1)} %get-tuple-element.62.refs_1_) | copy-start | bytes 1376260
  113.6 3.5 %copy-start.9 = (bf16[128,896]{1,0:T(8,128)(2,1)S(1)}, bf16[128,896]{1,0:T(8,128)(2,1)}, u32[]{:S(2)}) copy-start(bf16[128,896]{1,0:T(8,128)(2,1)} %get-tuple-element.63.refs_2_) | copy-start | bytes 688132
  113.8 8.4 %collective-permute-start.28 = (bf16[128,1024]{1,0:T(8,128)(2,1)S(1)}, bf16[128,1024]{1,0:T(8,128)(2,1)S(1)}, u32[]{:S(2)}, u32[]{:S(2)}) collective-permute-start(bf16[128,1024]{1,0:T(8,128)(2,1)S(1)} %get-tuple-element.58), channel_id=1, source_target_pairs={{0,4},{1,5},{2,6},{3,7},{4,8},{5,9},{6,10},{7,11},{8,12},{9,13},{1... | collective-permute-start | bytes 786440 | tf_op jit(solution)/shard_map/ppermute | solution.py:36
  113.9 8.3 %collective-permute-start.29 = (bf16[128,1024]{1,0:T(8,128)(2,1)S(1)}, bf16[128,1024]{1,0:T(8,128)(2,1)S(1)}, u32[]{:S(2)}, u32[]{:S(2)}) collective-permute-start(bf16[128,1024]{1,0:T(8,128)(2,1)S(1)} %get-tuple-element.59), channel_id=1, source_target_pairs={{0,28},{1,29},{2,30},{3,31},{4,0},{5,1},{6,2},{7,3},{8,4},{9,5},{1... | collective-permute-start | bytes 786440 | tf_op jit(solution)/shard_map/ppermute | solution.py:36
  120.6 5.1 %copy-start.4 = (bf16[640,896]{1,0:T(8,128)(2,1)S(1)}, bf16[640,896]{1,0:T(8,128)(2,1)}, u32[]{:S(2)}) copy-start(bf16[640,896]{1,0:T(8,128)(2,1)} %get-tuple-element.67.refs_0_) | copy-start | bytes 3440644
  120.6 5.1 %copy-start.6 = (bf16[256,896]{1,0:T(8,128)(2,1)S(1)}, bf16[256,896]{1,0:T(8,128)(2,1)}, u32[]{:S(2)}) copy-start(bf16[256,896]{1,0:T(8,128)(2,1)} %get-tuple-element.68.refs_1_) | copy-start | bytes 1376260
  120.6 5.1 %copy-start.8 = (bf16[128,896]{1,0:T(8,128)(2,1)S(1)}, bf16[128,896]{1,0:T(8,128)(2,1)}, u32[]{:S(2)}) copy-start(bf16[128,896]{1,0:T(8,128)(2,1)} %get-tuple-element.69.refs_2_) | copy-start | bytes 688132
  122.3 7.7 %collective-permute-start.30 = (bf16[128,1024]{1,0:T(8,128)(2,1)S(1)}, bf16[128,1024]{1,0:T(8,128)(2,1)S(1)}, u32[]{:S(2)}, u32[]{:S(2)}) collective-permute-start(bf16[128,1024]{1,0:T(8,128)(2,1)S(1)} %get-tuple-element.65), channel_id=1, source_target_pairs={{0,4},{1,5},{2,6},{3,7},{4,8},{5,9},{6,10},{7,11},{8,12},{9,13},{1... | collective-permute-start | bytes 786440 | tf_op jit(solution)/shard_map/ppermute | solution.py:36
  122.4 7.6 %collective-permute-start.31 = (bf16[128,1024]{1,0:T(8,128)(2,1)S(1)}, bf16[128,1024]{1,0:T(8,128)(2,1)S(1)}, u32[]{:S(2)}, u32[]{:S(2)}) collective-permute-start(bf16[128,1024]{1,0:T(8,128)(2,1)S(1)} %get-tuple-element.66), channel_id=1, source_target_pairs={{0,28},{1,29},{2,30},{3,31},{4,0},{5,1},{6,2},{7,3},{8,4},{9,5},{1... | collective-permute-start | bytes 786440 | tf_op jit(solution)/shard_map/ppermute | solution.py:36
  130.1 5.1 %collective-permute-start.32 = (bf16[32,1024]{1,0:T(8,128)(2,1)S(1)}, bf16[32,1024]{1,0:T(8,128)(2,1)S(1)}, u32[]{:S(2)}, u32[]{:S(2)}) collective-permute-start(bf16[32,1024]{1,0:T(8,128)(2,1)S(1)} %get-tuple-element.72), channel_id=1, source_target_pairs={{0,1},{1,2},{2,3},{3,0},{4,5},{5,6},{6,7},{7,4},{8,9},{9,10},{10,1... | collective-permute-start | bytes 196616 | tf_op jit(solution)/shard_map/ppermute | solution.py:41
  132.7 5.8 %collective-permute-start.33 = (bf16[32,1024]{1,0:T(8,128)(2,1)S(1)}, bf16[32,1024]{1,0:T(8,128)(2,1)S(1)}, u32[]{:S(2)}, u32[]{:S(2)}) collective-permute-start(bf16[32,1024]{1,0:T(8,128)(2,1)S(1)} %get-tuple-element.73), channel_id=1, source_target_pairs={{0,2},{1,3},{2,0},{3,1},{4,6},{5,7},{6,4},{7,5},{8,10},{9,11},{10,... | collective-permute-start | bytes 196616 | tf_op jit(solution)/shard_map/ppermute | solution.py:41
  133.8 5.5 %collective-permute-start.34 = (bf16[32,1024]{1,0:T(8,128)(2,1)S(1)}, bf16[32,1024]{1,0:T(8,128)(2,1)S(1)}, u32[]{:S(2)}, u32[]{:S(2)}) collective-permute-start(bf16[32,1024]{1,0:T(8,128)(2,1)S(1)} %get-tuple-element.74), channel_id=1, source_target_pairs={{0,3},{1,0},{2,1},{3,2},{4,7},{5,4},{6,5},{7,6},{8,11},{9,8},{10,9... | collective-permute-start | bytes 196616 | tf_op jit(solution)/shard_map/ppermute | solution.py:41
Sparse Core Ops, SparseCore 0:
  25.3 76.8 all-gather.1

commit v5 on v4

--- a/solution.py
+++ b/solution.py
@@ -429,13 +429,6 @@
     )(p, up, down, after)
 
 
-def scatter_z_y(p, up, down, marks):
-    for mark, i, j in ((marks[0], 2, 3), (marks[1], 1, 4)):
-        up, down = step(step_kernel, p, i, j, from_z(up, -1), from_z(down, 1), mark)
-    own, *sent = own_of(p, from_z(up, -1), from_z(down, 1), marks[2])
-    return total_of(own, [from_y(v, -k) for k, v in enumerate(sent, 1)])
-
-
 def on_device(
     inputs,
     cotangent,
@@ -484,10 +477,13 @@
     near = second(*args, 0, 5, ends[0])
     d_gate, d_up, _ = zip(near, middle, far)
 
-    x_t, mark_1 = turn(place, x_all, near[2])
-    grad_gate, mark_2 = product(x_t, d_gate, 512, mark_1)
-    grad_up, mark_3 = product(x_t, d_up, 512, mark_2)
-    grad_input = scatter_z_y(near[2], *ends, (mark_1, mark_2, mark_3))
+    ends = step(step_kernel, near[2], 2, 3, from_z(ends[0], -1), from_z(ends[1], 1))
+    x_t, mark = turn(place, x_all, ends[0])
+    ends = step(step_kernel, near[2], 1, 4, from_z(ends[0], -1), from_z(ends[1], 1), mark)
+    grad_gate, mark = product(x_t, d_gate, 512, ends[0])
+    own, *sent = own_of(near[2], from_z(ends[0], -1), from_z(ends[1], 1), mark)
+    grad_up, mark = product(x_t, d_up, 512, sent[0])
+    grad_input = total_of(own, [from_y(v, -k) for k, v in enumerate(sent, 1)], mark)
     return (grad_input, grad_gate, grad_up, grad_down)
 
 

time: 147 us -> 145 us (0.986)
  waiting for transfers between devices: 48.9 us -> 46.7 us
    ppermute x6, waiting for transfers between devices: 9.29 us -> 5.8 us  [from_y(): return lax.ppermute(v, 'col', perm)]
  transfers between devices with their start and end apart: 36 -> 36, of which waited for: 23 -> 23; matrix products, arithmetic and copies ran while one was open for 0% -> 0% of each run, Pallas kernels for 20% -> 21%
where the time goes in v5:
time: 145 us
  starting transfers between devices  49.8 us (34%)
  waiting for transfers between devices  46.7 us (32%)
  Pallas kernels  31.6 us (22%)
  between operations  14.4 us (10%)
  local copies, waits for them, and re-layouts  1.89 us (1%)
    ppermute x16, starting transfers between devices, from_z(): return lax.ppermute(v, 'col', perm)  27.4 us
    ppermute x10, waiting for transfers between devices, from_x(): return lax.ppermute(v, 'row', perm)  24.2 us
    ppermute x10, starting transfers between devices, from_x(): return lax.ppermute(v, 'row', perm)  14.3 us
    ppermute x16, waiting for transfers between devices, from_z(): return lax.ppermute(v, 'col', perm)  13.7 us
    pallas_call x3, Pallas kernels, product(): pl.pallas_call(functools.partial(product_kernel, len(parts)), grid=(m //...  10.1 us
    pallas_call x3, Pallas kernels, second(): pl.pallas_call(second_kernel, grid_spec=pltpu.PrefetchScalarGridSpec(num_...  8.56 us
    ppermute x6, starting transfers between devices, from_y(): return lax.ppermute(v, 'col', perm)  7.78 us
    ppermute x6, waiting for transfers between devices, from_y(): return lax.ppermute(v, 'col', perm)  5.8 us
  transfers between devices with their start and end apart: 36, of which 23 were waited for; matrix products, arithmetic and copies ran while one was open for 0% of the time, Pallas kernels for 21%

profile of v5, /device:TPU:24, one launch (start us, length us, event | category | flops | bytes accessed | tf_op | source)
XLA Modules:
  0.0 144.8 jit_solution(16598325824081982112)
XLA Ops:
  7.2 0.9 weigh.1.after
  8.2 0.8 collective-permute-start
  9.0 2.7 %collective-permute-start.1 = (bf16[32,1024]{1,0:T(8,128)(2,1)S(1)}, bf16[32,1024]{1,0:T(8,128)(2,1)S(1)}, u32[]{:S(2)}, u32[]{:S(2)}) collective-permute-start(bf16[32,1024]{1,0:T(8,128)(2,1)S(1)} %weigh.1.after), channel_id=1, source_target_pairs={{0,2},{1,3},{2,0},{3,1},{4,6},{5,7},{6,4},{7,5},{8,10},{9,11},{10,... | collective-permute-start | bytes 196616 | tf_op jit(solution)/shard_map/ppermute | solution.py:41
  12.1 1.9 %collective-permute-done = bf16[32,1024]{1,0:T(8,128)(2,1)S(1)} collective-permute-done((bf16[32,1024]{1,0:T(8,128)(2,1)S(1)}, bf16[32,1024]{1,0:T(8,128)(2,1)S(1)}, u32[]{:S(2)}, u32[]{:S(2)}) %collective-permute-start) | collective-permute-done | bytes 65568 | tf_op jit(solution)/shard_map/ppermute | solution.py:41
  14.7 1.2 collective-permute-done.2
  15.9 5.3 %collective-permute-start.3 = (bf16[128,1024]{1,0:T(8,128)(2,1)S(1)}, bf16[128,1024]{1,0:T(8,128)(2,1)S(1)}, u32[]{:S(2)}, u32[]{:S(2)}) collective-permute-start(bf16[128,1024]{1,0:T(8,128)(2,1)S(1)} %pad_maximum_fusion.1), channel_id=1, source_target_pairs={{0,28},{1,29},{2,30},{3,31},{4,0},{5,1},{6,2},{7,3},{8,4},{9,5},{1... | collective-permute-start | bytes 786440 | tf_op jit(solution)/shard_map/ppermute | solution.py:36
  21.2 1.1 pack.1
  22.3 2.8 %collective-permute-start.9 = (bf16[2,128,896]{2,1,0:T(8,128)(2,1)S(1)}, bf16[2,128,896]{2,1,0:T(8,128)(2,1)S(1)}, u32[]{:S(2)}, u32[]{:S(2)}) collective-permute-start(bf16[2,128,896]{2,1,0:T(8,128)(2,1)S(1)} %pack.1), channel_id=1, source_target_pairs={{0,192},{32,224},{64,0},{96,32},{128,64},{160,96},{192,128},{224,1... | collective-permute-start | bytes 1376264 | tf_op jit(solution)/shard_map/ppermute | solution.py:46
  25.7 3.7 %collective-permute-start.4 = (bf16[128,1024]{1,0:T(8,128)(2,1)S(1)}, bf16[128,1024]{1,0:T(8,128)(2,1)S(1)}, u32[]{:S(2)}, u32[]{:S(2)}) collective-permute-start(bf16[128,1024]{1,0:T(8,128)(2,1)S(1)} %collective-permute-done.3), channel_id=1, source_target_pairs={{0,28},{1,29},{2,30},{3,31},{4,0},{5,1},{6,2},{7,3},{8,4},{9,5},{1... | collective-permute-start | bytes 786440 | tf_op jit(solution)/shard_map/ppermute | solution.py:36
  29.4 4.1 %collective-permute-done.9 = bf16[2,128,896]{2,1,0:T(8,128)(2,1)S(1)} collective-permute-done((bf16[2,128,896]{2,1,0:T(8,128)(2,1)S(1)}, bf16[2,128,896]{2,1,0:T(8,128)(2,1)S(1)}, u32[]{:S(2)}, u32[]{:S(2)}) %collective-permute-start.9) | collective-permute-done | bytes 458784 | tf_op jit(solution)/shard_map/ppermute | solution.py:46
  33.5 3.8 %collective-permute-start.10 = (bf16[128,896]{1,0:T(8,128)(2,1)S(1)}, bf16[128,896]{1,0:T(8,128)(2,1)S(1)}, u32[]{:S(2)}, u32[]{:S(2)}) collective-permute-start(bf16[128,896]{1,0:T(8,128)(2,1)S(1)} %slice_bitcast_fusion.1), channel_id=1, source_target_pairs={{0,192},{32,224},{64,0},{96,32},{128,64},{160,96},{192,128},{224,1... | collective-permute-start | bytes 688136 | tf_op jit(solution)/shard_map/ppermute | solution.py:46
  37.4 3.0 %collective-permute-start.7 = (bf16[128,1024]{1,0:T(8,128)(2,1)S(1)}, bf16[128,1024]{1,0:T(8,128)(2,1)S(1)}, u32[]{:S(2)}, u32[]{:S(2)}) collective-permute-start(bf16[128,1024]{1,0:T(8,128)(2,1)S(1)} %collective-permute-done.4), channel_id=1, source_target_pairs={{0,28},{1,29},{2,30},{3,31},{4,0},{5,1},{6,2},{7,3},{8,4},{9,5},{1... | collective-permute-start | bytes 786440 | tf_op jit(solution)/shard_map/ppermute | solution.py:36
  40.8 3.8 %collective-permute-done.12.r2 = bf16[128,896]{1,0:T(8,128)(2,1)S(1)} collective-permute-done((bf16[128,896]{1,0:T(8,128)(2,1)S(1)}, bf16[128,896]{1,0:T(8,128)(2,1)S(1)}, u32[]{:S(2)}, u32[]{:S(2)}) %collective-permute-start.12) | collective-permute-done | bytes 229408 | tf_op jit(solution)/shard_map/ppermute | solution.py:46
  45.1 3.4 %collective-permute-done.8.d = bf16[128,1024]{1,0:T(8,128)(2,1)S(1)} collective-permute-done((bf16[128,1024]{1,0:T(8,128)(2,1)S(1)}, bf16[128,1024]{1,0:T(8,128)(2,1)S(1)}, u32[]{:S(2)}, u32[]{:S(2)}) %collective-permute-start.8) | collective-permute-done | bytes 262176 | tf_op jit(solution)/shard_map/ppermute | solution.py:36
  48.6 2.0 %collective-permute-start.14 = (bf16[64,1024]{1,0:T(8,128)(2,1)S(1)}, bf16[64,1024]{1,0:T(8,128)(2,1)S(1)}, u32[]{:S(2)}, u32[]{:S(2)}) collective-permute-start(bf16[64,1024]{1,0:T(8,128)(2,1)S(1)} %get-tuple-element.42), channel_id=1, source_target_pairs={{0,4},{1,5},{2,6},{3,7},{4,8},{5,9},{6,10},{7,11},{8,12},{9,13},{1... | collective-permute-start | bytes 393224 | tf_op jit(solution)/shard_map/ppermute | solution.py:36
  50.7 3.1 %collective-permute-done.13.low.refs_1_ = bf16[64,1024]{1,0:T(8,128)(2,1)S(1)} collective-permute-done((bf16[64,1024]{1,0:T(8,128)(2,1)S(1)}, bf16[64,1024]{1,0:T(8,128)(2,1)S(1)}, u32[]{:S(2)}, u32[]{:S(2)}) %collective-permute-start.13) | collective-permute-done | bytes 131104 | tf_op jit(solution)/shard_map/ppermute | solution.py:36
  53.8 1.6 %collective-permute-done.14.high.refs_2_ = bf16[64,1024]{1,0:T(8,128)(2,1)S(1)} collective-permute-done((bf16[64,1024]{1,0:T(8,128)(2,1)S(1)}, bf16[64,1024]{1,0:T(8,128)(2,1)S(1)}, u32[]{:S(2)}, u32[]{:S(2)}) %collective-permute-start.14) | collective-permute-done | bytes 131104 | tf_op jit(solution)/shard_map/ppermute | solution.py:36
  55.4 1.8 %first.3.after = bf16[4,128,896]{2,1,0:T(8,128)(2,1)S(1)} custom-call(s32[12]{0:T(128)S(1)} %stack.67.s, bf16[7,128,1024]{2,1,0:T(8,128)(2,1)S(1)} %bitcast_dynamic-update-slice_fusion.dy, bf16[64,1024]{1,0:T(8,128)(2,1)S(1)} %collective-permute-done.13.low.refs_1_, bf16[64,1024]{1,0:T(8,128)(2,1)S(1)} %collective-permute-done.14.high.refs_2_, ...), custom_call_target="tpu_custom_call" | custom-call | flops 939524096 | bytes 5767168 | tf_op jit(solution)/shard_map/first/pallas_call | solution.py:151
  57.3 1.8 %first.2.own = f32[4,128,896]{2,1,0:T(8,128)S(1)} custom-call(s32[12]{0:T(128)S(1)} %stack.67.s, bf16[7,128,1024]{2,1,0:T(8,128)(2,1)S(1)} %bitcast_dynamic-update-slice_fusion.dy, bf16[64,1024]{1,0:T(8,128)(2,1)S(1)} %collective-permute-done.13.low.refs_1_, bf16[64,1024]{1,0:T(8,128)(2,1)S(1)} %collective-permute-done.14.high.refs_2_, ...), custom_call_target="tpu_custom_call" | custom-call | flops 939524096 | bytes 5767168 | tf_op jit(solution)/shard_map/first/pallas_call | solution.py:151
  60.0 4.2 %collective-permute-start.17 = (bf16[128,896]{1,0:T(8,128)(2,1)S(1)}, bf16[128,896]{1,0:T(8,128)(2,1)S(1)}, u32[]{:S(2)}, u32[]{:S(2)}) collective-permute-start(bf16[128,896]{1,0:T(8,128)(2,1)S(1)} %get-tuple-element.45), channel_id=1, source_target_pairs={{0,128},{32,160},{64,192},{96,224},{128,0},{160,32},{192,64},{224,... | collective-permute-start | bytes 688136 | tf_op jit(solution)/shard_map/ppermute | solution.py:46
  64.2 3.7 %prep.1 = (bf16[896,1024]{1,0:T(8,128)(2,1)S(1)}, f32[1024,896]{1,0:T(8,128)S(1)}, f32[1024,896]{1,0:T(8,128)S(1)}, f32[8,128]{1,0:T(8,128)S(1)}) custom-call(s32[12]{0:T(128)S(1)} %stack.67.s, bf16[4,2,128,896]{3,2,1,0:T(8,128)(2,1)S(1)} %pad_maximum_fusion.mine, bf16[4,2,128,896]{3,2,1,0:T(8,128)(2,1)S(1)} %collective-permute-done.19.other, ...), custom_call_target="tpu_custom_call" | custom-call | flops 27525120 | bytes 12845056 | tf_op jit(solution)/shard_map/prep/pallas_call | solution.py:252
  68.0 0.9 collective-permute-done.16.r1
  68.8 5.9 %collective-permute-done.17.r2 = bf16[128,896]{1,0:T(8,128)(2,1)S(1)} collective-permute-done((bf16[128,896]{1,0:T(8,128)(2,1)S(1)}, bf16[128,896]{1,0:T(8,128)(2,1)S(1)}, u32[]{:S(2)}, u32[]{:S(2)}) %collective-permute-start.17) | collective-permute-done | bytes 229408 | tf_op jit(solution)/shard_map/ppermute | solution.py:46
  74.9 2.3 %collective-permute-start.20 = (bf16[128,896]{1,0:T(8,128)(2,1)S(1)}, bf16[128,896]{1,0:T(8,128)(2,1)S(1)}, u32[]{:S(2)}, u32[]{:S(2)}) collective-permute-start(bf16[128,896]{1,0:T(8,128)(2,1)S(1)} %total.2.refs_3_.a), channel_id=1, source_target_pairs={{0,192},{32,224},{64,0},{96,32},{128,64},{160,96},{192,128},{224,1... | collective-permute-start | bytes 688136 | tf_op jit(solution)/shard_map/ppermute | solution.py:46
  77.4 0.8 collective-permute-start.22
  78.1 3.2 %product.3 = (bf16[896,1024]{1,0:T(8,128)(2,1)}, f32[8,128]{1,0:T(8,128)S(1)}) custom-call(bf16[896,1024]{1,0:T(8,128)(2,1)S(1)} %get-tuple-element.48.a, bf16[896,1024]{1,0:T(8,128)(2,1)S(1)} %bitcast.30, bf16[64,1024]{1,0:T(8,128)(2,1)S(1)} %collective-permute-done.13.low.refs_1_, bf16[64,1024]{1,0:T(8,128)(2,1)S(1)} %collective-permute-done.14.high.refs_2_, ...), custom_call_target="tpu_custom_call" | custom-call | flops 1879048192 | bytes 5767168 | tf_op jit(solution)/shard_map/product/pallas_call | solution.py:358
  81.3 5.8 %collective-permute-done.20.b = bf16[128,896]{1,0:T(8,128)(2,1)S(1)} collective-permute-done((bf16[128,896]{1,0:T(8,128)(2,1)S(1)}, bf16[128,896]{1,0:T(8,128)(2,1)S(1)}, u32[]{:S(2)}, u32[]{:S(2)}) %collective-permute-start.20) | collective-permute-done | bytes 229408 | tf_op jit(solution)/shard_map/ppermute | solution.py:46
  87.2 3.4 %collective-permute-done.22.d = bf16[128,896]{1,0:T(8,128)(2,1)S(1)} collective-permute-done((bf16[128,896]{1,0:T(8,128)(2,1)S(1)}, bf16[128,896]{1,0:T(8,128)(2,1)S(1)}, u32[]{:S(2)}, u32[]{:S(2)}) %collective-permute-start.22) | collective-permute-done | bytes 229408 | tf_op jit(solution)/shard_map/ppermute | solution.py:46
  90.7 2.5 %collective-permute-done.23.other = bf16[4,128,896]{2,1,0:T(8,128)(2,1)S(1)} collective-permute-done((bf16[4,128,896]{2,1,0:T(8,128)(2,1)S(1)}, bf16[4,128,896]{2,1,0:T(8,128)(2,1)S(1)}, u32[]{:S(2)}, u32[]{:S(2)}) %collective-permute-start.23) | collective-permute-done | bytes 917536 | tf_op jit(solution)/shard_map/ppermute | solution.py:50
  93.2 2.4 %second.3 = (bf16[128,896]{1,0:T(8,128)(2,1)}, bf16[128,896]{1,0:T(8,128)(2,1)}, bf16[128,1024]{1,0:T(8,128)(2,1)S(1)}) custom-call(s32[12]{0:T(128)S(1)} %stack.67.s, bf16[4,128,896]{2,1,0:T(8,128)(2,1)S(1)} %join.1.mine, bf16[4,128,896]{2,1,0:T(8,128)(2,1)S(1)} %collective-permute-done.23.other, f32[1024,896]{1,0:T(8,128)S(1)} %get-tuple-element.50.a, ...), custom_call_target="tpu_custom_call" | custom-call | flops 469762048 | bytes 5505024 | tf_op jit(solution)/shard_map/second/pallas_call | solution.py:329
  96.2 2.8 %collective-permute-start.25 = (bf16[64,1024]{1,0:T(8,128)(2,1)S(1)}, bf16[64,1024]{1,0:T(8,128)(2,1)S(1)}, u32[]{:S(2)}, u32[]{:S(2)}) collective-permute-start(bf16[64,1024]{1,0:T(8,128)(2,1)S(1)} %get-tuple-element.78), channel_id=1, source_target_pairs={{0,28},{1,29},{2,30},{3,31},{4,0},{5,1},{6,2},{7,3},{8,4},{9,5},{1... | collective-permute-start | bytes 393224 | tf_op jit(solution)/shard_map/ppermute | solution.py:36
  98.9 2.5 %second.4 = (bf16[256,896]{1,0:T(8,128)(2,1)}, bf16[256,896]{1,0:T(8,128)(2,1)}, bf16[256,1024]{1,0:T(8,128)(2,1)S(1)}) custom-call(s32[12]{0:T(128)S(1)} %stack.67.s, bf16[4,128,896]{2,1,0:T(8,128)(2,1)S(1)} %join.1.mine, bf16[4,128,896]{2,1,0:T(8,128)(2,1)S(1)} %collective-permute-done.23.other, f32[1024,896]{1,0:T(8,128)S(1)} %get-tuple-element.50.a, ...), custom_call_target="tpu_custom_call" | custom-call | flops 939524096 | bytes 7340032 | tf_op jit(solution)/shard_map/second/pallas_call | solution.py:329
  101.4 1.4 collective-permute-done.24.up
  103.0 3.2 %collective-permute-start.27 = (bf16[128,1024]{1,0:T(8,128)(2,1)S(1)}, bf16[128,1024]{1,0:T(8,128)(2,1)S(1)}, u32[]{:S(2)}, u32[]{:S(2)}) collective-permute-start(bf16[128,1024]{1,0:T(8,128)(2,1)S(1)} %get-tuple-element.56), channel_id=1, source_target_pairs={{0,28},{1,29},{2,30},{3,31},{4,0},{5,1},{6,2},{7,3},{8,4},{9,5},{1... | collective-permute-start | bytes 786440 | tf_op jit(solution)/shard_map/ppermute | solution.py:36
  106.2 3.7 %second.5 = (bf16[640,896]{1,0:T(8,128)(2,1)}, bf16[640,896]{1,0:T(8,128)(2,1)}, bf16[640,1024]{1,0:T(8,128)(2,1)S(1)}) custom-call(s32[12]{0:T(128)S(1)} %stack.67.s, bf16[4,128,896]{2,1,0:T(8,128)(2,1)S(1)} %join.1.mine, bf16[4,128,896]{2,1,0:T(8,128)(2,1)S(1)} %collective-permute-done.23.other, f32[1024,896]{1,0:T(8,128)S(1)} %get-tuple-element.50.a, ...), custom_call_target="tpu_custom_call" | custom-call | flops 2348810240 | bytes 12845056 | tf_op jit(solution)/shard_map/second/pallas_call | solution.py:329
  109.9 2.0 %collective-permute-done.26.up = bf16[128,1024]{1,0:T(8,128)(2,1)S(1)} collective-permute-done((bf16[128,1024]{1,0:T(8,128)(2,1)S(1)}, bf16[128,1024]{1,0:T(8,128)(2,1)S(1)}, u32[]{:S(2)}, u32[]{:S(2)}) %collective-permute-start.26) | collective-permute-done | bytes 262176 | tf_op jit(solution)/shard_map/ppermute | solution.py:36
  112.1 3.2 %collective-permute-start.29 = (bf16[128,1024]{1,0:T(8,128)(2,1)S(1)}, bf16[128,1024]{1,0:T(8,128)(2,1)S(1)}, u32[]{:S(2)}, u32[]{:S(2)}) collective-permute-start(bf16[128,1024]{1,0:T(8,128)(2,1)S(1)} %get-tuple-element.58), channel_id=1, source_target_pairs={{0,28},{1,29},{2,30},{3,31},{4,0},{5,1},{6,2},{7,3},{8,4},{9,5},{1... | collective-permute-start | bytes 786440 | tf_op jit(solution)/shard_map/ppermute | solution.py:36
  115.3 1.6 %copy-done.3 = bf16[1024,1024]{1,0:T(8,128)(2,1)S(1)} copy-done((bf16[1024,1024]{1,0:T(8,128)(2,1)S(1)}, bf16[1024,1024]{1,0:T(8,128)(2,1)}, u32[]{:S(2)}) %copy-start.3) | copy-done | bytes 2097176
  116.9 2.1 %turn.1 = (bf16[1024,1024]{1,0:T(8,128)(2,1)S(1)}, f32[8,128]{1,0:T(8,128)S(1)}) custom-call(s32[12]{0:T(128)S(1)} %stack.67.s, bf16[1024,1024]{1,0:T(8,128)(2,1)S(1)} %copy-done.3, bf16[128,1024]{1,0:T(8,128)(2,1)S(1)} %get-tuple-element.57.after), custom_call_target="tpu_custom_call" | custom-call | bytes 4194304 | tf_op jit(solution)/shard_map/turn/pallas_call | solution.py:285
  119.1 1.0 collective-permute-done.28.up
  120.7 2.8 %collective-permute-start.31 = (bf16[128,1024]{1,0:T(8,128)(2,1)S(1)}, bf16[128,1024]{1,0:T(8,128)(2,1)S(1)}, u32[]{:S(2)}, u32[]{:S(2)}) collective-permute-start(bf16[128,1024]{1,0:T(8,128)(2,1)S(1)} %get-tuple-element.61), channel_id=1, source_target_pairs={{0,28},{1,29},{2,30},{3,31},{4,0},{5,1},{6,2},{7,3},{8,4},{9,5},{1... | collective-permute-start | bytes 786440 | tf_op jit(solution)/shard_map/ppermute | solution.py:36
  123.5 3.5 %product.4 = (bf16[1024,896]{1,0:T(8,128)(2,1)}, f32[8,128]{1,0:T(8,128)S(1)}) custom-call(bf16[1024,1024]{1,0:T(8,128)(2,1)S(1)} %get-tuple-element.62.a, bf16[640,896]{1,0:T(8,128)(2,1)S(1)} %copy-done.5, bf16[256,896]{1,0:T(8,128)(2,1)S(1)} %copy-done.7, bf16[128,896]{1,0:T(8,128)(2,1)S(1)} %copy-done.9, bf16[128,1024]{1,0:T(8,128)(2,1)S(1)} %get-tuple-element.60.refs_3_), custom_call_target="tpu_custom_call" | custom-call | flops 1879048192 | bytes 5767168 | tf_op jit(solution)/shard_map/product/pallas_call | solution.py:358
  127.0 0.9 collective-permute-done.30.up
  128.0 2.6 %collective-permute-start.32 = (bf16[32,1024]{1,0:T(8,128)(2,1)S(1)}, bf16[32,1024]{1,0:T(8,128)(2,1)S(1)}, u32[]{:S(2)}, u32[]{:S(2)}) collective-permute-start(bf16[32,1024]{1,0:T(8,128)(2,1)S(1)} %get-tuple-element.68.refs_3_), channel_id=1, source_target_pairs={{0,1},{1,2},{2,3},{3,0},{4,5},{5,6},{6,7},{7,4},{8,9},{9,10},{10,1... | collective-permute-start | bytes 196616 | tf_op jit(solution)/shard_map/ppermute | solution.py:41
  130.5 1.3 collective-permute-start.33
  131.8 3.5 %product.5 = (bf16[1024,896]{1,0:T(8,128)(2,1)}, f32[8,128]{1,0:T(8,128)S(1)}) custom-call(bf16[1024,1024]{1,0:T(8,128)(2,1)S(1)} %get-tuple-element.62.a, bf16[640,896]{1,0:T(8,128)(2,1)S(1)} %copy-done.4, bf16[256,896]{1,0:T(8,128)(2,1)S(1)} %copy-done.6, bf16[128,896]{1,0:T(8,128)(2,1)S(1)} %copy-done.8, bf16[32,1024]{1,0:T(8,128)(2,1)S(1)} %get-tuple-element.68.refs_3_), custom_call_target="tpu_custom_call" | custom-call | flops 1879048192 | bytes 5767168 | tf_op jit(solution)/shard_map/product/pallas_call | solution.py:358
  135.3 1.0 collective-permute-done.33.r2
  136.3 1.0 collective-permute-done.34.r3
  (80 shorter events, 6.6 us)
Async XLA Ops:
  7.2 108.2 %all-gather.2.cloned.1.call-start = ((), (), s32[]{:S(2)}) async-start(), calls=%async_computation | async-start | bytes 2162688 | tf_op jit(solution)/shard_map/all_gather | solution.py:448
  8.2 5.9 %collective-permute-start = (bf16[32,1024]{1,0:T(8,128)(2,1)S(1)}, bf16[32,1024]{1,0:T(8,128)(2,1)S(1)}, u32[]{:S(2)}, u32[]{:S(2)}) collective-permute-start(bf16[32,1024]{1,0:T(8,128)(2,1)S(1)} %weigh.1.after), channel_id=1, source_target_pairs={{0,3},{1,0},{2,1},{3,2},{4,7},{5,4},{6,5},{7,6},{8,11},{9,8},{10,9... | collective-permute-start | bytes 196616 | tf_op jit(solution)/shard_map/ppermute | solution.py:41
  9.0 5.8 %collective-permute-start.1 = (bf16[32,1024]{1,0:T(8,128)(2,1)S(1)}, bf16[32,1024]{1,0:T(8,128)(2,1)S(1)}, u32[]{:S(2)}, u32[]{:S(2)}) collective-permute-start(bf16[32,1024]{1,0:T(8,128)(2,1)S(1)} %weigh.1.after), channel_id=1, source_target_pairs={{0,2},{1,3},{2,0},{3,1},{4,6},{5,7},{6,4},{7,5},{8,10},{9,11},{10,... | collective-permute-start | bytes 196616 | tf_op jit(solution)/shard_map/ppermute | solution.py:41
  11.7 4.3 %collective-permute-start.2 = (bf16[32,1024]{1,0:T(8,128)(2,1)S(1)}, bf16[32,1024]{1,0:T(8,128)(2,1)S(1)}, u32[]{:S(2)}, u32[]{:S(2)}) collective-permute-start(bf16[32,1024]{1,0:T(8,128)(2,1)S(1)} %weigh.1.after), channel_id=1, source_target_pairs={{0,1},{1,2},{2,3},{3,0},{4,5},{5,6},{6,7},{7,4},{8,9},{9,10},{10,1... | collective-permute-start | bytes 196616 | tf_op jit(solution)/shard_map/ppermute | solution.py:41
  15.9 9.7 %collective-permute-start.3 = (bf16[128,1024]{1,0:T(8,128)(2,1)S(1)}, bf16[128,1024]{1,0:T(8,128)(2,1)S(1)}, u32[]{:S(2)}, u32[]{:S(2)}) collective-permute-start(bf16[128,1024]{1,0:T(8,128)(2,1)S(1)} %pad_maximum_fusion.1), channel_id=1, source_target_pairs={{0,28},{1,29},{2,30},{3,31},{4,0},{5,1},{6,2},{7,3},{8,4},{9,5},{1... | collective-permute-start | bytes 786440 | tf_op jit(solution)/shard_map/ppermute | solution.py:36
  21.2 8.1 %collective-permute-start.5 = (bf16[128,1024]{1,0:T(8,128)(2,1)S(1)}, bf16[128,1024]{1,0:T(8,128)(2,1)S(1)}, u32[]{:S(2)}, u32[]{:S(2)}) collective-permute-start(bf16[128,1024]{1,0:T(8,128)(2,1)S(1)} %pad_maximum_fusion.1), channel_id=1, source_target_pairs={{0,4},{1,5},{2,6},{3,7},{4,8},{5,9},{6,10},{7,11},{8,12},{9,13},{1... | collective-permute-start | bytes 786440 | tf_op jit(solution)/shard_map/ppermute | solution.py:36
  22.3 11.2 %collective-permute-start.9 = (bf16[2,128,896]{2,1,0:T(8,128)(2,1)S(1)}, bf16[2,128,896]{2,1,0:T(8,128)(2,1)S(1)}, u32[]{:S(2)}, u32[]{:S(2)}) collective-permute-start(bf16[2,128,896]{2,1,0:T(8,128)(2,1)S(1)} %pack.1), channel_id=1, source_target_pairs={{0,192},{32,224},{64,0},{96,32},{128,64},{160,96},{192,128},{224,1... | collective-permute-start | bytes 1376264 | tf_op jit(solution)/shard_map/ppermute | solution.py:46
  25.1 12.2 %collective-permute-start.11 = (bf16[2,128,896]{2,1,0:T(8,128)(2,1)S(1)}, bf16[2,128,896]{2,1,0:T(8,128)(2,1)S(1)}, u32[]{:S(2)}, u32[]{:S(2)}) collective-permute-start(bf16[2,128,896]{2,1,0:T(8,128)(2,1)S(1)} %pack.1), channel_id=1, source_target_pairs={{0,64},{32,96},{64,128},{96,160},{128,192},{160,224},{192,0},{224,... | collective-permute-start | bytes 1376264 | tf_op jit(solution)/shard_map/ppermute | solution.py:46
  25.7 11.8 %collective-permute-start.4 = (bf16[128,1024]{1,0:T(8,128)(2,1)S(1)}, bf16[128,1024]{1,0:T(8,128)(2,1)S(1)}, u32[]{:S(2)}, u32[]{:S(2)}) collective-permute-start(bf16[128,1024]{1,0:T(8,128)(2,1)S(1)} %collective-permute-done.3), channel_id=1, source_target_pairs={{0,28},{1,29},{2,30},{3,31},{4,0},{5,1},{6,2},{7,3},{8,4},{9,5},{1... | collective-permute-start | bytes 786440 | tf_op jit(solution)/shard_map/ppermute | solution.py:36
  29.3 11.1 %collective-permute-start.6 = (bf16[128,1024]{1,0:T(8,128)(2,1)S(1)}, bf16[128,1024]{1,0:T(8,128)(2,1)S(1)}, u32[]{:S(2)}, u32[]{:S(2)}) collective-permute-start(bf16[128,1024]{1,0:T(8,128)(2,1)S(1)} %collective-permute-done.5), channel_id=1, source_target_pairs={{0,4},{1,5},{2,6},{3,7},{4,8},{5,9},{6,10},{7,11},{8,12},{9,13},{1... | collective-permute-start | bytes 786440 | tf_op jit(solution)/shard_map/ppermute | solution.py:36
  33.5 7.3 %collective-permute-start.10 = (bf16[128,896]{1,0:T(8,128)(2,1)S(1)}, bf16[128,896]{1,0:T(8,128)(2,1)S(1)}, u32[]{:S(2)}, u32[]{:S(2)}) collective-permute-start(bf16[128,896]{1,0:T(8,128)(2,1)S(1)} %slice_bitcast_fusion.1), channel_id=1, source_target_pairs={{0,192},{32,224},{64,0},{96,32},{128,64},{160,96},{192,128},{224,1... | collective-permute-start | bytes 688136 | tf_op jit(solution)/shard_map/ppermute | solution.py:46
  37.3 7.3 %collective-permute-start.12 = (bf16[128,896]{1,0:T(8,128)(2,1)S(1)}, bf16[128,896]{1,0:T(8,128)(2,1)S(1)}, u32[]{:S(2)}, u32[]{:S(2)}) collective-permute-start(bf16[128,896]{1,0:T(8,128)(2,1)S(1)} %slice_bitcast_fusion), channel_id=1, source_target_pairs={{0,64},{32,96},{64,128},{96,160},{128,192},{160,224},{192,0},{224,... | collective-permute-start | bytes 688136 | tf_op jit(solution)/shard_map/ppermute | solution.py:46
  37.4 7.7 %collective-permute-start.7 = (bf16[128,1024]{1,0:T(8,128)(2,1)S(1)}, bf16[128,1024]{1,0:T(8,128)(2,1)S(1)}, u32[]{:S(2)}, u32[]{:S(2)}) collective-permute-start(bf16[128,1024]{1,0:T(8,128)(2,1)S(1)} %collective-permute-done.4), channel_id=1, source_target_pairs={{0,28},{1,29},{2,30},{3,31},{4,0},{5,1},{6,2},{7,3},{8,4},{9,5},{1... | collective-permute-start | bytes 786440 | tf_op jit(solution)/shard_map/ppermute | solution.py:36
  40.5 8.0 %collective-permute-start.8 = (bf16[128,1024]{1,0:T(8,128)(2,1)S(1)}, bf16[128,1024]{1,0:T(8,128)(2,1)S(1)}, u32[]{:S(2)}, u32[]{:S(2)}) collective-permute-start(bf16[128,1024]{1,0:T(8,128)(2,1)S(1)} %collective-permute-done.6), channel_id=1, source_target_pairs={{0,4},{1,5},{2,6},{3,7},{4,8},{5,9},{6,10},{7,11},{8,12},{9,13},{1... | collective-permute-start | bytes 786440 | tf_op jit(solution)/shard_map/ppermute | solution.py:36
  45.0 10.4 %copy-start.2 = (bf16[896,1024]{1,0:T(8,128)(2,1)S(1)}, bf16[896,1024]{1,0:T(8,128)(2,1)}, u32[]{:S(2)}) copy-start(bf16[896,1024]{1,0:T(8,128)(2,1)} %w.3) | copy-start | bytes 5505028
  45.0 19.3 %collective-permute-start.19 = (bf16[4,2,128,896]{3,2,1,0:T(8,128)(2,1)S(1)}, bf16[4,2,128,896]{3,2,1,0:T(8,128)(2,1)S(1)}, u32[]{:S(2)}, u32[]{:S(2)}) collective-permute-start(bf16[4,2,128,896]{3,2,1,0:T(8,128)(2,1)S(1)} %pad_maximum_fusion.mine), channel_id=1, source_target_pairs={{0,32},{32,0},{64,96},{96,64},{128,160},{160,128},{192,224},{224,1... | collective-permute-start | bytes 5505032 | tf_op jit(solution)/shard_map/ppermute | solution.py:50
  48.5 5.3 %collective-permute-start.13 = (bf16[64,1024]{1,0:T(8,128)(2,1)S(1)}, bf16[64,1024]{1,0:T(8,128)(2,1)S(1)}, u32[]{:S(2)}, u32[]{:S(2)}) collective-permute-start(bf16[64,1024]{1,0:T(8,128)(2,1)S(1)} %get-tuple-element.41), channel_id=1, source_target_pairs={{0,28},{1,29},{2,30},{3,31},{4,0},{5,1},{6,2},{7,3},{8,4},{9,5},{1... | collective-permute-start | bytes 393224 | tf_op jit(solution)/shard_map/ppermute | solution.py:36
  48.6 6.8 %collective-permute-start.14 = (bf16[64,1024]{1,0:T(8,128)(2,1)S(1)}, bf16[64,1024]{1,0:T(8,128)(2,1)S(1)}, u32[]{:S(2)}, u32[]{:S(2)}) collective-permute-start(bf16[64,1024]{1,0:T(8,128)(2,1)S(1)} %get-tuple-element.42), channel_id=1, source_target_pairs={{0,4},{1,5},{2,6},{3,7},{4,8},{5,9},{6,10},{7,11},{8,12},{9,13},{1... | collective-permute-start | bytes 393224 | tf_op jit(solution)/shard_map/ppermute | solution.py:36
  57.2 2.6 %collective-permute-start.15 = (bf16[4,128,896]{2,1,0:T(8,128)(2,1)S(1)}, bf16[4,128,896]{2,1,0:T(8,128)(2,1)S(1)}, u32[]{:S(2)}, u32[]{:S(2)}) collective-permute-start(bf16[4,128,896]{2,1,0:T(8,128)(2,1)S(1)} %first.3.after), channel_id=1, source_target_pairs={{0,32},{32,0},{64,96},{96,64},{128,160},{160,128},{192,224},{224,1... | collective-permute-start | bytes 2752520 | tf_op jit(solution)/shard_map/ppermute | solution.py:50
  59.9 8.9 %collective-permute-start.16 = (bf16[128,896]{1,0:T(8,128)(2,1)S(1)}, bf16[128,896]{1,0:T(8,128)(2,1)S(1)}, u32[]{:S(2)}, u32[]{:S(2)}) collective-permute-start(bf16[128,896]{1,0:T(8,128)(2,1)S(1)} %get-tuple-element.44), channel_id=1, source_target_pairs={{0,64},{32,96},{64,128},{96,160},{128,192},{160,224},{192,0},{224,... | collective-permute-start | bytes 688136 | tf_op jit(solution)/shard_map/ppermute | solution.py:46
  60.0 14.8 %collective-permute-start.17 = (bf16[128,896]{1,0:T(8,128)(2,1)S(1)}, bf16[128,896]{1,0:T(8,128)(2,1)S(1)}, u32[]{:S(2)}, u32[]{:S(2)}) collective-permute-start(bf16[128,896]{1,0:T(8,128)(2,1)S(1)} %get-tuple-element.45), channel_id=1, source_target_pairs={{0,128},{32,160},{64,192},{96,224},{128,0},{160,32},{192,64},{224,... | collective-permute-start | bytes 688136 | tf_op jit(solution)/shard_map/ppermute | solution.py:46
  64.2 10.5 %collective-permute-start.18 = (bf16[128,896]{1,0:T(8,128)(2,1)S(1)}, bf16[128,896]{1,0:T(8,128)(2,1)S(1)}, u32[]{:S(2)}, u32[]{:S(2)}) collective-permute-start(bf16[128,896]{1,0:T(8,128)(2,1)S(1)} %get-tuple-element.46), channel_id=1, source_target_pairs={{0,192},{32,224},{64,0},{96,32},{128,64},{160,96},{192,128},{224,1... | collective-permute-start | bytes 688136 | tf_op jit(solution)/shard_map/ppermute | solution.py:46
  74.9 12.3 %collective-permute-start.20 = (bf16[128,896]{1,0:T(8,128)(2,1)S(1)}, bf16[128,896]{1,0:T(8,128)(2,1)S(1)}, u32[]{:S(2)}, u32[]{:S(2)}) collective-permute-start(bf16[128,896]{1,0:T(8,128)(2,1)S(1)} %total.2.refs_3_.a), channel_id=1, source_target_pairs={{0,192},{32,224},{64,0},{96,32},{128,64},{160,96},{192,128},{224,1... | collective-permute-start | bytes 688136 | tf_op jit(solution)/shard_map/ppermute | solution.py:46
  77.2 10.0 %collective-permute-start.21 = (bf16[128,896]{1,0:T(8,128)(2,1)S(1)}, bf16[128,896]{1,0:T(8,128)(2,1)S(1)}, u32[]{:S(2)}, u32[]{:S(2)}) collective-permute-start(bf16[128,896]{1,0:T(8,128)(2,1)S(1)} %total.2.refs_3_.a), channel_id=1, source_target_pairs={{0,128},{32,160},{64,192},{96,224},{128,0},{160,32},{192,64},{224,... | collective-permute-start | bytes 688136 | tf_op jit(solution)/shard_map/ppermute | solution.py:46
  77.4 13.2 %collective-permute-start.22 = (bf16[128,896]{1,0:T(8,128)(2,1)S(1)}, bf16[128,896]{1,0:T(8,128)(2,1)S(1)}, u32[]{:S(2)}, u32[]{:S(2)}) collective-permute-start(bf16[128,896]{1,0:T(8,128)(2,1)S(1)} %total.2.refs_3_.a), channel_id=1, source_target_pairs={{0,64},{32,96},{64,128},{96,160},{128,192},{160,224},{192,0},{224,... | collective-permute-start | bytes 688136 | tf_op jit(solution)/shard_map/ppermute | solution.py:46
  78.1 15.1 %copy-start.1 = (bf16[1024,896]{1,0:T(8,128)(2,1)S(1)}, bf16[1024,896]{1,0:T(8,128)(2,1)}, u32[]{:S(2)}) copy-start(bf16[1024,896]{1,0:T(8,128)(2,1)} %uw.5) | copy-start | bytes 5505028
  81.3 11.9 %copy-start = (bf16[1024,896]{1,0:T(8,128)(2,1)S(1)}, bf16[1024,896]{1,0:T(8,128)(2,1)}, u32[]{:S(2)}) copy-start(bf16[1024,896]{1,0:T(8,128)(2,1)} %gw.5) | copy-start | bytes 5505028
  90.6 2.6 %collective-permute-start.23 = (bf16[4,128,896]{2,1,0:T(8,128)(2,1)S(1)}, bf16[4,128,896]{2,1,0:T(8,128)(2,1)S(1)}, u32[]{:S(2)}, u32[]{:S(2)}) collective-permute-start(bf16[4,128,896]{2,1,0:T(8,128)(2,1)S(1)} %join.1.mine), channel_id=1, source_target_pairs={{0,32},{32,0},{64,96},{96,64},{128,160},{160,128},{192,224},{224,1... | collective-permute-start | bytes 2752520 | tf_op jit(solution)/shard_map/ppermute | solution.py:50
  95.6 7.2 %collective-permute-start.24 = (bf16[64,1024]{1,0:T(8,128)(2,1)S(1)}, bf16[64,1024]{1,0:T(8,128)(2,1)S(1)}, u32[]{:S(2)}, u32[]{:S(2)}) collective-permute-start(bf16[64,1024]{1,0:T(8,128)(2,1)S(1)} %get-tuple-element.79), channel_id=1, source_target_pairs={{0,4},{1,5},{2,6},{3,7},{4,8},{5,9},{6,10},{7,11},{8,12},{9,13},{1... | collective-permute-start | bytes 393224 | tf_op jit(solution)/shard_map/ppermute | solution.py:36
  96.2 6.6 %collective-permute-start.25 = (bf16[64,1024]{1,0:T(8,128)(2,1)S(1)}, bf16[64,1024]{1,0:T(8,128)(2,1)S(1)}, u32[]{:S(2)}, u32[]{:S(2)}) collective-permute-start(bf16[64,1024]{1,0:T(8,128)(2,1)S(1)} %get-tuple-element.78), channel_id=1, source_target_pairs={{0,28},{1,29},{2,30},{3,31},{4,0},{5,1},{6,2},{7,3},{8,4},{9,5},{1... | collective-permute-start | bytes 393224 | tf_op jit(solution)/shard_map/ppermute | solution.py:36
  102.9 9.0 %collective-permute-start.26 = (bf16[128,1024]{1,0:T(8,128)(2,1)S(1)}, bf16[128,1024]{1,0:T(8,128)(2,1)S(1)}, u32[]{:S(2)}, u32[]{:S(2)}) collective-permute-start(bf16[128,1024]{1,0:T(8,128)(2,1)S(1)} %get-tuple-element.54.after), channel_id=1, source_target_pairs={{0,4},{1,5},{2,6},{3,7},{4,8},{5,9},{6,10},{7,11},{8,12},{9,13},{1... | collective-permute-start | bytes 786440 | tf_op jit(solution)/shard_map/ppermute | solution.py:36
  103.0 8.9 %collective-permute-start.27 = (bf16[128,1024]{1,0:T(8,128)(2,1)S(1)}, bf16[128,1024]{1,0:T(8,128)(2,1)S(1)}, u32[]{:S(2)}, u32[]{:S(2)}) collective-permute-start(bf16[128,1024]{1,0:T(8,128)(2,1)S(1)} %get-tuple-element.56), channel_id=1, source_target_pairs={{0,28},{1,29},{2,30},{3,31},{4,0},{5,1},{6,2},{7,3},{8,4},{9,5},{1... | collective-permute-start | bytes 786440 | tf_op jit(solution)/shard_map/ppermute | solution.py:36
  112.0 8.1 %collective-permute-start.28 = (bf16[128,1024]{1,0:T(8,128)(2,1)S(1)}, bf16[128,1024]{1,0:T(8,128)(2,1)S(1)}, u32[]{:S(2)}, u32[]{:S(2)}) collective-permute-start(bf16[128,1024]{1,0:T(8,128)(2,1)S(1)} %get-tuple-element.57.after), channel_id=1, source_target_pairs={{0,4},{1,5},{2,6},{3,7},{4,8},{5,9},{6,10},{7,11},{8,12},{9,13},{1... | collective-permute-start | bytes 786440 | tf_op jit(solution)/shard_map/ppermute | solution.py:36
  112.1 8.0 %collective-permute-start.29 = (bf16[128,1024]{1,0:T(8,128)(2,1)S(1)}, bf16[128,1024]{1,0:T(8,128)(2,1)S(1)}, u32[]{:S(2)}, u32[]{:S(2)}) collective-permute-start(bf16[128,1024]{1,0:T(8,128)(2,1)S(1)} %get-tuple-element.58), channel_id=1, source_target_pairs={{0,28},{1,29},{2,30},{3,31},{4,0},{5,1},{6,2},{7,3},{8,4},{9,5},{1... | collective-permute-start | bytes 786440 | tf_op jit(solution)/shard_map/ppermute | solution.py:36
  115.3 1.6 %copy-start.3 = (bf16[1024,1024]{1,0:T(8,128)(2,1)S(1)}, bf16[1024,1024]{1,0:T(8,128)(2,1)}, u32[]{:S(2)}) copy-start(bf16[1024,1024]{1,0:T(8,128)(2,1)} %all-gather.2.cloned.1.call-done.x_in) | copy-start | bytes 6291460
  119.0 4.5 %copy-start.5 = (bf16[640,896]{1,0:T(8,128)(2,1)S(1)}, bf16[640,896]{1,0:T(8,128)(2,1)}, u32[]{:S(2)}) copy-start(bf16[640,896]{1,0:T(8,128)(2,1)} %get-tuple-element.63.refs_0_) | copy-start | bytes 3440644
  119.0 4.5 %copy-start.7 = (bf16[256,896]{1,0:T(8,128)(2,1)S(1)}, bf16[256,896]{1,0:T(8,128)(2,1)}, u32[]{:S(2)}) copy-start(bf16[256,896]{1,0:T(8,128)(2,1)} %get-tuple-element.64.refs_1_) | copy-start | bytes 1376260
  119.0 4.5 %copy-start.9 = (bf16[128,896]{1,0:T(8,128)(2,1)S(1)}, bf16[128,896]{1,0:T(8,128)(2,1)}, u32[]{:S(2)}) copy-start(bf16[128,896]{1,0:T(8,128)(2,1)} %get-tuple-element.65.refs_2_) | copy-start | bytes 688132
  120.2 7.7 %collective-permute-start.30 = (bf16[128,1024]{1,0:T(8,128)(2,1)S(1)}, bf16[128,1024]{1,0:T(8,128)(2,1)S(1)}, u32[]{:S(2)}, u32[]{:S(2)}) collective-permute-start(bf16[128,1024]{1,0:T(8,128)(2,1)S(1)} %get-tuple-element.60.refs_3_), channel_id=1, source_target_pairs={{0,4},{1,5},{2,6},{3,7},{4,8},{5,9},{6,10},{7,11},{8,12},{9,13},{1... | collective-permute-start | bytes 786440 | tf_op jit(solution)/shard_map/ppermute | solution.py:36
  120.7 7.2 %collective-permute-start.31 = (bf16[128,1024]{1,0:T(8,128)(2,1)S(1)}, bf16[128,1024]{1,0:T(8,128)(2,1)S(1)}, u32[]{:S(2)}, u32[]{:S(2)}) collective-permute-start(bf16[128,1024]{1,0:T(8,128)(2,1)S(1)} %get-tuple-element.61), channel_id=1, source_target_pairs={{0,28},{1,29},{2,30},{3,31},{4,0},{5,1},{6,2},{7,3},{8,4},{9,5},{1... | collective-permute-start | bytes 786440 | tf_op jit(solution)/shard_map/ppermute | solution.py:36
  127.0 4.8 %copy-start.4 = (bf16[640,896]{1,0:T(8,128)(2,1)S(1)}, bf16[640,896]{1,0:T(8,128)(2,1)}, u32[]{:S(2)}) copy-start(bf16[640,896]{1,0:T(8,128)(2,1)} %get-tuple-element.71.refs_0_) | copy-start | bytes 3440644
  127.0 4.8 %copy-start.6 = (bf16[256,896]{1,0:T(8,128)(2,1)S(1)}, bf16[256,896]{1,0:T(8,128)(2,1)}, u32[]{:S(2)}) copy-start(bf16[256,896]{1,0:T(8,128)(2,1)} %get-tuple-element.72.refs_1_) | copy-start | bytes 1376260
  127.0 4.8 %copy-start.8 = (bf16[128,896]{1,0:T(8,128)(2,1)S(1)}, bf16[128,896]{1,0:T(8,128)(2,1)}, u32[]{:S(2)}) copy-start(bf16[128,896]{1,0:T(8,128)(2,1)} %get-tuple-element.73.refs_2_) | copy-start | bytes 688132
  128.0 7.3 %collective-permute-start.32 = (bf16[32,1024]{1,0:T(8,128)(2,1)S(1)}, bf16[32,1024]{1,0:T(8,128)(2,1)S(1)}, u32[]{:S(2)}, u32[]{:S(2)}) collective-permute-start(bf16[32,1024]{1,0:T(8,128)(2,1)S(1)} %get-tuple-element.68.refs_3_), channel_id=1, source_target_pairs={{0,1},{1,2},{2,3},{3,0},{4,5},{5,6},{6,7},{7,4},{8,9},{9,10},{10,1... | collective-permute-start | bytes 196616 | tf_op jit(solution)/shard_map/ppermute | solution.py:41
  130.5 5.8 %collective-permute-start.33 = (bf16[32,1024]{1,0:T(8,128)(2,1)S(1)}, bf16[32,1024]{1,0:T(8,128)(2,1)S(1)}, u32[]{:S(2)}, u32[]{:S(2)}) collective-permute-start(bf16[32,1024]{1,0:T(8,128)(2,1)S(1)} %get-tuple-element.69), channel_id=1, source_target_pairs={{0,2},{1,3},{2,0},{3,1},{4,6},{5,7},{6,4},{7,5},{8,10},{9,11},{10,... | collective-permute-start | bytes 196616 | tf_op jit(solution)/shard_map/ppermute | solution.py:41
  131.8 5.5 %collective-permute-start.34 = (bf16[32,1024]{1,0:T(8,128)(2,1)S(1)}, bf16[32,1024]{1,0:T(8,128)(2,1)S(1)}, u32[]{:S(2)}, u32[]{:S(2)}) collective-permute-start(bf16[32,1024]{1,0:T(8,128)(2,1)S(1)} %get-tuple-element.70), channel_id=1, source_target_pairs={{0,3},{1,0},{2,1},{3,2},{4,7},{5,4},{6,5},{7,6},{8,11},{9,8},{10,9... | collective-permute-start | bytes 196616 | tf_op jit(solution)/shard_map/ppermute | solution.py:41
Sparse Core Ops, SparseCore 0:
  25.3 76.8 all-gather.1
